TPU v7x, 32 devices: a whole 2x2x4 slice. The times are simulated.
32 devices in a mesh: inner: 4 (over y, x), outer: 8 (over z, core).
Axes of the slice: x: 2, y: 2, z: 4, core: 2. Of those that a mesh axis runs over, the one named last changes fastest.
Arguments:
- queries: bfloat16 [8, 2048, 768], P('outer', 'inner'), may hold values from -8 to 8
- key_rows: bfloat16 [8, 2048, 768], P('outer', 'inner'), may hold values from -8 to 8
- values: bfloat16 [8, 2048, 768], P('outer', 'inner'), may hold values from -6 to 6
- out_weight: bfloat16 [768, 768], replicated, may hold values from -0.21875 to 0.21875
Outputs:
- attention_out: bfloat16 [8, 2048, 768], P('outer', 'inner')
All inputs are finite; a program needn't handle non-finite values.
Results may differ from a plain program's by a relative error of at most 0.0052.
Values may be sent and summed in bfloat16 or wider, within the bound.
No kernel may reach another device: no remote copies, remote signals or barrier semaphores. Data moves between devices by JAX's collectives and lax.ppermute only.
A program may use at most 64 MiB of HBM per device.

v0:
```python
import math

import jax
import jax.numpy as jnp
import numpy as np
from jax import lax
from jax.experimental import pallas as pl
from jax.experimental.pallas import tpu as pltpu
from jax.sharding import PartitionSpec as P

HEAD_DIM = 64
GSTEP = 64
PAIR = 2 * HEAD_DIM
CHUNK = 256
LANES = 128
LOG2E = math.log2(math.e)
VMEM_BYTES = 16 * 1024 * 1024
JOIN_VMEM_BYTES = 8 * 1024 * 1024
FETCH_VMEM_BYTES = 60 * 1024 * 1024


def across(block, axis, flip):
    return lax.ppermute(block, axis, [(i, i ^ flip) for i in range(lax.axis_size(axis))])


def after(block, *others):
    return lax.optimization_barrier((block, *others))[0]


def join_after(pieces, other):
    width = pieces[0][0].shape[1]
    total = sum(high - low for _, low, high in pieces)

    def kernel(*refs):
        out_ref, at = refs[-1], 0
        for ref, (_, low, high) in zip(refs, pieces):
            out_ref[at : at + high - low, :] = ref[low:high, :]
            at += high - low

    return pl.pallas_call(
        kernel,
        out_shape=jax.ShapeDtypeStruct((total, width), pieces[0][0].dtype),
        in_specs=[pl.BlockSpec(memory_space=pltpu.VMEM)] * len(pieces)
        + [pl.BlockSpec(memory_space=pl.ANY)],
        compiler_params=pltpu.CompilerParams(vmem_limit_bytes=JOIN_VMEM_BYTES),
        cost_estimate=pl.CostEstimate(
            flops=0, bytes_accessed=4 * total * width, transcendentals=0
        ),
    )(*[block for block, _, _ in pieces], other)


def runs(counts):
    found = []
    for at, value in enumerate(counts):
        if found and found[-1][2] == value:
            found[-1][1] = at + 1
        else:
            found.append([at, at + 1, int(value)])
    return [tuple(entry) for entry in found]


def order_rows(select, key_rows, values, prefixes):
    tokens, width = key_rows.shape

    pieces = [
        (half, low, min(CHUNK, width - low)) for half in range(2) for low in range(0, width, CHUNK)
    ]

    def kernel(select_hbm, key_hbm, value_hbm, *refs):
        out_refs, (select_ref, row_ref, sems) = refs[: len(prefixes)], refs[len(prefixes) :]
        copies = [pltpu.make_async_copy(select_hbm, select_ref, sems.at[0])]
        for at, (half, low, size) in enumerate(pieces):
            source = (key_hbm, value_hbm)[half].at[:, low : low + size]
            target = row_ref.at[half, :, low : low + size]
            copies.append(pltpu.make_async_copy(source, target, sems.at[1 + at]))
        for copy in copies:
            copy.start()
        copies[0].wait()
        for copy, (half, low, size) in zip(copies[1:], pieces):
            copy.wait()
            moved = jnp.dot(
                select_ref[...],
                row_ref[half, :, low : low + size],
                preferred_element_type=jnp.float32,
            ).astype(jnp.bfloat16)
            cols = slice(half * width + low, half * width + low + size)
            for (first, last), out_ref in zip(prefixes, out_refs):
                out_ref[:, cols] = moved[first:last]

    return pl.pallas_call(
        kernel,
        out_shape=[
            jax.ShapeDtypeStruct((high - low, 2 * width), jnp.bfloat16) for low, high in prefixes
        ],
        in_specs=[pl.BlockSpec(memory_space=pltpu.HBM)] * 3,
        scratch_shapes=[
            pltpu.VMEM(select.shape, jnp.bfloat16),
            pltpu.VMEM((2, tokens, width), jnp.bfloat16),
            pltpu.SemaphoreType.DMA((1 + len(pieces),)),
        ],
        compiler_params=pltpu.CompilerParams(vmem_limit_bytes=FETCH_VMEM_BYTES),
        cost_estimate=pl.CostEstimate(
            flops=4 * select.size * width, bytes_accessed=6 * tokens * width, transcendentals=0
        ),
    )(select, key_rows, values)


def attend(queries, sets, counts=None, row_strides=None, part=(0, 1), states=(), out_weight=None, wait=None):
    tokens = queries.shape[0]
    width = queries.shape[1] // part[1]
    heads, pairs = width // HEAD_DIM, width // PAIR
    joined = [not isinstance(block, tuple) for block in sets]
    sizes = [(block if whole else block[0]).shape[0] for block, whole in zip(sets, joined)]
    keys = sum(sizes)
    padded = -(-keys // LANES) * LANES
    row_runs = [(0, keys, 1)] if counts is None else runs(counts)
    scale = HEAD_DIM**-0.5 * LOG2E
    final = out_weight is not None
    groups = max(len(states), 1)

    def kernel(*refs):
        refs = list(refs)
        query_ref = refs.pop(0)
        set_refs = []
        for whole in joined:
            ref = refs.pop(0)
            set_refs.append((ref, 0, ref, width) if whole else (ref, 0, refs.pop(0), 0))
        state_refs = [[refs.pop(0) for _ in range(3)] for _ in states]
        if wait is not None:
            refs.pop(1 if final else 0)
        if final:
            weight_ref, out_ref, attended_ref = refs.pop(0), refs.pop(0), refs.pop(-1)
        else:
            numer_out, peak_out, total_out = [refs.pop(0) for _ in range(3)]
        score_ref, value_ref = refs.pop(0), refs.pop(0)
        if row_strides is not None:
            offset_ref = refs.pop(0)
            row = lax.broadcasted_iota(jnp.int32, (keys, LANES), 0)
            rank = sum((row & (s - 1) == 0).astype(jnp.int32) for s in row_strides)
            offsets = jnp.zeros((keys, LANES), jnp.float32)
            for times in range(1, len(row_strides) + 1):
                offsets = jnp.where(rank == times, math.log2(1 + times), offsets)
            offset_ref[...] = offsets

        ones = jnp.ones((16, padded), jnp.bfloat16)
        key_chunks = []
        at = 0
        for entry, size in zip(set_refs, sizes):
            for low in range(0, size, CHUNK):
                count = min(CHUNK, size - low)
                key_chunks.append((entry[0], low, count, at))
                at += count
        value_chunks = [(low, min(CHUNK, padded - low)) for low in range(0, padded, CHUNK)]

        def column(pair):
            return pl.multiple_of(pair * PAIR, PAIR)

        def head_queries(pair, half):
            turned = query_ref[:, pl.ds(column(pair), PAIR)].T
            row = lax.broadcasted_iota(jnp.int32, turned.shape, 0)
            own = (row < HEAD_DIM) if half == 0 else (row >= HEAD_DIM)
            return jnp.where(own, turned, jnp.zeros_like(turned))

        def score(pair, half, query_head, chunk, running):
            ref, low, count, at = chunk
            scores = jnp.dot(
                ref[low : low + count, pl.ds(column(pair), PAIR)],
                query_head,
                preferred_element_type=jnp.float32,
            )
            score_ref[half, at : at + count, :] = scores
            tallest = jnp.max(scores.reshape(count // 8, 8, tokens), axis=0)
            return tallest if running is None else jnp.maximum(running, tallest)

        def weigh(half, peak, weighted, chunk, gathered):
            low, size = chunk
            high = min(low + size, keys)
            pieces = []
            for first, last, times in row_runs:
                first, last = max(first, low), min(last, high)
                if first < last:
                    offset = peak - math.log2(times)
                    power = score_ref[half, first:last, :] * scale - offset
                    if row_strides is not None:
                        extra = offset_ref[first:last, :]
                        power = power + jnp.concatenate([extra] * (tokens // LANES), axis=1)
                    pieces.append(jnp.exp2(power))
            if low + size > keys:
                pieces.append(jnp.zeros((low + size - keys, tokens), jnp.float32))
            probs = (pieces[0] if len(pieces) == 1 else jnp.concatenate(pieces, axis=0)).astype(
                jnp.bfloat16
            )
            product = jnp.dot(
                weighted[:, low : low + size], probs, preferred_element_type=jnp.float32
            )
            return product if gathered is None else gathered + product

        def one_group(first_pair, last_pair, earlier):
            def local_rows(pair, half):
                start = (pair - first_pair) * PAIR + half * HEAD_DIM
                return pl.ds(pl.multiple_of(start, HEAD_DIM), HEAD_DIM)

            def local_head(pair, half):
                return pl.ds(2 * (pair - first_pair) + half, 1)

            def finish(pair, half, gathered, peak, before):
                numer, total = gathered[:HEAD_DIM], gathered[HEAD_DIM : HEAD_DIM + 1]
                if earlier is not None:
                    factor = jnp.exp2(before - peak)
                    numer = numer + factor * earlier[0][local_rows(pair, half), :]
                    total = total + factor * earlier[2][local_head(pair, half), :]
                start = pl.multiple_of(column(pair) + half * HEAD_DIM, HEAD_DIM)
                rows = pl.ds(start, HEAD_DIM)
                if final:
                    attended_ref[half] = (numer / total).astype(jnp.bfloat16)
                    if half == 1:
                        both = attended_ref[...].reshape(PAIR, tokens)
                        out_ref[:, pl.ds(column(pair), PAIR)] = both.T
                else:
                    head = pl.ds(2 * pair + half, 1)
                    numer_out[rows, :] = numer
                    peak_out[head, :] = peak
                    total_out[head, :] = total

            def overlap(pair, half, running, values_t, next_pair, next_half):
                peak = jnp.max(running, axis=0, keepdims=True) * scale
                before = None
                if earlier is not None:
                    before = earlier[1][local_head(pair, half), :]
                    peak = jnp.maximum(peak, before)
                weighted = jnp.concatenate(
                    [values_t[half * HEAD_DIM : (half + 1) * HEAD_DIM], ones], axis=0
                )
                query_head = head_queries(next_pair, next_half)
                next_running, gathered = None, None
                for step in range(max(len(key_chunks), len(value_chunks))):
                    if step < len(key_chunks):
                        next_running = score(
                            next_pair, next_half, query_head, key_chunks[step], next_running
                        )
                    if step < len(value_chunks):
                        gathered = weigh(half, peak, weighted, value_chunks[step], gathered)
                finish(pair, half, gathered, peak, before)
                return next_running

            def pair_step(pair, running):
                at = 0
                for (_, _, ref, shift), size in zip(set_refs, sizes):
                    value_ref[at : at + size, :] = ref[:, pl.ds(column(pair) + shift, PAIR)]
                    at += size
                if padded > keys:
                    value_ref[keys:, :] = jnp.zeros((padded - keys, PAIR), jnp.bfloat16)
                values_t = value_ref[...].T
                running = overlap(pair, 0, running, values_t, pair, 1)
                later = jnp.minimum(pair + 1, last_pair - 1)
                return overlap(pair, 1, running, values_t, later, 0)

            first_head = head_queries(first_pair, 0)
            running = None
            for chunk in key_chunks:
                running = score(first_pair, 0, first_head, chunk, running)
            lax.fori_loop(first_pair, last_pair, pair_step, running)

        for group in range(groups):
            one_group(
                group * pairs // groups,
                (group + 1) * pairs // groups,
                state_refs[group] if states else None,
            )
        if final:
            out_ref[...] = jnp.dot(
                out_ref[...], weight_ref[...], preferred_element_type=jnp.float32
            ).astype(jnp.bfloat16)

    if final:
        out_shape = jax.ShapeDtypeStruct((tokens, width), jnp.bfloat16)
    else:
        out_shape = [
            jax.ShapeDtypeStruct((width, tokens), jnp.float32),
            jax.ShapeDtypeStruct((heads, tokens), jnp.float32),
            jax.ShapeDtypeStruct((heads, tokens), jnp.float32),
        ]
    scratch = [
        pltpu.VMEM((2, padded, tokens), jnp.float32),
        pltpu.VMEM((padded, PAIR), jnp.bfloat16),
    ]
    if row_strides is not None:
        scratch.append(pltpu.VMEM((keys, LANES), jnp.float32))
    if final:
        scratch.append(pltpu.VMEM((2, HEAD_DIM, tokens), jnp.bfloat16))
    operands = [queries]
    for block, whole in zip(sets, joined):
        operands += [block] if whole else list(block)
    whole_spec = pl.BlockSpec(memory_space=pltpu.VMEM)
    specs = [whole_spec] * len(operands)
    if part[1] > 1:
        specs = [
            pl.BlockSpec((array.shape[0], array.shape[1] // part[1]), lambda step: (0, part[0]))
            for array in operands
        ]
    for array in [array for state in states for array in state] + ([out_weight] if final else []):
        operands.append(array)
        specs.append(whole_spec)
    if wait is not None:
        operands.append(wait)
        specs.append(pl.BlockSpec(memory_space=pl.ANY))
    return pl.pallas_call(
        kernel,
        out_shape=out_shape,
        grid=(1,) if part[1] > 1 else (),
        in_specs=specs,
        scratch_shapes=scratch,
        compiler_params=pltpu.CompilerParams(
            vmem_limit_bytes=VMEM_BYTES
        ),
        cost_estimate=pl.CostEstimate(
            flops=16 * tokens * keys * width,
            bytes_accessed=(4 * keys * width + 4 * tokens * width),
            transcendentals=tokens * keys * heads,
        ),
    )(*operands)


def local(queries, key_rows, values, out_weight):
    query_rows, own_keys, own_values = queries[0], key_rows[0], values[0]
    tokens = query_rows.shape[0]
    n_inner, n_outer = lax.axis_size("inner"), lax.axis_size("outer")
    inner_bits = n_inner.bit_length() - 1
    strides = [1 << (bit + 1) for bit in range(inner_bits + 1)]
    sends = [tokens >> (bit + 1) for bit in range(inner_bits + 1)]
    n_global = tokens // GSTEP

    rows = np.arange(0, tokens, 2)
    rank = sum((rows % s == 0).astype(np.int64) for s in strides + [GSTEP])
    order = rows[np.lexsort((rows, -rank))]
    select = np.zeros((sends[0], tokens), np.float32)
    select[np.arange(sends[0]), order] = 1.0

    def prefix_counts(level, low, high):
        return sum((order[low:high] % s == 0).astype(np.int64) for s in strides[level:])

    first_a, first_b, far = order_rows(
        jnp.asarray(select, jnp.bfloat16),
        own_keys,
        own_values,
        [(0, sends[1]), (sends[1], sends[0]), (0, n_global)],
    )

    held = {0: (first_a, 0)}
    for bit in range(1, inner_bits):
        held[1 << bit] = (across(first_a[: sends[bit]], "inner", 1 << bit), 0)
    held[1] = (across(first_a, "inner", 1), 0)
    own_set = [(own_keys, own_values)]
    own_states, moved, flip = [], far, 2
    while flip < n_outer or len(own_states) < 2:
        if flip < n_outer:
            came = across(moved, "outer", flip)
            flip *= 2
        if len(own_states) < 2:
            own_states.append(
                attend(
                    query_rows,
                    own_set,
                    row_strides=strides,
                    part=(len(own_states), 2),
                    wait=moved,
                )
            )
        moved = join_after([(moved, 0, moved.shape[0]), (came, 0, came.shape[0])], own_states[-1][1])
    far = moved
    n_far = far.shape[0]
    fars = {0: (far, 0)}

    def first_rows(where, count):
        return (where[0], where[1], where[1] + count)

    near_b = across(
        join_after([(first_b, 0, sends[0] - sends[1]), (far, 0, n_far)], far), "inner", 1
    )
    fars[1] = (near_b, sends[0] - sends[1])
    own_done = far

    known = [0] + [1 << bit for bit in range(inner_bits)]
    late = [d for d in range(n_inner) if d not in known]
    last = sends[inner_bits]
    late_sets = [near_b]
    late_counts = [prefix_counts(0, sends[1], sends[0]), np.ones(n_far, np.int64)]
    for bit in range(1, inner_bits):
        count = sends[bit]
        others = range(1, 1 << bit)
        pieces = [first_rows(held[d], count) for d in others] + [first_rows(fars[0], n_far)]
        own_done = join_after(pieces, own_done)
        came = across(own_done, "inner", 1 << bit)
        for at, d in enumerate(others):
            held[d | 1 << bit] = (came, at * count)
        fars[1 << bit] = (came, len(others) * count)
        late_sets.append(came)
        late_counts += [prefix_counts(bit, 0, count)] * len(others) + [np.ones(n_far, np.int64)]
    for d in late:
        fars[d] = (across(far, "inner", d), 0)
        late_sets.append(fars[d][0])
        late_counts.append(np.ones(n_far, np.int64))
    pieces = [first_rows(held[d], last) for d in known]
    moved = join_after(pieces, own_done)
    early_core = across(moved, "outer", 1)

    early_sets = [held[d][0] for d in known[1:]] + [early_core, far]
    early_counts = [prefix_counts(0, 0, sends[1])]
    early_counts += [prefix_counts(bit, 0, sends[bit]) for bit in range(1, inner_bits)]
    early_counts.append(np.ones(early_core.shape[0] + n_far, np.int64))
    state = attend(query_rows, early_sets, np.concatenate(early_counts), states=own_states)

    pieces = [first_rows(held[d], last) for d in late]
    pieces += [first_rows(fars[d], n_far) for d in range(n_inner)]
    late_core = across(join_after(pieces, state[1]), "outer", 1)
    state = attend(query_rows, late_sets, np.concatenate(late_counts), states=[state])
    result = attend(query_rows, [late_core], states=[state], out_weight=out_weight)
    return result[None]


def solution(mesh):
    placed = (P("outer", "inner", None), P("outer", "inner", None), P("outer", "inner", None), P())
    return jax.shard_map(
        local, mesh=mesh, in_specs=placed, out_specs=P("outer", "inner", None), check_vma=False
    )
```

profile of v0, /device:TPU:0, one launch (start us, length us, event | category | flops | bytes accessed | tf_op | source)
XLA Modules:
  0.0 46.3 jit_solution(16141060715346295488)
XLA Ops:
  0.0 3.8 %shard_map.55 = (bf16[128,1536]{1,0:T(8,128)(2,1)}, bf16[128,1536]{1,0:T(8,128)(2,1)}, bf16[8,1536]{1,0:T(8,128)(2,1)}) custom-call(bf16[256,512]{1,0:T(8,128)(2,1)} %constant.2.clone.select_hbm, bf16[512,768]{1,0:T(8,128)(2,1)} %bitcast.4, bf16[512,768]{1,0:T(8,128)(2,1)} %bitcast.7), custom_call_target="tpu_custom_call" | custom-call | flops 402653184 | bytes 2359296 | tf_op jit(solution)/shard_map/pallas_call | solution.py:90
  3.8 3.0 %collective-permute-start = (bf16[128,1536]{1,0:T(8,128)(2,1)}, bf16[128,1536]{1,0:T(8,128)(2,1)S(1)}, u32[]{:S(2)}, u32[]{:S(2)}) collective-permute-start(bf16[128,1536]{1,0:T(8,128)(2,1)} %get-tuple-element.20.refs_0_), channel_id=1, source_target_pairs={{0,8},{8,0},{16,24},{24,16},{1,9},{9,1},{17,25},{25,17},{2,10},{10... | collective-permute-start | bytes 1179656 | tf_op jit(solution)/shard_map/ppermute | solution.py:23
  6.8 1.5 %collective-permute-start.6 = (bf16[128,1536]{1,0:T(8,128)(2,1)}, bf16[128,1536]{1,0:T(8,128)(2,1)S(1)}, u32[]{:S(2)}, u32[]{:S(2)}) collective-permute-start(bf16[128,1536]{1,0:T(8,128)(2,1)} %get-tuple-element.20.refs_0_), channel_id=1, source_target_pairs={{0,16},{8,24},{16,0},{24,8},{1,17},{9,25},{17,1},{25,9},{2,18},{10... | collective-permute-start | bytes 1179656 | tf_op jit(solution)/shard_map/ppermute | solution.py:23
  8.3 1.6 %collective-permute-start.1 = (bf16[8,1536]{1,0:T(8,128)(2,1)}, bf16[8,1536]{1,0:T(8,128)(2,1)S(1)}, u32[]{:S(2)}, u32[]{:S(2)}) collective-permute-start(bf16[8,1536]{1,0:T(8,128)(2,1)} %get-tuple-element.21.refs_3_.refs_0_), channel_id=1, source_target_pairs={{0,2},{1,3},{2,0},{3,1},{4,6},{5,7},{6,4},{7,5},{8,10},{9,11},{10,... | collective-permute-start | bytes 73736 | tf_op jit(solution)/shard_map/ppermute | solution.py:23
  9.9 1.1 %copy-done.3 = bf16[1,512,768]{2,1,0:T(8,128)(2,1)S(1)} copy-done((bf16[1,512,768]{2,1,0:T(8,128)(2,1)S(1)}, bf16[1,512,768]{2,1,0:T(8,128)(2,1)}, u32[]{:S(2)}) %copy-start.3) | copy-done | bytes 786456
  11.0 0.7 %copy-done.7 = bf16[8,1536]{1,0:T(8,128)(2,1)S(1)} copy-done((bf16[8,1536]{1,0:T(8,128)(2,1)S(1)}, bf16[8,1536]{1,0:T(8,128)(2,1)}, u32[]{:S(2)}) %copy-start.7) | copy-done | bytes 24600
  11.8 2.9 %shard_map.56 = (f32[384,512]{1,0:T(8,128)S(1)}, f32[6,512]{1,0:T(8,128)S(1)}, f32[6,512]{1,0:T(8,128)S(1)}) custom-call(bf16[512,768]{1,0:T(8,128)(2,1)S(1)} %bitcast.10, bf16[512,768]{1,0:T(8,128)(2,1)S(1)} %bitcast.5, bf16[512,768]{1,0:T(8,128)(2,1)S(1)} %bitcast.8, bf16[8,1536]{1,0:T(8,128)(2,1)S(1)} %copy-done.7), custom_call_target="tpu_custom_call" | custom-call | flops 1610612736 | bytes 1572864 | tf_op jit(solution)/shard_map/pallas_call | solution.py:307
  14.7 0.0 copy-start.6
  14.7 2.7 %collective-permute-start.2 = (bf16[16,1536]{1,0:T(8,128)(2,1)S(1)}, bf16[16,1536]{1,0:T(8,128)(2,1)S(1)}, u32[]{:S(2)}, u32[]{:S(2)}) collective-permute-start(bf16[16,1536]{1,0:T(8,128)(2,1)S(1)} %shard_map.57.refs_3_.refs_0_), channel_id=1, source_target_pairs={{0,4},{1,5},{2,6},{3,7},{4,0},{5,1},{6,2},{7,3},{8,12},{9,13},{10,... | collective-permute-start | bytes 147464 | tf_op jit(solution)/shard_map/ppermute | solution.py:23
  17.4 2.9 %shard_map.58 = (f32[384,512]{1,0:T(8,128)S(1)}, f32[6,512]{1,0:T(8,128)S(1)}, f32[6,512]{1,0:T(8,128)S(1)}) custom-call(bf16[512,768]{1,0:T(8,128)(2,1)S(1)} %bitcast.11, bf16[512,768]{1,0:T(8,128)(2,1)S(1)} %bitcast.6, bf16[512,768]{1,0:T(8,128)(2,1)S(1)} %bitcast.9, bf16[16,1536]{1,0:T(8,128)(2,1)S(1)} %shard_map.57.refs_3_.refs_0_), custom_call_target="tpu_custom_call" | custom-call | flops 1610612736 | bytes 1572864 | tf_op jit(solution)/shard_map/pallas_call | solution.py:307
  20.4 0.0 collective-permute-done.2.refs_1_
  20.4 0.0 collective-permute-done.6.refs_2_
  20.5 0.1 collective-permute-start.7
  20.6 0.8 %copy-done.5 = bf16[128,1536]{1,0:T(8,128)(2,1)S(1)} copy-done((bf16[128,1536]{1,0:T(8,128)(2,1)S(1)}, bf16[128,1536]{1,0:T(8,128)(2,1)}, u32[]{:S(2)}) %copy-start.5) | copy-done | bytes 393240
  21.4 0.6 %collective-permute-start.4 = (bf16[160,1536]{1,0:T(8,128)(2,1)S(1)}, bf16[160,1536]{1,0:T(8,128)(2,1)S(1)}, u32[]{:S(2)}, u32[]{:S(2)}) collective-permute-start(bf16[160,1536]{1,0:T(8,128)(2,1)S(1)} %shard_map.61), channel_id=1, source_target_pairs={{0,8},{8,0},{16,24},{24,16},{1,9},{9,1},{17,25},{25,17},{2,10},{10... | collective-permute-start | bytes 1474568 | tf_op jit(solution)/shard_map/ppermute | solution.py:23
  22.0 0.5 %collective-permute-start.3 = (bf16[160,1536]{1,0:T(8,128)(2,1)S(1)}, bf16[160,1536]{1,0:T(8,128)(2,1)S(1)}, u32[]{:S(2)}, u32[]{:S(2)}) collective-permute-start(bf16[160,1536]{1,0:T(8,128)(2,1)S(1)} %shard_map.60.refs_3_), channel_id=1, source_target_pairs={{0,16},{8,24},{16,0},{24,8},{1,17},{9,25},{17,1},{25,9},{2,18},{10... | collective-permute-start | bytes 1474568 | tf_op jit(solution)/shard_map/ppermute | solution.py:23
  22.5 2.4 %collective-permute-start.5 = (bf16[32,1536]{1,0:T(8,128)(2,1)S(1)}, bf16[32,1536]{1,0:T(8,128)(2,1)S(1)}, u32[]{:S(2)}, u32[]{:S(2)}) collective-permute-start(bf16[32,1536]{1,0:T(8,128)(2,1)S(1)} %shard_map.59.refs_1_.refs_2_.refs_4_), channel_id=1, source_target_pairs={{0,24},{8,16},{16,8},{24,0},{1,25},{9,17},{17,9},{25,1},{2,26},{10... | collective-permute-start | bytes 294920 | tf_op jit(solution)/shard_map/ppermute | solution.py:23
  25.0 5.5 %shard_map.63 = (f32[768,512]{1,0:T(8,128)S(1)}, f32[12,512]{1,0:T(8,128)S(1)}, f32[12,512]{1,0:T(8,128)S(1)}) custom-call(bf16[512,768]{1,0:T(8,128)(2,1)S(1)} %bitcast.12, bf16[128,1536]{1,0:T(8,128)(2,1)S(1)} %collective-permute-done.refs_0_.refs_1_, bf16[128,1536]{1,0:T(8,128)(2,1)S(1)} %collective-permute-done.6.refs_2_, ...), custom_call_target="tpu_custom_call" | custom-call | flops 3019898880 | bytes 3047424 | tf_op jit(solution)/shard_map/pallas_call | solution.py:307
  30.4 6.0 %collective-permute-done.5.refs_4_.refs_3_ = bf16[32,1536]{1,0:T(8,128)(2,1)S(1)} collective-permute-done((bf16[32,1536]{1,0:T(8,128)(2,1)S(1)}, bf16[32,1536]{1,0:T(8,128)(2,1)S(1)}, u32[]{:S(2)}, u32[]{:S(2)}) %collective-permute-start.5) | collective-permute-done | bytes 98336 | tf_op jit(solution)/shard_map/ppermute | solution.py:23
  36.5 0.2 collective-permute-done.3.refs_0_.refs_3_.refs_2_
  36.7 0.1 collective-permute-start.8
  36.8 0.0 copy-start
  36.8 4.2 %shard_map.65 = (f32[768,512]{1,0:T(8,128)S(1)}, f32[12,512]{1,0:T(8,128)S(1)}, f32[12,512]{1,0:T(8,128)S(1)}) custom-call(bf16[512,768]{1,0:T(8,128)(2,1)S(1)} %bitcast.13, bf16[160,1536]{1,0:T(8,128)(2,1)S(1)} %collective-permute-done.4.refs_2_.refs_1_, bf16[160,1536]{1,0:T(8,128)(2,1)S(1)} %collective-permute-done.3.refs_0_.refs_3_.refs_2_, ...), custom_call_target="tpu_custom_call" | custom-call | flops 2214592512 | bytes 2654208 | tf_op jit(solution)/shard_map/pallas_call | solution.py:307
  41.1 5.2 %shard_map.66 = bf16[512,768]{1,0:T(8,128)(2,1)} custom-call(bf16[512,768]{1,0:T(8,128)(2,1)S(1)} %bitcast.14, bf16[192,1536]{1,0:T(8,128)(2,1)S(1)} %collective-permute-done.8.refs_1_, f32[768,512]{1,0:T(8,128)S(1)} %get-tuple-element.32.refs_2_, f32[12,512]{1,0:T(8,128)S(1)} %get-tuple-element.33.refs_3_, f32[12,512]{1,0:T(8,128)S(1)} %get-tuple-element.34.refs_4_, ...), custom_call_target="tpu_custom_call" | custom-call | flops 1207959552 | bytes 2162688 | tf_op jit(solution)/shard_map/pallas_call | solution.py:307
  (22 shorter events, 0.2 us)
Async XLA Ops:
  0.0 9.9 %copy-start.1 = (bf16[1,512,768]{2,1,0:T(8,128)(2,1)S(1)}, bf16[1,512,768]{2,1,0:T(8,128)(2,1)}, u32[]{:S(2)}) copy-start(bf16[1,512,768]{2,1,0:T(8,128)(2,1)} %param.6) | copy-start | bytes 2359300
  0.0 9.9 %copy-start.2 = (bf16[1,512,768]{2,1,0:T(8,128)(2,1)S(1)}, bf16[1,512,768]{2,1,0:T(8,128)(2,1)}, u32[]{:S(2)}) copy-start(bf16[1,512,768]{2,1,0:T(8,128)(2,1)} %param.7) | copy-start | bytes 2359300
  3.8 16.6 %collective-permute-start = (bf16[128,1536]{1,0:T(8,128)(2,1)}, bf16[128,1536]{1,0:T(8,128)(2,1)S(1)}, u32[]{:S(2)}, u32[]{:S(2)}) collective-permute-start(bf16[128,1536]{1,0:T(8,128)(2,1)} %get-tuple-element.20.refs_0_), channel_id=1, source_target_pairs={{0,8},{8,0},{16,24},{24,16},{1,9},{9,1},{17,25},{25,17},{2,10},{10... | collective-permute-start | bytes 1179656 | tf_op jit(solution)/shard_map/ppermute | solution.py:23
  6.8 13.7 %collective-permute-start.6 = (bf16[128,1536]{1,0:T(8,128)(2,1)}, bf16[128,1536]{1,0:T(8,128)(2,1)S(1)}, u32[]{:S(2)}, u32[]{:S(2)}) collective-permute-start(bf16[128,1536]{1,0:T(8,128)(2,1)} %get-tuple-element.20.refs_0_), channel_id=1, source_target_pairs={{0,16},{8,24},{16,0},{24,8},{1,17},{9,25},{17,1},{25,9},{2,18},{10... | collective-permute-start | bytes 1179656 | tf_op jit(solution)/shard_map/ppermute | solution.py:23
  8.3 6.4 %collective-permute-start.1 = (bf16[8,1536]{1,0:T(8,128)(2,1)}, bf16[8,1536]{1,0:T(8,128)(2,1)S(1)}, u32[]{:S(2)}, u32[]{:S(2)}) collective-permute-start(bf16[8,1536]{1,0:T(8,128)(2,1)} %get-tuple-element.21.refs_3_.refs_0_), channel_id=1, source_target_pairs={{0,2},{1,3},{2,0},{3,1},{4,6},{5,7},{6,4},{7,5},{8,10},{9,11},{10,... | collective-permute-start | bytes 73736 | tf_op jit(solution)/shard_map/ppermute | solution.py:23
  9.9 1.1 %copy-start.3 = (bf16[1,512,768]{2,1,0:T(8,128)(2,1)S(1)}, bf16[1,512,768]{2,1,0:T(8,128)(2,1)}, u32[]{:S(2)}) copy-start(bf16[1,512,768]{2,1,0:T(8,128)(2,1)} %param.5) | copy-start | bytes 2359300
  11.0 0.7 %copy-start.7 = (bf16[8,1536]{1,0:T(8,128)(2,1)S(1)}, bf16[8,1536]{1,0:T(8,128)(2,1)}, u32[]{:S(2)}) copy-start(bf16[8,1536]{1,0:T(8,128)(2,1)} %get-tuple-element.21.refs_3_.refs_0_) | copy-start | bytes 73732
  11.8 5.6 %copy-start.4 = (bf16[1,512,768]{2,1,0:T(8,128)(2,1)S(1)}, bf16[1,512,768]{2,1,0:T(8,128)(2,1)}, u32[]{:S(2)}) copy-start(bf16[1,512,768]{2,1,0:T(8,128)(2,1)} %param.5) | copy-start | bytes 2359300
  14.7 5.7 %copy-start.6 = (bf16[128,1536]{1,0:T(8,128)(2,1)S(1)}, bf16[128,1536]{1,0:T(8,128)(2,1)}, u32[]{:S(2)}) copy-start(bf16[128,1536]{1,0:T(8,128)(2,1)} %get-tuple-element.20.refs_0_) | copy-start | bytes 1179652
  14.7 5.6 %collective-permute-start.2 = (bf16[16,1536]{1,0:T(8,128)(2,1)S(1)}, bf16[16,1536]{1,0:T(8,128)(2,1)S(1)}, u32[]{:S(2)}, u32[]{:S(2)}) collective-permute-start(bf16[16,1536]{1,0:T(8,128)(2,1)S(1)} %shard_map.57.refs_3_.refs_0_), channel_id=1, source_target_pairs={{0,4},{1,5},{2,6},{3,7},{4,0},{5,1},{6,2},{7,3},{8,12},{9,13},{10,... | collective-permute-start | bytes 147464 | tf_op jit(solution)/shard_map/ppermute | solution.py:23
  20.4 1.0 %copy-start.5 = (bf16[128,1536]{1,0:T(8,128)(2,1)S(1)}, bf16[128,1536]{1,0:T(8,128)(2,1)}, u32[]{:S(2)}) copy-start(bf16[128,1536]{1,0:T(8,128)(2,1)} %get-tuple-element.24.refs_0_) | copy-start | bytes 1179652
  20.5 4.5 %collective-permute-start.7 = (bf16[192,1536]{1,0:T(8,128)(2,1)S(1)}, bf16[192,1536]{1,0:T(8,128)(2,1)S(1)}, u32[]{:S(2)}, u32[]{:S(2)}) collective-permute-start(bf16[192,1536]{1,0:T(8,128)(2,1)S(1)} %shard_map.62), channel_id=1, source_target_pairs={{0,1},{1,0},{2,3},{3,2},{4,5},{5,4},{6,7},{7,6},{8,9},{9,8},{10,11... | collective-permute-start | bytes 1769480 | tf_op jit(solution)/shard_map/ppermute | solution.py:23
  21.4 15.1 %collective-permute-start.4 = (bf16[160,1536]{1,0:T(8,128)(2,1)S(1)}, bf16[160,1536]{1,0:T(8,128)(2,1)S(1)}, u32[]{:S(2)}, u32[]{:S(2)}) collective-permute-start(bf16[160,1536]{1,0:T(8,128)(2,1)S(1)} %shard_map.61), channel_id=1, source_target_pairs={{0,8},{8,0},{16,24},{24,16},{1,9},{9,1},{17,25},{25,17},{2,10},{10... | collective-permute-start | bytes 1474568 | tf_op jit(solution)/shard_map/ppermute | solution.py:23
  22.0 14.7 %collective-permute-start.3 = (bf16[160,1536]{1,0:T(8,128)(2,1)S(1)}, bf16[160,1536]{1,0:T(8,128)(2,1)S(1)}, u32[]{:S(2)}, u32[]{:S(2)}) collective-permute-start(bf16[160,1536]{1,0:T(8,128)(2,1)S(1)} %shard_map.60.refs_3_), channel_id=1, source_target_pairs={{0,16},{8,24},{16,0},{24,8},{1,17},{9,25},{17,1},{25,9},{2,18},{10... | collective-permute-start | bytes 1474568 | tf_op jit(solution)/shard_map/ppermute | solution.py:23
  22.5 14.0 %collective-permute-start.5 = (bf16[32,1536]{1,0:T(8,128)(2,1)S(1)}, bf16[32,1536]{1,0:T(8,128)(2,1)S(1)}, u32[]{:S(2)}, u32[]{:S(2)}) collective-permute-start(bf16[32,1536]{1,0:T(8,128)(2,1)S(1)} %shard_map.59.refs_1_.refs_2_.refs_4_), channel_id=1, source_target_pairs={{0,24},{8,16},{16,8},{24,0},{1,25},{9,17},{17,9},{25,1},{2,26},{10... | collective-permute-start | bytes 294920 | tf_op jit(solution)/shard_map/ppermute | solution.py:23
  36.7 4.3 %collective-permute-start.8 = (bf16[192,1536]{1,0:T(8,128)(2,1)S(1)}, bf16[192,1536]{1,0:T(8,128)(2,1)S(1)}, u32[]{:S(2)}, u32[]{:S(2)}) collective-permute-start(bf16[192,1536]{1,0:T(8,128)(2,1)S(1)} %shard_map.64), channel_id=1, source_target_pairs={{0,1},{1,0},{2,3},{3,2},{4,5},{5,4},{6,7},{7,6},{8,9},{9,8},{10,11... | collective-permute-start | bytes 1769480 | tf_op jit(solution)/shard_map/ppermute | solution.py:23
  36.8 4.3 %copy-start = (bf16[768,768]{1,0:T(8,128)(2,1)S(1)}, bf16[768,768]{1,0:T(8,128)(2,1)}, u32[]{:S(2)}) copy-start(bf16[768,768]{1,0:T(8,128)(2,1)} %refs_5_.1) | copy-start | bytes 3538948
where the time goes:
time: 46.6 us; the launch traced here: 46.3 us
  Pallas kernels  24.7 us (53%)
  starting transfers between devices  12.5 us (27%)
  waiting for transfers between devices  6.26 us (13%)
  local copies, waits for them, and re-layouts  2.68 us (6%)
    pallas_call x5, Pallas kernels, attend(): pl.pallas_call(kernel, out_shape=out_shape, grid=(1,) if part[1] > 1 else...  20.8 us
    ppermute x9, starting transfers between devices, across(): lax.ppermute(block, axis, [(i, i ^ flip) for i in range(lax.axis_size(axi...  12.5 us
    ppermute x9, waiting for transfers between devices, across(): lax.ppermute(block, axis, [(i, i ^ flip) for i in range(lax.axis_size(axi...  6.26 us
    pallas_call x1, Pallas kernels, order_rows(): pl.pallas_call(kernel, out_shape=[jax.ShapeDtypeStruct((high - low, 2 * w...  3.77 us
    unnamed x16, local copies, waits for them, and re-layouts  2.68 us
  transfers between devices with their start and end apart: 9, of which 2 were waited for; matrix products, arithmetic and copies ran while one was open for 0% of the time, Pallas kernels for 34%

commit v1 on v0

--- a/solution.py
+++ b/solution.py
@@ -12,6 +12,7 @@
 GSTEP = 64
 PAIR = 2 * HEAD_DIM
 CHUNK = 256
+KEY_CHUNK = 512
 LANES = 128
 LOG2E = math.log2(math.e)
 VMEM_BYTES = 16 * 1024 * 1024
@@ -62,30 +63,23 @@
 def order_rows(select, key_rows, values, prefixes):
     tokens, width = key_rows.shape
 
-    pieces = [
-        (half, low, min(CHUNK, width - low)) for half in range(2) for low in range(0, width, CHUNK)
-    ]
-
     def kernel(select_hbm, key_hbm, value_hbm, *refs):
         out_refs, (select_ref, row_ref, sems) = refs[: len(prefixes)], refs[len(prefixes) :]
-        copies = [pltpu.make_async_copy(select_hbm, select_ref, sems.at[0])]
-        for at, (half, low, size) in enumerate(pieces):
-            source = (key_hbm, value_hbm)[half].at[:, low : low + size]
-            target = row_ref.at[half, :, low : low + size]
-            copies.append(pltpu.make_async_copy(source, target, sems.at[1 + at]))
+        copies = [
+            pltpu.make_async_copy(select_hbm, select_ref, sems.at[0]),
+            pltpu.make_async_copy(key_hbm, row_ref.at[0], sems.at[1]),
+            pltpu.make_async_copy(value_hbm, row_ref.at[1], sems.at[2]),
+        ]
         for copy in copies:
             copy.start()
         copies[0].wait()
-        for copy, (half, low, size) in zip(copies[1:], pieces):
-            copy.wait()
+        for half in range(2):
+            copies[1 + half].wait()
             moved = jnp.dot(
-                select_ref[...],
-                row_ref[half, :, low : low + size],
-                preferred_element_type=jnp.float32,
+                select_ref[...], row_ref[half], preferred_element_type=jnp.float32
             ).astype(jnp.bfloat16)
-            cols = slice(half * width + low, half * width + low + size)
-            for (first, last), out_ref in zip(prefixes, out_refs):
-                out_ref[:, cols] = moved[first:last]
+            for (low, high), out_ref in zip(prefixes, out_refs):
+                out_ref[:, half * width : (half + 1) * width] = moved[low:high]
 
     return pl.pallas_call(
         kernel,
@@ -96,7 +90,7 @@
         scratch_shapes=[
             pltpu.VMEM(select.shape, jnp.bfloat16),
             pltpu.VMEM((2, tokens, width), jnp.bfloat16),
-            pltpu.SemaphoreType.DMA((1 + len(pieces),)),
+            pltpu.SemaphoreType.DMA((3,)),
         ],
         compiler_params=pltpu.CompilerParams(vmem_limit_bytes=FETCH_VMEM_BYTES),
         cost_estimate=pl.CostEstimate(
@@ -132,7 +126,7 @@
             weight_ref, out_ref, attended_ref = refs.pop(0), refs.pop(0), refs.pop(-1)
         else:
             numer_out, peak_out, total_out = [refs.pop(0) for _ in range(3)]
-        score_ref, value_ref = refs.pop(0), refs.pop(0)
+        score_ref, value_ref, key_ref = refs.pop(0), refs.pop(0), refs.pop(0)
         if row_strides is not None:
             offset_ref = refs.pop(0)
             row = lax.broadcasted_iota(jnp.int32, (keys, LANES), 0)
@@ -143,13 +137,7 @@
             offset_ref[...] = offsets
 
         ones = jnp.ones((16, padded), jnp.bfloat16)
-        key_chunks = []
-        at = 0
-        for entry, size in zip(set_refs, sizes):
-            for low in range(0, size, CHUNK):
-                count = min(CHUNK, size - low)
-                key_chunks.append((entry[0], low, count, at))
-                at += count
+        key_chunks = [(low, min(KEY_CHUNK, keys - low)) for low in range(0, keys, KEY_CHUNK)]
         value_chunks = [(low, min(CHUNK, padded - low)) for low in range(0, padded, CHUNK)]
 
         def column(pair):
@@ -161,14 +149,18 @@
             own = (row < HEAD_DIM) if half == 0 else (row >= HEAD_DIM)
             return jnp.where(own, turned, jnp.zeros_like(turned))
 
-        def score(pair, half, query_head, chunk, running):
-            ref, low, count, at = chunk
+        def load_keys(pair):
+            at = 0
+            for (ref, _, _, _), size in zip(set_refs, sizes):
+                key_ref[at : at + size, :] = ref[:, pl.ds(column(pair), PAIR)]
+                at += size
+
+        def score(half, query_head, chunk, running):
+            low, count = chunk
             scores = jnp.dot(
-                ref[low : low + count, pl.ds(column(pair), PAIR)],
-                query_head,
-                preferred_element_type=jnp.float32,
+                key_ref[low : low + count, :], query_head, preferred_element_type=jnp.float32
             )
-            score_ref[half, at : at + count, :] = scores
+            score_ref[half, low : low + count, :] = scores
             tallest = jnp.max(scores.reshape(count // 8, 8, tokens), axis=0)
             return tallest if running is None else jnp.maximum(running, tallest)
 
@@ -231,12 +223,14 @@
                 weighted = jnp.concatenate(
                     [values_t[half * HEAD_DIM : (half + 1) * HEAD_DIM], ones], axis=0
                 )
+                if next_half == 0:
+                    load_keys(next_pair)
                 query_head = head_queries(next_pair, next_half)
                 next_running, gathered = None, None
                 for step in range(max(len(key_chunks), len(value_chunks))):
                     if step < len(key_chunks):
                         next_running = score(
-                            next_pair, next_half, query_head, key_chunks[step], next_running
+                            next_half, query_head, key_chunks[step], next_running
                         )
                     if step < len(value_chunks):
                         gathered = weigh(half, peak, weighted, value_chunks[step], gathered)
@@ -255,10 +249,11 @@
                 later = jnp.minimum(pair + 1, last_pair - 1)
                 return overlap(pair, 1, running, values_t, later, 0)
 
+            load_keys(first_pair)
             first_head = head_queries(first_pair, 0)
             running = None
             for chunk in key_chunks:
-                running = score(first_pair, 0, first_head, chunk, running)
+                running = score(0, first_head, chunk, running)
             lax.fori_loop(first_pair, last_pair, pair_step, running)
 
         for group in range(groups):
@@ -282,6 +277,7 @@
         ]
     scratch = [
         pltpu.VMEM((2, padded, tokens), jnp.float32),
+        pltpu.VMEM((padded, PAIR), jnp.bfloat16),
         pltpu.VMEM((padded, PAIR), jnp.bfloat16),
     ]
     if row_strides is not None:
@@ -363,7 +359,7 @@
                     own_set,
                     row_strides=strides,
                     part=(len(own_states), 2),
-                    wait=moved,
+                    wait=moved if own_states else None,
                 )
             )
         moved = join_after([(moved, 0, moved.shape[0]), (came, 0, came.shape[0])], own_states[-1][1])

time: 46.6 us -> 44.6 us (0.957)
  Pallas kernels: 24.7 us -> 22.8 us
  waiting for transfers between devices: 6.26 us -> 7.04 us
  local copies, waits for them, and re-layouts: 2.68 us -> 1.95 us
    pallas_call x5, Pallas kernels: 20.8 us -> 19.5 us  [attend(): pl.pallas_call(kernel, out_shape=out_shape, grid=(1,) if part[1] > 1 else...]
    ppermute x9, waiting for transfers between devices: 6.26 us -> 7.04 us  [across(): lax.ppermute(block, axis, [(i, i ^ flip) for i in range(lax.axis_size(axi...]
    unnamed x16 -> x14, local copies, waits for them, and re-layouts: 2.68 us -> 1.95 us
    pallas_call x1, Pallas kernels: 3.77 us -> 3.08 us  [order_rows(): pl.pallas_call(kernel, out_shape=[jax.ShapeDtypeStruct((high - low, 2 * w...]
  transfers between devices with their start and end apart: 9 -> 9, of which waited for: 2 -> 2; matrix products, arithmetic and copies ran while one was open for 0% -> 0% of each run, Pallas kernels for 34% -> 32%
where the time goes in v1:
time: 44.6 us; the launch traced here: 44.4 us
  Pallas kernels  22.8 us (51%)
  starting transfers between devices  12.4 us (28%)
  waiting for transfers between devices  7.04 us (16%)
  local copies, waits for them, and re-layouts  1.95 us (4%)
    pallas_call x5, Pallas kernels, attend(): pl.pallas_call(kernel, out_shape=out_shape, grid=(1,) if part[1] > 1 else...  19.5 us
    ppermute x9, starting transfers between devices, across(): lax.ppermute(block, axis, [(i, i ^ flip) for i in range(lax.axis_size(axi...  12.4 us
    ppermute x9, waiting for transfers between devices, across(): lax.ppermute(block, axis, [(i, i ^ flip) for i in range(lax.axis_size(axi...  7.04 us
    pallas_call x1, Pallas kernels, order_rows(): pl.pallas_call(kernel, out_shape=[jax.ShapeDtypeStruct((high - low, 2 * w...  3.08 us
    unnamed x14, local copies, waits for them, and re-layouts  1.95 us
  transfers between devices with their start and end apart: 9, of which 2 were waited for; matrix products, arithmetic and copies ran while one was open for 0% of the time, Pallas kernels for 32%

profile of v1, /device:TPU:0, one launch (start us, length us, event | category | flops | bytes accessed | tf_op | source)
XLA Modules:
  0.0 44.4 jit_solution(16521179611140787903)
XLA Ops:
  0.0 3.1 %shard_map.55 = (bf16[128,1536]{1,0:T(8,128)(2,1)}, bf16[128,1536]{1,0:T(8,128)(2,1)}, bf16[8,1536]{1,0:T(8,128)(2,1)}) custom-call(bf16[256,512]{1,0:T(8,128)(2,1)} %constant.2.clone.select_hbm, bf16[512,768]{1,0:T(8,128)(2,1)} %bitcast.4, bf16[512,768]{1,0:T(8,128)(2,1)} %bitcast.7), custom_call_target="tpu_custom_call" | custom-call | flops 402653184 | bytes 2359296 | tf_op jit(solution)/shard_map/pallas_call | solution.py:84
  3.1 3.0 %collective-permute-start = (bf16[128,1536]{1,0:T(8,128)(2,1)}, bf16[128,1536]{1,0:T(8,128)(2,1)S(1)}, u32[]{:S(2)}, u32[]{:S(2)}) collective-permute-start(bf16[128,1536]{1,0:T(8,128)(2,1)} %get-tuple-element.20.refs_0_), channel_id=1, source_target_pairs={{0,8},{8,0},{16,24},{24,16},{1,9},{9,1},{17,25},{25,17},{2,10},{10... | collective-permute-start | bytes 1179656 | tf_op jit(solution)/shard_map/ppermute | solution.py:24
  6.1 1.5 %collective-permute-start.6 = (bf16[128,1536]{1,0:T(8,128)(2,1)}, bf16[128,1536]{1,0:T(8,128)(2,1)S(1)}, u32[]{:S(2)}, u32[]{:S(2)}) collective-permute-start(bf16[128,1536]{1,0:T(8,128)(2,1)} %get-tuple-element.20.refs_0_), channel_id=1, source_target_pairs={{0,16},{8,24},{16,0},{24,8},{1,17},{9,25},{17,1},{25,9},{2,18},{10... | collective-permute-start | bytes 1179656 | tf_op jit(solution)/shard_map/ppermute | solution.py:24
  7.6 1.6 %collective-permute-start.1 = (bf16[8,1536]{1,0:T(8,128)(2,1)}, bf16[8,1536]{1,0:T(8,128)(2,1)S(1)}, u32[]{:S(2)}, u32[]{:S(2)}) collective-permute-start(bf16[8,1536]{1,0:T(8,128)(2,1)} %get-tuple-element.21.refs_0_), channel_id=1, source_target_pairs={{0,2},{1,3},{2,0},{3,1},{4,6},{5,7},{6,4},{7,5},{8,10},{9,11},{10,... | collective-permute-start | bytes 73736 | tf_op jit(solution)/shard_map/ppermute | solution.py:24
  9.2 1.1 %copy-done.3 = bf16[1,512,768]{2,1,0:T(8,128)(2,1)S(1)} copy-done((bf16[1,512,768]{2,1,0:T(8,128)(2,1)S(1)}, bf16[1,512,768]{2,1,0:T(8,128)(2,1)}, u32[]{:S(2)}) %copy-start.3) | copy-done | bytes 786456
  10.3 2.9 %shard_map.56 = (f32[384,512]{1,0:T(8,128)S(1)}, f32[6,512]{1,0:T(8,128)S(1)}, f32[6,512]{1,0:T(8,128)S(1)}) custom-call(bf16[512,768]{1,0:T(8,128)(2,1)S(1)} %bitcast.10, bf16[512,768]{1,0:T(8,128)(2,1)S(1)} %bitcast.5, bf16[512,768]{1,0:T(8,128)(2,1)S(1)} %bitcast.8), custom_call_target="tpu_custom_call" | custom-call | flops 1610612736 | bytes 1572864 | tf_op jit(solution)/shard_map/pallas_call | solution.py:303
  13.3 0.0 copy-start.5
  13.3 2.7 %collective-permute-start.2 = (bf16[16,1536]{1,0:T(8,128)(2,1)S(1)}, bf16[16,1536]{1,0:T(8,128)(2,1)S(1)}, u32[]{:S(2)}, u32[]{:S(2)}) collective-permute-start(bf16[16,1536]{1,0:T(8,128)(2,1)S(1)} %shard_map.57.refs_3_.refs_0_), channel_id=1, source_target_pairs={{0,4},{1,5},{2,6},{3,7},{4,0},{5,1},{6,2},{7,3},{8,12},{9,13},{10,... | collective-permute-start | bytes 147464 | tf_op jit(solution)/shard_map/ppermute | solution.py:24
  15.9 2.9 %shard_map.58 = (f32[384,512]{1,0:T(8,128)S(1)}, f32[6,512]{1,0:T(8,128)S(1)}, f32[6,512]{1,0:T(8,128)S(1)}) custom-call(bf16[512,768]{1,0:T(8,128)(2,1)S(1)} %bitcast.11, bf16[512,768]{1,0:T(8,128)(2,1)S(1)} %bitcast.6, bf16[512,768]{1,0:T(8,128)(2,1)S(1)} %bitcast.9, bf16[16,1536]{1,0:T(8,128)(2,1)S(1)} %shard_map.57.refs_3_.refs_0_), custom_call_target="tpu_custom_call" | custom-call | flops 1610612736 | bytes 1572864 | tf_op jit(solution)/shard_map/pallas_call | solution.py:303
  18.9 0.0 collective-permute-done.2.refs_1_
  18.9 0.0 collective-permute-done.refs_0_.refs_1_
  19.0 0.0 collective-permute-done.6.refs_2_
  19.0 0.1 collective-permute-start.7
  19.1 0.8 %copy-done.4 = bf16[128,1536]{1,0:T(8,128)(2,1)S(1)} copy-done((bf16[128,1536]{1,0:T(8,128)(2,1)S(1)}, bf16[128,1536]{1,0:T(8,128)(2,1)}, u32[]{:S(2)}) %copy-start.4) | copy-done | bytes 393240
  19.9 0.6 %collective-permute-start.4 = (bf16[160,1536]{1,0:T(8,128)(2,1)S(1)}, bf16[160,1536]{1,0:T(8,128)(2,1)S(1)}, u32[]{:S(2)}, u32[]{:S(2)}) collective-permute-start(bf16[160,1536]{1,0:T(8,128)(2,1)S(1)} %shard_map.61), channel_id=1, source_target_pairs={{0,8},{8,0},{16,24},{24,16},{1,9},{9,1},{17,25},{25,17},{2,10},{10... | collective-permute-start | bytes 1474568 | tf_op jit(solution)/shard_map/ppermute | solution.py:24
  20.5 0.5 %collective-permute-start.3 = (bf16[160,1536]{1,0:T(8,128)(2,1)S(1)}, bf16[160,1536]{1,0:T(8,128)(2,1)S(1)}, u32[]{:S(2)}, u32[]{:S(2)}) collective-permute-start(bf16[160,1536]{1,0:T(8,128)(2,1)S(1)} %shard_map.60.refs_3_), channel_id=1, source_target_pairs={{0,16},{8,24},{16,0},{24,8},{1,17},{9,25},{17,1},{25,9},{2,18},{10... | collective-permute-start | bytes 1474568 | tf_op jit(solution)/shard_map/ppermute | solution.py:24
  21.0 2.4 %collective-permute-start.5 = (bf16[32,1536]{1,0:T(8,128)(2,1)S(1)}, bf16[32,1536]{1,0:T(8,128)(2,1)S(1)}, u32[]{:S(2)}, u32[]{:S(2)}) collective-permute-start(bf16[32,1536]{1,0:T(8,128)(2,1)S(1)} %shard_map.59.refs_1_.refs_2_.refs_4_), channel_id=1, source_target_pairs={{0,24},{8,16},{16,8},{24,0},{1,25},{9,17},{17,9},{25,1},{2,26},{10... | collective-permute-start | bytes 294920 | tf_op jit(solution)/shard_map/ppermute | solution.py:24
  23.5 4.7 %shard_map.63 = (f32[768,512]{1,0:T(8,128)S(1)}, f32[12,512]{1,0:T(8,128)S(1)}, f32[12,512]{1,0:T(8,128)S(1)}) custom-call(bf16[512,768]{1,0:T(8,128)(2,1)S(1)} %bitcast.12, bf16[128,1536]{1,0:T(8,128)(2,1)S(1)} %collective-permute-done.refs_0_.refs_1_, bf16[128,1536]{1,0:T(8,128)(2,1)S(1)} %collective-permute-done.6.refs_2_, ...), custom_call_target="tpu_custom_call" | custom-call | flops 3019898880 | bytes 3047424 | tf_op jit(solution)/shard_map/pallas_call | solution.py:303
  28.2 6.8 %collective-permute-done.5.refs_4_.refs_3_ = bf16[32,1536]{1,0:T(8,128)(2,1)S(1)} collective-permute-done((bf16[32,1536]{1,0:T(8,128)(2,1)S(1)}, bf16[32,1536]{1,0:T(8,128)(2,1)S(1)}, u32[]{:S(2)}, u32[]{:S(2)}) %collective-permute-start.5) | collective-permute-done | bytes 98336 | tf_op jit(solution)/shard_map/ppermute | solution.py:24
  35.0 0.2 collective-permute-done.3.refs_0_.refs_3_.refs_2_
  35.2 0.1 collective-permute-start.8
  35.3 0.0 copy-start
  35.3 3.8 %shard_map.65 = (f32[768,512]{1,0:T(8,128)S(1)}, f32[12,512]{1,0:T(8,128)S(1)}, f32[12,512]{1,0:T(8,128)S(1)}) custom-call(bf16[512,768]{1,0:T(8,128)(2,1)S(1)} %bitcast.13, bf16[160,1536]{1,0:T(8,128)(2,1)S(1)} %collective-permute-done.4.refs_2_.refs_1_, bf16[160,1536]{1,0:T(8,128)(2,1)S(1)} %collective-permute-done.3.refs_0_.refs_3_.refs_2_, ...), custom_call_target="tpu_custom_call" | custom-call | flops 2214592512 | bytes 2654208 | tf_op jit(solution)/shard_map/pallas_call | solution.py:303
  39.2 5.2 %shard_map.66 = bf16[512,768]{1,0:T(8,128)(2,1)} custom-call(bf16[512,768]{1,0:T(8,128)(2,1)S(1)} %bitcast.14, bf16[192,1536]{1,0:T(8,128)(2,1)S(1)} %collective-permute-done.8.refs_1_, f32[768,512]{1,0:T(8,128)S(1)} %get-tuple-element.32.refs_2_, f32[12,512]{1,0:T(8,128)S(1)} %get-tuple-element.33.refs_3_, f32[12,512]{1,0:T(8,128)S(1)} %get-tuple-element.34.refs_4_, ...), custom_call_target="tpu_custom_call" | custom-call | flops 1207959552 | bytes 2162688 | tf_op jit(solution)/shard_map/pallas_call | solution.py:303
  (20 shorter events, 0.2 us)
Async XLA Ops:
  0.0 9.2 %copy-start.1 = (bf16[1,512,768]{2,1,0:T(8,128)(2,1)S(1)}, bf16[1,512,768]{2,1,0:T(8,128)(2,1)}, u32[]{:S(2)}) copy-start(bf16[1,512,768]{2,1,0:T(8,128)(2,1)} %param.6) | copy-start | bytes 2359300
  0.0 9.2 %copy-start.2 = (bf16[1,512,768]{2,1,0:T(8,128)(2,1)S(1)}, bf16[1,512,768]{2,1,0:T(8,128)(2,1)}, u32[]{:S(2)}) copy-start(bf16[1,512,768]{2,1,0:T(8,128)(2,1)} %param.7) | copy-start | bytes 2359300
  3.1 15.8 %collective-permute-start = (bf16[128,1536]{1,0:T(8,128)(2,1)}, bf16[128,1536]{1,0:T(8,128)(2,1)S(1)}, u32[]{:S(2)}, u32[]{:S(2)}) collective-permute-start(bf16[128,1536]{1,0:T(8,128)(2,1)} %get-tuple-element.20.refs_0_), channel_id=1, source_target_pairs={{0,8},{8,0},{16,24},{24,16},{1,9},{9,1},{17,25},{25,17},{2,10},{10... | collective-permute-start | bytes 1179656 | tf_op jit(solution)/shard_map/ppermute | solution.py:24
  6.1 12.9 %collective-permute-start.6 = (bf16[128,1536]{1,0:T(8,128)(2,1)}, bf16[128,1536]{1,0:T(8,128)(2,1)S(1)}, u32[]{:S(2)}, u32[]{:S(2)}) collective-permute-start(bf16[128,1536]{1,0:T(8,128)(2,1)} %get-tuple-element.20.refs_0_), channel_id=1, source_target_pairs={{0,16},{8,24},{16,0},{24,8},{1,17},{9,25},{17,1},{25,9},{2,18},{10... | collective-permute-start | bytes 1179656 | tf_op jit(solution)/shard_map/ppermute | solution.py:24
  7.6 5.6 %collective-permute-start.1 = (bf16[8,1536]{1,0:T(8,128)(2,1)}, bf16[8,1536]{1,0:T(8,128)(2,1)S(1)}, u32[]{:S(2)}, u32[]{:S(2)}) collective-permute-start(bf16[8,1536]{1,0:T(8,128)(2,1)} %get-tuple-element.21.refs_0_), channel_id=1, source_target_pairs={{0,2},{1,3},{2,0},{3,1},{4,6},{5,7},{6,4},{7,5},{8,10},{9,11},{10,... | collective-permute-start | bytes 73736 | tf_op jit(solution)/shard_map/ppermute | solution.py:24
  9.2 1.1 %copy-start.3 = (bf16[1,512,768]{2,1,0:T(8,128)(2,1)S(1)}, bf16[1,512,768]{2,1,0:T(8,128)(2,1)}, u32[]{:S(2)}) copy-start(bf16[1,512,768]{2,1,0:T(8,128)(2,1)} %param.5) | copy-start | bytes 2359300
  10.3 2.9 %copy-start.6 = (bf16[8,1536]{1,0:T(8,128)(2,1)S(1)}, bf16[8,1536]{1,0:T(8,128)(2,1)}, u32[]{:S(2)}) copy-start(bf16[8,1536]{1,0:T(8,128)(2,1)} %get-tuple-element.21.refs_0_) | copy-start | bytes 73732
  13.3 5.7 %copy-start.5 = (bf16[128,1536]{1,0:T(8,128)(2,1)S(1)}, bf16[128,1536]{1,0:T(8,128)(2,1)}, u32[]{:S(2)}) copy-start(bf16[128,1536]{1,0:T(8,128)(2,1)} %get-tuple-element.20.refs_0_) | copy-start | bytes 1179652
  13.3 5.6 %collective-permute-start.2 = (bf16[16,1536]{1,0:T(8,128)(2,1)S(1)}, bf16[16,1536]{1,0:T(8,128)(2,1)S(1)}, u32[]{:S(2)}, u32[]{:S(2)}) collective-permute-start(bf16[16,1536]{1,0:T(8,128)(2,1)S(1)} %shard_map.57.refs_3_.refs_0_), channel_id=1, source_target_pairs={{0,4},{1,5},{2,6},{3,7},{4,0},{5,1},{6,2},{7,3},{8,12},{9,13},{10,... | collective-permute-start | bytes 147464 | tf_op jit(solution)/shard_map/ppermute | solution.py:24
  18.9 1.0 %copy-start.4 = (bf16[128,1536]{1,0:T(8,128)(2,1)S(1)}, bf16[128,1536]{1,0:T(8,128)(2,1)}, u32[]{:S(2)}) copy-start(bf16[128,1536]{1,0:T(8,128)(2,1)} %get-tuple-element.24.refs_0_) | copy-start | bytes 1179652
  19.0 4.5 %collective-permute-start.7 = (bf16[192,1536]{1,0:T(8,128)(2,1)S(1)}, bf16[192,1536]{1,0:T(8,128)(2,1)S(1)}, u32[]{:S(2)}, u32[]{:S(2)}) collective-permute-start(bf16[192,1536]{1,0:T(8,128)(2,1)S(1)} %shard_map.62), channel_id=1, source_target_pairs={{0,1},{1,0},{2,3},{3,2},{4,5},{5,4},{6,7},{7,6},{8,9},{9,8},{10,11... | collective-permute-start | bytes 1769480 | tf_op jit(solution)/shard_map/ppermute | solution.py:24
  19.9 15.1 %collective-permute-start.4 = (bf16[160,1536]{1,0:T(8,128)(2,1)S(1)}, bf16[160,1536]{1,0:T(8,128)(2,1)S(1)}, u32[]{:S(2)}, u32[]{:S(2)}) collective-permute-start(bf16[160,1536]{1,0:T(8,128)(2,1)S(1)} %shard_map.61), channel_id=1, source_target_pairs={{0,8},{8,0},{16,24},{24,16},{1,9},{9,1},{17,25},{25,17},{2,10},{10... | collective-permute-start | bytes 1474568 | tf_op jit(solution)/shard_map/ppermute | solution.py:24
  20.5 14.7 %collective-permute-start.3 = (bf16[160,1536]{1,0:T(8,128)(2,1)S(1)}, bf16[160,1536]{1,0:T(8,128)(2,1)S(1)}, u32[]{:S(2)}, u32[]{:S(2)}) collective-permute-start(bf16[160,1536]{1,0:T(8,128)(2,1)S(1)} %shard_map.60.refs_3_), channel_id=1, source_target_pairs={{0,16},{8,24},{16,0},{24,8},{1,17},{9,25},{17,1},{25,9},{2,18},{10... | collective-permute-start | bytes 1474568 | tf_op jit(solution)/shard_map/ppermute | solution.py:24
  21.0 13.9 %collective-permute-start.5 = (bf16[32,1536]{1,0:T(8,128)(2,1)S(1)}, bf16[32,1536]{1,0:T(8,128)(2,1)S(1)}, u32[]{:S(2)}, u32[]{:S(2)}) collective-permute-start(bf16[32,1536]{1,0:T(8,128)(2,1)S(1)} %shard_map.59.refs_1_.refs_2_.refs_4_), channel_id=1, source_target_pairs={{0,24},{8,16},{16,8},{24,0},{1,25},{9,17},{17,9},{25,1},{2,26},{10... | collective-permute-start | bytes 294920 | tf_op jit(solution)/shard_map/ppermute | solution.py:24
  35.2 3.9 %collective-permute-start.8 = (bf16[192,1536]{1,0:T(8,128)(2,1)S(1)}, bf16[192,1536]{1,0:T(8,128)(2,1)S(1)}, u32[]{:S(2)}, u32[]{:S(2)}) collective-permute-start(bf16[192,1536]{1,0:T(8,128)(2,1)S(1)} %shard_map.64), channel_id=1, source_target_pairs={{0,1},{1,0},{2,3},{3,2},{4,5},{5,4},{6,7},{7,6},{8,9},{9,8},{10,11... | collective-permute-start | bytes 1769480 | tf_op jit(solution)/shard_map/ppermute | solution.py:24
  35.3 3.9 %copy-start = (bf16[768,768]{1,0:T(8,128)(2,1)S(1)}, bf16[768,768]{1,0:T(8,128)(2,1)}, u32[]{:S(2)}) copy-start(bf16[768,768]{1,0:T(8,128)(2,1)} %refs_5_.1) | copy-start | bytes 3538948

commit v2 on v1

--- a/solution.py
+++ b/solution.py
@@ -13,6 +13,7 @@
 PAIR = 2 * HEAD_DIM
 CHUNK = 256
 KEY_CHUNK = 512
+UNROLL = 3
 LANES = 128
 LOG2E = math.log2(math.e)
 VMEM_BYTES = 16 * 1024 * 1024
@@ -126,7 +127,7 @@
             weight_ref, out_ref, attended_ref = refs.pop(0), refs.pop(0), refs.pop(-1)
         else:
             numer_out, peak_out, total_out = [refs.pop(0) for _ in range(3)]
-        score_ref, value_ref, key_ref = refs.pop(0), refs.pop(0), refs.pop(0)
+        score_ref, value_ref, key_ref, turned_ref = [refs.pop(0) for _ in range(4)]
         if row_strides is not None:
             offset_ref = refs.pop(0)
             row = lax.broadcasted_iota(jnp.int32, (keys, LANES), 0)
@@ -143,13 +144,14 @@
         def column(pair):
             return pl.multiple_of(pair * PAIR, PAIR)
 
-        def head_queries(pair, half):
-            turned = query_ref[:, pl.ds(column(pair), PAIR)].T
+        def head_queries(half):
+            turned = turned_ref[...]
             row = lax.broadcasted_iota(jnp.int32, turned.shape, 0)
             own = (row < HEAD_DIM) if half == 0 else (row >= HEAD_DIM)
             return jnp.where(own, turned, jnp.zeros_like(turned))
 
-        def load_keys(pair):
+        def load(pair):
+            turned_ref[...] = query_ref[:, pl.ds(column(pair), PAIR)].T
             at = 0
             for (ref, _, _, _), size in zip(set_refs, sizes):
                 key_ref[at : at + size, :] = ref[:, pl.ds(column(pair), PAIR)]
@@ -204,7 +206,7 @@
                 start = pl.multiple_of(column(pair) + half * HEAD_DIM, HEAD_DIM)
                 rows = pl.ds(start, HEAD_DIM)
                 if final:
-                    attended_ref[half] = (numer / total).astype(jnp.bfloat16)
+                    attended_ref[half] = (numer * (1.0 / total)).astype(jnp.bfloat16)
                     if half == 1:
                         both = attended_ref[...].reshape(PAIR, tokens)
                         out_ref[:, pl.ds(column(pair), PAIR)] = both.T
@@ -224,8 +226,8 @@
                     [values_t[half * HEAD_DIM : (half + 1) * HEAD_DIM], ones], axis=0
                 )
                 if next_half == 0:
-                    load_keys(next_pair)
-                query_head = head_queries(next_pair, next_half)
+                    load(next_pair)
+                query_head = head_queries(next_half)
                 next_running, gathered = None, None
                 for step in range(max(len(key_chunks), len(value_chunks))):
                     if step < len(key_chunks):
@@ -249,12 +251,12 @@
                 later = jnp.minimum(pair + 1, last_pair - 1)
                 return overlap(pair, 1, running, values_t, later, 0)
 
-            load_keys(first_pair)
-            first_head = head_queries(first_pair, 0)
+            load(first_pair)
+            first_head = head_queries(0)
             running = None
             for chunk in key_chunks:
                 running = score(0, first_head, chunk, running)
-            lax.fori_loop(first_pair, last_pair, pair_step, running)
+            lax.fori_loop(first_pair, last_pair, pair_step, running, unroll=UNROLL)
 
         for group in range(groups):
             one_group(
@@ -279,6 +281,7 @@
         pltpu.VMEM((2, padded, tokens), jnp.float32),
         pltpu.VMEM((padded, PAIR), jnp.bfloat16),
         pltpu.VMEM((padded, PAIR), jnp.bfloat16),
+        pltpu.VMEM((PAIR, tokens), jnp.bfloat16),
     ]
     if row_strides is not None:
         scratch.append(pltpu.VMEM((keys, LANES), jnp.float32))
@@ -370,17 +373,14 @@
     def first_rows(where, count):
         return (where[0], where[1], where[1] + count)
 
-    near_b = across(
-        join_after([(first_b, 0, sends[0] - sends[1]), (far, 0, n_far)], far), "inner", 1
-    )
-    fars[1] = (near_b, sends[0] - sends[1])
+    near_b = across(first_b, "inner", 1)
+    fars[1] = (across(far, "inner", 1), 0)
     own_done = far
 
     known = [0] + [1 << bit for bit in range(inner_bits)]
     late = [d for d in range(n_inner) if d not in known]
     last = sends[inner_bits]
-    late_sets = [near_b]
-    late_counts = [prefix_counts(0, sends[1], sends[0]), np.ones(n_far, np.int64)]
+    late_sets, late_counts = [], []
     for bit in range(1, inner_bits):
         count = sends[bit]
         others = range(1, 1 << bit)
@@ -394,23 +394,19 @@
         late_counts += [prefix_counts(bit, 0, count)] * len(others) + [np.ones(n_far, np.int64)]
     for d in late:
         fars[d] = (across(far, "inner", d), 0)
-        late_sets.append(fars[d][0])
-        late_counts.append(np.ones(n_far, np.int64))
-    pieces = [first_rows(held[d], last) for d in known]
-    moved = join_after(pieces, own_done)
-    early_core = across(moved, "outer", 1)
-
-    early_sets = [held[d][0] for d in known[1:]] + [early_core, far]
-    early_counts = [prefix_counts(0, 0, sends[1])]
+    late_sets += [fars[d][0] for d in [0, 1] + late]
+    late_counts.append(np.ones(n_far * (2 + len(late)), np.int64))
+
+    early_sets = [held[1][0], near_b] + [held[d][0] for d in known[2:]]
+    early_counts = [prefix_counts(0, 0, sends[0])]
     early_counts += [prefix_counts(bit, 0, sends[bit]) for bit in range(1, inner_bits)]
-    early_counts.append(np.ones(early_core.shape[0] + n_far, np.int64))
     state = attend(query_rows, early_sets, np.concatenate(early_counts), states=own_states)
 
-    pieces = [first_rows(held[d], last) for d in late]
+    pieces = [first_rows(held[d], last) for d in range(n_inner)]
     pieces += [first_rows(fars[d], n_far) for d in range(n_inner)]
-    late_core = across(join_after(pieces, state[1]), "outer", 1)
+    core = across(join_after(pieces, state[1]), "outer", 1)
     state = attend(query_rows, late_sets, np.concatenate(late_counts), states=[state])
-    result = attend(query_rows, [late_core], states=[state], out_weight=out_weight)
+    result = attend(query_rows, [core], states=[state], out_weight=out_weight)
     return result[None]
 
 

time: 44.6 us -> 41.7 us (0.935)
  Pallas kernels: 22.8 us -> 20.1 us
  local copies, waits for them, and re-layouts: 1.95 us -> 1.16 us
  starting transfers between devices: 12.4 us -> 12.9 us
    pallas_call x5, Pallas kernels: 19.5 us -> 16.9 us  [attend(): pl.pallas_call(kernel, out_shape=out_shape, grid=(1,) if part[1] > 1 else...]
    unnamed x14, local copies, waits for them, and re-layouts: 1.95 us -> 1.16 us
    ppermute x9, starting transfers between devices: 12.4 us -> 12.9 us  [across(): lax.ppermute(block, axis, [(i, i ^ flip) for i in range(lax.axis_size(axi...]
  transfers between devices with their start and end apart: 9 -> 9, of which waited for: 2 -> 3; matrix products, arithmetic and copies ran while one was open for 0% -> 0% of each run, Pallas kernels for 32% -> 28%
where the time goes in v2:
time: 41.7 us; the launch traced here: 41.6 us
  Pallas kernels  20.1 us (48%)
  starting transfers between devices  12.9 us (31%)
  waiting for transfers between devices  7.23 us (17%)
  local copies, waits for them, and re-layouts  1.16 us (3%)
    pallas_call x5, Pallas kernels, attend(): pl.pallas_call(kernel, out_shape=out_shape, grid=(1,) if part[1] > 1 else...  16.9 us
    ppermute x9, starting transfers between devices, across(): lax.ppermute(block, axis, [(i, i ^ flip) for i in range(lax.axis_size(axi...  12.9 us
    ppermute x9, waiting for transfers between devices, across(): lax.ppermute(block, axis, [(i, i ^ flip) for i in range(lax.axis_size(axi...  7.23 us
    pallas_call x1, Pallas kernels, order_rows(): pl.pallas_call(kernel, out_shape=[jax.ShapeDtypeStruct((high - low, 2 * w...  3.08 us
    unnamed x14, local copies, waits for them, and re-layouts  1.16 us
  transfers between devices with their start and end apart: 9, of which 3 were waited for; matrix products, arithmetic and copies ran while one was open for 0% of the time, Pallas kernels for 28%

profile of v2, /device:TPU:0, one launch (start us, length us, event | category | flops | bytes accessed | tf_op | source)
XLA Modules:
  0.0 41.6 jit_solution(17640146387666816769)
XLA Ops:
  0.0 3.1 %shard_map.55 = (bf16[128,1536]{1,0:T(8,128)(2,1)}, bf16[128,1536]{1,0:T(8,128)(2,1)}, bf16[8,1536]{1,0:T(8,128)(2,1)}) custom-call(bf16[256,512]{1,0:T(8,128)(2,1)} %constant.2.clone.select_hbm, bf16[512,768]{1,0:T(8,128)(2,1)} %bitcast.4, bf16[512,768]{1,0:T(8,128)(2,1)} %bitcast.7), custom_call_target="tpu_custom_call" | custom-call | flops 402653184 | bytes 2359296 | tf_op jit(solution)/shard_map/pallas_call | solution.py:85
  3.1 3.0 %collective-permute-start = (bf16[128,1536]{1,0:T(8,128)(2,1)}, bf16[128,1536]{1,0:T(8,128)(2,1)S(1)}, u32[]{:S(2)}, u32[]{:S(2)}) collective-permute-start(bf16[128,1536]{1,0:T(8,128)(2,1)} %get-tuple-element.20.refs_0_), channel_id=1, source_target_pairs={{0,8},{8,0},{16,24},{24,16},{1,9},{9,1},{17,25},{25,17},{2,10},{10... | collective-permute-start | bytes 1179656 | tf_op jit(solution)/shard_map/ppermute | solution.py:25
  6.1 1.5 %collective-permute-start.1 = (bf16[128,1536]{1,0:T(8,128)(2,1)}, bf16[128,1536]{1,0:T(8,128)(2,1)S(1)}, u32[]{:S(2)}, u32[]{:S(2)}) collective-permute-start(bf16[128,1536]{1,0:T(8,128)(2,1)} %get-tuple-element.20.refs_0_), channel_id=1, source_target_pairs={{0,16},{8,24},{16,0},{24,8},{1,17},{9,25},{17,1},{25,9},{2,18},{10... | collective-permute-start | bytes 1179656 | tf_op jit(solution)/shard_map/ppermute | solution.py:25
  7.6 1.6 %collective-permute-start.2 = (bf16[8,1536]{1,0:T(8,128)(2,1)}, bf16[8,1536]{1,0:T(8,128)(2,1)S(1)}, u32[]{:S(2)}, u32[]{:S(2)}) collective-permute-start(bf16[8,1536]{1,0:T(8,128)(2,1)} %get-tuple-element.21.refs_0_), channel_id=1, source_target_pairs={{0,2},{1,3},{2,0},{3,1},{4,6},{5,7},{6,4},{7,5},{8,10},{9,11},{10,... | collective-permute-start | bytes 73736 | tf_op jit(solution)/shard_map/ppermute | solution.py:25
  9.2 0.5 %collective-permute-start.7 = (bf16[128,1536]{1,0:T(8,128)(2,1)}, bf16[128,1536]{1,0:T(8,128)(2,1)S(1)}, u32[]{:S(2)}, u32[]{:S(2)}) collective-permute-start(bf16[128,1536]{1,0:T(8,128)(2,1)} %get-tuple-element.24), channel_id=1, source_target_pairs={{0,8},{8,0},{16,24},{24,16},{1,9},{9,1},{17,25},{25,17},{2,10},{10... | collective-permute-start | bytes 1179656 | tf_op jit(solution)/shard_map/ppermute | solution.py:25
  9.7 1.1 %copy-done.5 = bf16[1,512,768]{2,1,0:T(8,128)(2,1)S(1)} copy-done((bf16[1,512,768]{2,1,0:T(8,128)(2,1)S(1)}, bf16[1,512,768]{2,1,0:T(8,128)(2,1)}, u32[]{:S(2)}) %copy-start.5) | copy-done | bytes 786456
  10.9 3.0 %shard_map.56 = (f32[384,512]{1,0:T(8,128)S(1)}, f32[6,512]{1,0:T(8,128)S(1)}, f32[6,512]{1,0:T(8,128)S(1)}) custom-call(bf16[512,768]{1,0:T(8,128)(2,1)S(1)} %bitcast.10, bf16[512,768]{1,0:T(8,128)(2,1)S(1)} %bitcast.5, bf16[512,768]{1,0:T(8,128)(2,1)S(1)} %bitcast.8), custom_call_target="tpu_custom_call" | custom-call | flops 1610612736 | bytes 1572864 | tf_op jit(solution)/shard_map/pallas_call | solution.py:306
  13.8 0.0 collective-permute-done.2.refs_1_
  13.9 2.7 %collective-permute-start.3 = (bf16[16,1536]{1,0:T(8,128)(2,1)S(1)}, bf16[16,1536]{1,0:T(8,128)(2,1)S(1)}, u32[]{:S(2)}, u32[]{:S(2)}) collective-permute-start(bf16[16,1536]{1,0:T(8,128)(2,1)S(1)} %shard_map.57.refs_3_.refs_0_), channel_id=1, source_target_pairs={{0,4},{1,5},{2,6},{3,7},{4,0},{5,1},{6,2},{7,3},{8,12},{9,13},{10,... | collective-permute-start | bytes 147464 | tf_op jit(solution)/shard_map/ppermute | solution.py:25
  16.5 3.0 %shard_map.58 = (f32[384,512]{1,0:T(8,128)S(1)}, f32[6,512]{1,0:T(8,128)S(1)}, f32[6,512]{1,0:T(8,128)S(1)}) custom-call(bf16[512,768]{1,0:T(8,128)(2,1)S(1)} %bitcast.11, bf16[512,768]{1,0:T(8,128)(2,1)S(1)} %bitcast.6, bf16[512,768]{1,0:T(8,128)(2,1)S(1)} %bitcast.9, bf16[16,1536]{1,0:T(8,128)(2,1)S(1)} %shard_map.57.refs_3_.refs_0_), custom_call_target="tpu_custom_call" | custom-call | flops 1610612736 | bytes 1572864 | tf_op jit(solution)/shard_map/pallas_call | solution.py:306
  19.5 0.0 copy-start.6
  19.6 0.0 collective-permute-done.refs_0_.refs_1_
  19.6 0.6 %collective-permute-start.4 = (bf16[160,1536]{1,0:T(8,128)(2,1)S(1)}, bf16[160,1536]{1,0:T(8,128)(2,1)S(1)}, u32[]{:S(2)}, u32[]{:S(2)}) collective-permute-start(bf16[160,1536]{1,0:T(8,128)(2,1)S(1)} %shard_map.60), channel_id=1, source_target_pairs={{0,16},{8,24},{16,0},{24,8},{1,17},{9,25},{17,1},{25,9},{2,18},{10... | collective-permute-start | bytes 1474568 | tf_op jit(solution)/shard_map/ppermute | solution.py:25
  20.2 2.4 %collective-permute-start.6 = (bf16[32,1536]{1,0:T(8,128)(2,1)S(1)}, bf16[32,1536]{1,0:T(8,128)(2,1)S(1)}, u32[]{:S(2)}, u32[]{:S(2)}) collective-permute-start(bf16[32,1536]{1,0:T(8,128)(2,1)S(1)} %shard_map.59.refs_1_.refs_2_.refs_4_), channel_id=1, source_target_pairs={{0,24},{8,16},{16,8},{24,0},{1,25},{9,17},{17,9},{25,1},{2,26},{10... | collective-permute-start | bytes 294920 | tf_op jit(solution)/shard_map/ppermute | solution.py:25
  22.6 0.5 %collective-permute-start.5 = (bf16[32,1536]{1,0:T(8,128)(2,1)S(1)}, bf16[32,1536]{1,0:T(8,128)(2,1)S(1)}, u32[]{:S(2)}, u32[]{:S(2)}) collective-permute-start(bf16[32,1536]{1,0:T(8,128)(2,1)S(1)} %shard_map.59.refs_1_.refs_2_.refs_4_), channel_id=1, source_target_pairs={{0,8},{8,0},{16,24},{24,16},{1,9},{9,1},{17,25},{25,17},{2,10},{10... | collective-permute-start | bytes 294920 | tf_op jit(solution)/shard_map/ppermute | solution.py:25
  23.2 1.5 %collective-permute-done.7.refs_2_ = bf16[128,1536]{1,0:T(8,128)(2,1)S(1)} collective-permute-done((bf16[128,1536]{1,0:T(8,128)(2,1)}, bf16[128,1536]{1,0:T(8,128)(2,1)S(1)}, u32[]{:S(2)}, u32[]{:S(2)}) %collective-permute-start.7) | collective-permute-done | bytes 393248 | tf_op jit(solution)/shard_map/ppermute | solution.py:25
  24.7 2.9 %shard_map.61 = (f32[768,512]{1,0:T(8,128)S(1)}, f32[12,512]{1,0:T(8,128)S(1)}, f32[12,512]{1,0:T(8,128)S(1)}) custom-call(bf16[512,768]{1,0:T(8,128)(2,1)S(1)} %bitcast.12, bf16[128,1536]{1,0:T(8,128)(2,1)S(1)} %collective-permute-done.refs_0_.refs_1_, bf16[128,1536]{1,0:T(8,128)(2,1)S(1)} %collective-permute-done.7.refs_2_, ...), custom_call_target="tpu_custom_call" | custom-call | flops 2415919104 | bytes 2752512 | tf_op jit(solution)/shard_map/pallas_call | solution.py:306
  27.6 0.7 %collective-permute-done.6.refs_7_.refs_4_ = bf16[32,1536]{1,0:T(8,128)(2,1)S(1)} collective-permute-done((bf16[32,1536]{1,0:T(8,128)(2,1)S(1)}, bf16[32,1536]{1,0:T(8,128)(2,1)S(1)}, u32[]{:S(2)}, u32[]{:S(2)}) %collective-permute-start.6) | collective-permute-done | bytes 98336 | tf_op jit(solution)/shard_map/ppermute | solution.py:25
  28.3 5.0 %collective-permute-done.4.refs_3_.refs_6_.refs_1_ = bf16[160,1536]{1,0:T(8,128)(2,1)S(1)} collective-permute-done((bf16[160,1536]{1,0:T(8,128)(2,1)S(1)}, bf16[160,1536]{1,0:T(8,128)(2,1)S(1)}, u32[]{:S(2)}, u32[]{:S(2)}) %collective-permute-start.4) | collective-permute-done | bytes 491552 | tf_op jit(solution)/shard_map/ppermute | solution.py:25
  33.3 0.1 shard_map.62
  33.4 0.1 collective-permute-start.8
  33.5 0.0 copy-start.4
  33.5 2.9 %shard_map.63 = (f32[768,512]{1,0:T(8,128)S(1)}, f32[12,512]{1,0:T(8,128)S(1)}, f32[12,512]{1,0:T(8,128)S(1)}) custom-call(bf16[512,768]{1,0:T(8,128)(2,1)S(1)} %bitcast.13, bf16[160,1536]{1,0:T(8,128)(2,1)S(1)} %collective-permute-done.4.refs_3_.refs_6_.refs_1_, bf16[32,1536]{1,0:T(8,128)(2,1)S(1)} %shard_map.59.refs_1_.refs_2_.refs_4_, ...), custom_call_target="tpu_custom_call" | custom-call | flops 1610612736 | bytes 2359296 | tf_op jit(solution)/shard_map/pallas_call | solution.py:306
  36.4 5.1 %shard_map.64 = bf16[512,768]{1,0:T(8,128)(2,1)} custom-call(bf16[512,768]{1,0:T(8,128)(2,1)S(1)} %bitcast.14, bf16[384,1536]{1,0:T(8,128)(2,1)S(1)} %collective-permute-done.8.refs_1_, f32[768,512]{1,0:T(8,128)S(1)} %get-tuple-element.32.refs_2_, f32[12,512]{1,0:T(8,128)S(1)} %get-tuple-element.33.refs_3_, f32[12,512]{1,0:T(8,128)S(1)} %get-tuple-element.34.refs_4_, ...), custom_call_target="tpu_custom_call" | custom-call | flops 2415919104 | bytes 2752512 | tf_op jit(solution)/shard_map/pallas_call | solution.py:306
  (18 shorter events, 0.1 us)
Async XLA Ops:
  0.0 9.7 %copy-start.1 = (bf16[1,512,768]{2,1,0:T(8,128)(2,1)S(1)}, bf16[1,512,768]{2,1,0:T(8,128)(2,1)}, u32[]{:S(2)}) copy-start(bf16[1,512,768]{2,1,0:T(8,128)(2,1)} %param.7) | copy-start | bytes 2359300
  0.0 9.7 %copy-start = (bf16[1,512,768]{2,1,0:T(8,128)(2,1)S(1)}, bf16[1,512,768]{2,1,0:T(8,128)(2,1)}, u32[]{:S(2)}) copy-start(bf16[1,512,768]{2,1,0:T(8,128)(2,1)} %param.6) | copy-start | bytes 2359300
  3.1 16.5 %collective-permute-start = (bf16[128,1536]{1,0:T(8,128)(2,1)}, bf16[128,1536]{1,0:T(8,128)(2,1)S(1)}, u32[]{:S(2)}, u32[]{:S(2)}) collective-permute-start(bf16[128,1536]{1,0:T(8,128)(2,1)} %get-tuple-element.20.refs_0_), channel_id=1, source_target_pairs={{0,8},{8,0},{16,24},{24,16},{1,9},{9,1},{17,25},{25,17},{2,10},{10... | collective-permute-start | bytes 1179656 | tf_op jit(solution)/shard_map/ppermute | solution.py:25
  6.1 18.6 %collective-permute-start.1 = (bf16[128,1536]{1,0:T(8,128)(2,1)}, bf16[128,1536]{1,0:T(8,128)(2,1)S(1)}, u32[]{:S(2)}, u32[]{:S(2)}) collective-permute-start(bf16[128,1536]{1,0:T(8,128)(2,1)} %get-tuple-element.20.refs_0_), channel_id=1, source_target_pairs={{0,16},{8,24},{16,0},{24,8},{1,17},{9,25},{17,1},{25,9},{2,18},{10... | collective-permute-start | bytes 1179656 | tf_op jit(solution)/shard_map/ppermute | solution.py:25
  7.6 6.2 %collective-permute-start.2 = (bf16[8,1536]{1,0:T(8,128)(2,1)}, bf16[8,1536]{1,0:T(8,128)(2,1)S(1)}, u32[]{:S(2)}, u32[]{:S(2)}) collective-permute-start(bf16[8,1536]{1,0:T(8,128)(2,1)} %get-tuple-element.21.refs_0_), channel_id=1, source_target_pairs={{0,2},{1,3},{2,0},{3,1},{4,6},{5,7},{6,4},{7,5},{8,10},{9,11},{10,... | collective-permute-start | bytes 73736 | tf_op jit(solution)/shard_map/ppermute | solution.py:25
  9.2 15.5 %collective-permute-start.7 = (bf16[128,1536]{1,0:T(8,128)(2,1)}, bf16[128,1536]{1,0:T(8,128)(2,1)S(1)}, u32[]{:S(2)}, u32[]{:S(2)}) collective-permute-start(bf16[128,1536]{1,0:T(8,128)(2,1)} %get-tuple-element.24), channel_id=1, source_target_pairs={{0,8},{8,0},{16,24},{24,16},{1,9},{9,1},{17,25},{25,17},{2,10},{10... | collective-permute-start | bytes 1179656 | tf_op jit(solution)/shard_map/ppermute | solution.py:25
  9.7 1.1 %copy-start.5 = (bf16[1,512,768]{2,1,0:T(8,128)(2,1)S(1)}, bf16[1,512,768]{2,1,0:T(8,128)(2,1)}, u32[]{:S(2)}) copy-start(bf16[1,512,768]{2,1,0:T(8,128)(2,1)} %param.5) | copy-start | bytes 2359300
  10.9 3.0 %copy-start.3 = (bf16[8,1536]{1,0:T(8,128)(2,1)S(1)}, bf16[8,1536]{1,0:T(8,128)(2,1)}, u32[]{:S(2)}) copy-start(bf16[8,1536]{1,0:T(8,128)(2,1)} %get-tuple-element.21.refs_0_) | copy-start | bytes 73732
  13.9 5.7 %collective-permute-start.3 = (bf16[16,1536]{1,0:T(8,128)(2,1)S(1)}, bf16[16,1536]{1,0:T(8,128)(2,1)S(1)}, u32[]{:S(2)}, u32[]{:S(2)}) collective-permute-start(bf16[16,1536]{1,0:T(8,128)(2,1)S(1)} %shard_map.57.refs_3_.refs_0_), channel_id=1, source_target_pairs={{0,4},{1,5},{2,6},{3,7},{4,0},{5,1},{6,2},{7,3},{8,12},{9,13},{10,... | collective-permute-start | bytes 147464 | tf_op jit(solution)/shard_map/ppermute | solution.py:25
  19.5 5.2 %copy-start.6 = (bf16[1,512,768]{2,1,0:T(8,128)(2,1)S(1)}, bf16[1,512,768]{2,1,0:T(8,128)(2,1)}, u32[]{:S(2)}) copy-start(bf16[1,512,768]{2,1,0:T(8,128)(2,1)} %param.5) | copy-start | bytes 2359300
  19.6 13.7 %collective-permute-start.4 = (bf16[160,1536]{1,0:T(8,128)(2,1)S(1)}, bf16[160,1536]{1,0:T(8,128)(2,1)S(1)}, u32[]{:S(2)}, u32[]{:S(2)}) collective-permute-start(bf16[160,1536]{1,0:T(8,128)(2,1)S(1)} %shard_map.60), channel_id=1, source_target_pairs={{0,16},{8,24},{16,0},{24,8},{1,17},{9,25},{17,1},{25,9},{2,18},{10... | collective-permute-start | bytes 1474568 | tf_op jit(solution)/shard_map/ppermute | solution.py:25
  20.2 8.1 %collective-permute-start.6 = (bf16[32,1536]{1,0:T(8,128)(2,1)S(1)}, bf16[32,1536]{1,0:T(8,128)(2,1)S(1)}, u32[]{:S(2)}, u32[]{:S(2)}) collective-permute-start(bf16[32,1536]{1,0:T(8,128)(2,1)S(1)} %shard_map.59.refs_1_.refs_2_.refs_4_), channel_id=1, source_target_pairs={{0,24},{8,16},{16,8},{24,0},{1,25},{9,17},{17,9},{25,1},{2,26},{10... | collective-permute-start | bytes 294920 | tf_op jit(solution)/shard_map/ppermute | solution.py:25
  22.6 5.7 %collective-permute-start.5 = (bf16[32,1536]{1,0:T(8,128)(2,1)S(1)}, bf16[32,1536]{1,0:T(8,128)(2,1)S(1)}, u32[]{:S(2)}, u32[]{:S(2)}) collective-permute-start(bf16[32,1536]{1,0:T(8,128)(2,1)S(1)} %shard_map.59.refs_1_.refs_2_.refs_4_), channel_id=1, source_target_pairs={{0,8},{8,0},{16,24},{24,16},{1,9},{9,1},{17,25},{25,17},{2,10},{10... | collective-permute-start | bytes 294920 | tf_op jit(solution)/shard_map/ppermute | solution.py:25
  24.7 8.7 %copy-start.2 = (bf16[128,1536]{1,0:T(8,128)(2,1)S(1)}, bf16[128,1536]{1,0:T(8,128)(2,1)}, u32[]{:S(2)}) copy-start(bf16[128,1536]{1,0:T(8,128)(2,1)} %get-tuple-element.20.refs_0_) | copy-start | bytes 1179652
  33.4 3.0 %collective-permute-start.8 = (bf16[384,1536]{1,0:T(8,128)(2,1)S(1)}, bf16[384,1536]{1,0:T(8,128)(2,1)S(1)}, u32[]{:S(2)}, u32[]{:S(2)}) collective-permute-start(bf16[384,1536]{1,0:T(8,128)(2,1)S(1)} %shard_map.62), channel_id=1, source_target_pairs={{0,1},{1,0},{2,3},{3,2},{4,5},{5,4},{6,7},{7,6},{8,9},{9,8},{10,11... | collective-permute-start | bytes 3538952 | tf_op jit(solution)/shard_map/ppermute | solution.py:25
  33.5 2.9 %copy-start.4 = (bf16[768,768]{1,0:T(8,128)(2,1)S(1)}, bf16[768,768]{1,0:T(8,128)(2,1)}, u32[]{:S(2)}) copy-start(bf16[768,768]{1,0:T(8,128)(2,1)} %refs_5_.1) | copy-start | bytes 3538948

commit v3 on v2

--- a/solution.py
+++ b/solution.py
@@ -18,7 +18,7 @@
 LOG2E = math.log2(math.e)
 VMEM_BYTES = 16 * 1024 * 1024
 JOIN_VMEM_BYTES = 8 * 1024 * 1024
-FETCH_VMEM_BYTES = 60 * 1024 * 1024
+FETCH_VMEM_BYTES = 56 * 1024 * 1024
 
 
 def across(block, axis, flip):
@@ -65,7 +65,10 @@
     tokens, width = key_rows.shape
 
     def kernel(select_hbm, key_hbm, value_hbm, *refs):
-        out_refs, (select_ref, row_ref, sems) = refs[: len(prefixes)], refs[len(prefixes) :]
+        out_refs, (select_ref, row_ref, moved_ref, sems) = (
+            refs[: len(prefixes)],
+            refs[len(prefixes) :],
+        )
         copies = [
             pltpu.make_async_copy(select_hbm, select_ref, sems.at[0]),
             pltpu.make_async_copy(key_hbm, row_ref.at[0], sems.at[1]),
@@ -74,13 +77,24 @@
         for copy in copies:
             copy.start()
         copies[0].wait()
+        stores = []
         for half in range(2):
             copies[1 + half].wait()
-            moved = jnp.dot(
+            moved_ref[half] = jnp.dot(
                 select_ref[...], row_ref[half], preferred_element_type=jnp.float32
             ).astype(jnp.bfloat16)
-            for (low, high), out_ref in zip(prefixes, out_refs):
-                out_ref[:, half * width : (half + 1) * width] = moved[low:high]
+            cols = slice(half * width, (half + 1) * width)
+            for (low, high), out_ref in zip(prefixes[:-1], out_refs):
+                stores.append(
+                    pltpu.make_async_copy(
+                        moved_ref.at[half, low:high], out_ref.at[:, cols], sems.at[3 + len(stores)]
+                    )
+                )
+                stores[-1].start()
+            low, high = prefixes[-1]
+            out_refs[-1][:, cols] = moved_ref[half, low : 2 * high, :][: high - low]
+        for store in stores:
+            store.wait()
 
     return pl.pallas_call(
         kernel,
@@ -88,10 +102,13 @@
             jax.ShapeDtypeStruct((high - low, 2 * width), jnp.bfloat16) for low, high in prefixes
         ],
         in_specs=[pl.BlockSpec(memory_space=pltpu.HBM)] * 3,
+        out_specs=[pl.BlockSpec(memory_space=pl.ANY)] * (len(prefixes) - 1)
+        + [pl.BlockSpec(memory_space=pltpu.VMEM)],
         scratch_shapes=[
             pltpu.VMEM(select.shape, jnp.bfloat16),
             pltpu.VMEM((2, tokens, width), jnp.bfloat16),
-            pltpu.SemaphoreType.DMA((3,)),
+            pltpu.VMEM((2, select.shape[0], width), jnp.bfloat16),
+            pltpu.SemaphoreType.DMA((3 + 2 * (len(prefixes) - 1),)),
         ],
         compiler_params=pltpu.CompilerParams(vmem_limit_bytes=FETCH_VMEM_BYTES),
         cost_estimate=pl.CostEstimate(
@@ -102,7 +119,9 @@
 
 def attend(queries, sets, counts=None, row_strides=None, part=(0, 1), states=(), out_weight=None, wait=None):
     tokens = queries.shape[0]
-    width = queries.shape[1] // part[1]
+    full = queries.shape[1]
+    width = full // part[1]
+    base = part[0] * width
     heads, pairs = width // HEAD_DIM, width // PAIR
     joined = [not isinstance(block, tuple) for block in sets]
     sizes = [(block if whole else block[0]).shape[0] for block, whole in zip(sets, joined)]
@@ -119,12 +138,13 @@
         set_refs = []
         for whole in joined:
             ref = refs.pop(0)
-            set_refs.append((ref, 0, ref, width) if whole else (ref, 0, refs.pop(0), 0))
+            set_refs.append((ref, ref, full) if whole else (ref, refs.pop(0), 0))
         state_refs = [[refs.pop(0) for _ in range(3)] for _ in states]
         if wait is not None:
             refs.pop(1 if final else 0)
         if final:
-            weight_ref, out_ref, attended_ref = refs.pop(0), refs.pop(0), refs.pop(-1)
+            weight_ref, out_hbm = refs.pop(0), refs.pop(0)
+            attended_ref, out_ref, result_ref, sems = refs[-4:]
         else:
             numer_out, peak_out, total_out = [refs.pop(0) for _ in range(3)]
         score_ref, value_ref, key_ref, turned_ref = [refs.pop(0) for _ in range(4)]
@@ -144,6 +164,9 @@
         def column(pair):
             return pl.multiple_of(pair * PAIR, PAIR)
 
+        def columns(pair, shift=0):
+            return pl.ds(pl.multiple_of(base + shift + pair * PAIR, PAIR), PAIR)
+
         def head_queries(half):
             turned = turned_ref[...]
             row = lax.broadcasted_iota(jnp.int32, turned.shape, 0)
@@ -151,10 +174,10 @@
             return jnp.where(own, turned, jnp.zeros_like(turned))
 
         def load(pair):
-            turned_ref[...] = query_ref[:, pl.ds(column(pair), PAIR)].T
+            turned_ref[...] = query_ref[:, columns(pair)].T
             at = 0
-            for (ref, _, _, _), size in zip(set_refs, sizes):
-                key_ref[at : at + size, :] = ref[:, pl.ds(column(pair), PAIR)]
+            for (ref, _, _), size in zip(set_refs, sizes):
+                key_ref[at : at + size, :] = ref[:, columns(pair)]
                 at += size
 
         def score(half, query_head, chunk, running):
@@ -241,8 +264,8 @@
 
             def pair_step(pair, running):
                 at = 0
-                for (_, _, ref, shift), size in zip(set_refs, sizes):
-                    value_ref[at : at + size, :] = ref[:, pl.ds(column(pair) + shift, PAIR)]
+                for (_, ref, shift), size in zip(set_refs, sizes):
+                    value_ref[at : at + size, :] = ref[:, columns(pair, shift)]
                     at += size
                 if padded > keys:
                     value_ref[keys:, :] = jnp.zeros((padded - keys, PAIR), jnp.bfloat16)
@@ -265,9 +288,18 @@
                 state_refs[group] if states else None,
             )
         if final:
-            out_ref[...] = jnp.dot(
-                out_ref[...], weight_ref[...], preferred_element_type=jnp.float32
-            ).astype(jnp.bfloat16)
+            copies = []
+            for at, low in enumerate(range(0, tokens, LANES)):
+                rows = slice(low, low + LANES)
+                result_ref[rows, :] = jnp.dot(
+                    out_ref[rows, :], weight_ref[...], preferred_element_type=jnp.float32
+                ).astype(jnp.bfloat16)
+                copies.append(
+                    pltpu.make_async_copy(result_ref.at[rows], out_hbm.at[rows], sems.at[at])
+                )
+                copies[-1].start()
+            for copy in copies:
+                copy.wait()
 
     if final:
         out_shape = jax.ShapeDtypeStruct((tokens, width), jnp.bfloat16)
@@ -287,16 +319,13 @@
         scratch.append(pltpu.VMEM((keys, LANES), jnp.float32))
     if final:
         scratch.append(pltpu.VMEM((2, HEAD_DIM, tokens), jnp.bfloat16))
+        scratch += [pltpu.VMEM((tokens, width), jnp.bfloat16)] * 2
+        scratch.append(pltpu.SemaphoreType.DMA((tokens // LANES,)))
     operands = [queries]
     for block, whole in zip(sets, joined):
         operands += [block] if whole else list(block)
     whole_spec = pl.BlockSpec(memory_space=pltpu.VMEM)
     specs = [whole_spec] * len(operands)
-    if part[1] > 1:
-        specs = [
-            pl.BlockSpec((array.shape[0], array.shape[1] // part[1]), lambda step: (0, part[0]))
-            for array in operands
-        ]
     for array in [array for state in states for array in state] + ([out_weight] if final else []):
         operands.append(array)
         specs.append(whole_spec)
@@ -306,8 +335,8 @@
     return pl.pallas_call(
         kernel,
         out_shape=out_shape,
-        grid=(1,) if part[1] > 1 else (),
         in_specs=specs,
+        **({"out_specs": pl.BlockSpec(memory_space=pl.ANY)} if final else {}),
         scratch_shapes=scratch,
         compiler_params=pltpu.CompilerParams(
             vmem_limit_bytes=VMEM_BYTES

time: 41.7 us -> 42.2 us (1.012)
    pallas_call x1, Pallas kernels: 3.08 us -> 3.62 us  [order_rows(): pl.pallas_call(kernel, out_shape=[jax.ShapeDtypeStruct((high - low, 2 * w...]
where the time goes in v3:
time: 42.2 us; the launch traced here: 42 us
  Pallas kernels  20.4 us (48%)
  starting transfers between devices  12.9 us (31%)
  waiting for transfers between devices  7.23 us (17%)
  local copies, waits for them, and re-layouts  1.16 us (3%)
    pallas_call x5, Pallas kernels, attend(): pl.pallas_call(kernel, out_shape=out_shape, in_specs=specs, **{'out_specs...  16.7 us
    ppermute x9, starting transfers between devices, across(): lax.ppermute(block, axis, [(i, i ^ flip) for i in range(lax.axis_size(axi...  12.9 us
    ppermute x9, waiting for transfers between devices, across(): lax.ppermute(block, axis, [(i, i ^ flip) for i in range(lax.axis_size(axi...  7.23 us
    pallas_call x1, Pallas kernels, order_rows(): pl.pallas_call(kernel, out_shape=[jax.ShapeDtypeStruct((high - low, 2 * w...  3.62 us
    unnamed x14, local copies, waits for them, and re-layouts  1.16 us
  transfers between devices with their start and end apart: 9, of which 3 were waited for; matrix products, arithmetic and copies ran while one was open for 0% of the time, Pallas kernels for 28%

profile of v3, /device:TPU:0, one launch (start us, length us, event | category | flops | bytes accessed | tf_op | source)
XLA Modules:
  0.0 42.0 jit_solution(12405344682643377417)
XLA Ops:
  0.0 3.6 %shard_map.55 = (bf16[128,1536]{1,0:T(8,128)(2,1)}, bf16[128,1536]{1,0:T(8,128)(2,1)}, bf16[8,1536]{1,0:T(8,128)(2,1)}) custom-call(bf16[256,512]{1,0:T(8,128)(2,1)} %constant.2.clone.select_hbm, bf16[512,768]{1,0:T(8,128)(2,1)} %bitcast.4, bf16[512,768]{1,0:T(8,128)(2,1)} %bitcast.7), custom_call_target="tpu_custom_call" | custom-call | flops 402653184 | bytes 2359296 | tf_op jit(solution)/shard_map/pallas_call | solution.py:99
  3.6 3.0 %collective-permute-start = (bf16[128,1536]{1,0:T(8,128)(2,1)}, bf16[128,1536]{1,0:T(8,128)(2,1)S(1)}, u32[]{:S(2)}, u32[]{:S(2)}) collective-permute-start(bf16[128,1536]{1,0:T(8,128)(2,1)} %get-tuple-element.20.refs_0_), channel_id=1, source_target_pairs={{0,8},{8,0},{16,24},{24,16},{1,9},{9,1},{17,25},{25,17},{2,10},{10... | collective-permute-start | bytes 1179656 | tf_op jit(solution)/shard_map/ppermute | solution.py:25
  6.6 1.5 %collective-permute-start.1 = (bf16[128,1536]{1,0:T(8,128)(2,1)}, bf16[128,1536]{1,0:T(8,128)(2,1)S(1)}, u32[]{:S(2)}, u32[]{:S(2)}) collective-permute-start(bf16[128,1536]{1,0:T(8,128)(2,1)} %get-tuple-element.20.refs_0_), channel_id=1, source_target_pairs={{0,16},{8,24},{16,0},{24,8},{1,17},{9,25},{17,1},{25,9},{2,18},{10... | collective-permute-start | bytes 1179656 | tf_op jit(solution)/shard_map/ppermute | solution.py:25
  8.2 1.6 %collective-permute-start.2 = (bf16[8,1536]{1,0:T(8,128)(2,1)}, bf16[8,1536]{1,0:T(8,128)(2,1)S(1)}, u32[]{:S(2)}, u32[]{:S(2)}) collective-permute-start(bf16[8,1536]{1,0:T(8,128)(2,1)} %get-tuple-element.21.refs_0_), channel_id=1, source_target_pairs={{0,2},{1,3},{2,0},{3,1},{4,6},{5,7},{6,4},{7,5},{8,10},{9,11},{10,... | collective-permute-start | bytes 73736 | tf_op jit(solution)/shard_map/ppermute | solution.py:25
  9.7 0.5 %collective-permute-start.7 = (bf16[128,1536]{1,0:T(8,128)(2,1)}, bf16[128,1536]{1,0:T(8,128)(2,1)S(1)}, u32[]{:S(2)}, u32[]{:S(2)}) collective-permute-start(bf16[128,1536]{1,0:T(8,128)(2,1)} %get-tuple-element.24), channel_id=1, source_target_pairs={{0,8},{8,0},{16,24},{24,16},{1,9},{9,1},{17,25},{25,17},{2,10},{10... | collective-permute-start | bytes 1179656 | tf_op jit(solution)/shard_map/ppermute | solution.py:25
  10.3 1.1 %copy-done.5 = bf16[1,512,768]{2,1,0:T(8,128)(2,1)S(1)} copy-done((bf16[1,512,768]{2,1,0:T(8,128)(2,1)S(1)}, bf16[1,512,768]{2,1,0:T(8,128)(2,1)}, u32[]{:S(2)}) %copy-start.5) | copy-done | bytes 786456
  11.4 2.9 %shard_map.56 = (f32[384,512]{1,0:T(8,128)S(1)}, f32[6,512]{1,0:T(8,128)S(1)}, f32[6,512]{1,0:T(8,128)S(1)}) custom-call(bf16[512,768]{1,0:T(8,128)(2,1)S(1)} %bitcast.10, bf16[512,768]{1,0:T(8,128)(2,1)S(1)} %bitcast.5, bf16[512,768]{1,0:T(8,128)(2,1)S(1)} %bitcast.8), custom_call_target="tpu_custom_call" | custom-call | flops 1610612736 | bytes 1572864 | tf_op jit(solution)/shard_map/pallas_call | solution.py:335
  14.3 0.0 collective-permute-done.2.refs_1_
  14.4 2.7 %collective-permute-start.3 = (bf16[16,1536]{1,0:T(8,128)(2,1)S(1)}, bf16[16,1536]{1,0:T(8,128)(2,1)S(1)}, u32[]{:S(2)}, u32[]{:S(2)}) collective-permute-start(bf16[16,1536]{1,0:T(8,128)(2,1)S(1)} %shard_map.57.refs_3_.refs_0_), channel_id=1, source_target_pairs={{0,4},{1,5},{2,6},{3,7},{4,0},{5,1},{6,2},{7,3},{8,12},{9,13},{10,... | collective-permute-start | bytes 147464 | tf_op jit(solution)/shard_map/ppermute | solution.py:25
  17.0 2.9 %shard_map.58 = (f32[384,512]{1,0:T(8,128)S(1)}, f32[6,512]{1,0:T(8,128)S(1)}, f32[6,512]{1,0:T(8,128)S(1)}) custom-call(bf16[512,768]{1,0:T(8,128)(2,1)S(1)} %bitcast.11, bf16[512,768]{1,0:T(8,128)(2,1)S(1)} %bitcast.6, bf16[512,768]{1,0:T(8,128)(2,1)S(1)} %bitcast.9, bf16[16,1536]{1,0:T(8,128)(2,1)S(1)} %shard_map.57.refs_3_.refs_0_), custom_call_target="tpu_custom_call" | custom-call | flops 1610612736 | bytes 1572864 | tf_op jit(solution)/shard_map/pallas_call | solution.py:335
  20.0 0.0 copy-start.6
  20.0 0.0 collective-permute-done.refs_0_.refs_1_
  20.0 0.6 %collective-permute-start.4 = (bf16[160,1536]{1,0:T(8,128)(2,1)S(1)}, bf16[160,1536]{1,0:T(8,128)(2,1)S(1)}, u32[]{:S(2)}, u32[]{:S(2)}) collective-permute-start(bf16[160,1536]{1,0:T(8,128)(2,1)S(1)} %shard_map.60), channel_id=1, source_target_pairs={{0,16},{8,24},{16,0},{24,8},{1,17},{9,25},{17,1},{25,9},{2,18},{10... | collective-permute-start | bytes 1474568 | tf_op jit(solution)/shard_map/ppermute | solution.py:25
  20.6 2.4 %collective-permute-start.6 = (bf16[32,1536]{1,0:T(8,128)(2,1)S(1)}, bf16[32,1536]{1,0:T(8,128)(2,1)S(1)}, u32[]{:S(2)}, u32[]{:S(2)}) collective-permute-start(bf16[32,1536]{1,0:T(8,128)(2,1)S(1)} %shard_map.59.refs_1_.refs_2_.refs_4_), channel_id=1, source_target_pairs={{0,24},{8,16},{16,8},{24,0},{1,25},{9,17},{17,9},{25,1},{2,26},{10... | collective-permute-start | bytes 294920 | tf_op jit(solution)/shard_map/ppermute | solution.py:25
  23.1 0.5 %collective-permute-start.5 = (bf16[32,1536]{1,0:T(8,128)(2,1)S(1)}, bf16[32,1536]{1,0:T(8,128)(2,1)S(1)}, u32[]{:S(2)}, u32[]{:S(2)}) collective-permute-start(bf16[32,1536]{1,0:T(8,128)(2,1)S(1)} %shard_map.59.refs_1_.refs_2_.refs_4_), channel_id=1, source_target_pairs={{0,8},{8,0},{16,24},{24,16},{1,9},{9,1},{17,25},{25,17},{2,10},{10... | collective-permute-start | bytes 294920 | tf_op jit(solution)/shard_map/ppermute | solution.py:25
  23.6 1.6 %collective-permute-done.7.refs_2_ = bf16[128,1536]{1,0:T(8,128)(2,1)S(1)} collective-permute-done((bf16[128,1536]{1,0:T(8,128)(2,1)}, bf16[128,1536]{1,0:T(8,128)(2,1)S(1)}, u32[]{:S(2)}, u32[]{:S(2)}) %collective-permute-start.7) | collective-permute-done | bytes 393248 | tf_op jit(solution)/shard_map/ppermute | solution.py:25
  25.2 2.9 %shard_map.61 = (f32[768,512]{1,0:T(8,128)S(1)}, f32[12,512]{1,0:T(8,128)S(1)}, f32[12,512]{1,0:T(8,128)S(1)}) custom-call(bf16[512,768]{1,0:T(8,128)(2,1)S(1)} %bitcast.12, bf16[128,1536]{1,0:T(8,128)(2,1)S(1)} %collective-permute-done.refs_0_.refs_1_, bf16[128,1536]{1,0:T(8,128)(2,1)S(1)} %collective-permute-done.7.refs_2_, ...), custom_call_target="tpu_custom_call" | custom-call | flops 2415919104 | bytes 2752512 | tf_op jit(solution)/shard_map/pallas_call | solution.py:335
  28.2 0.7 %collective-permute-done.6.refs_7_.refs_4_ = bf16[32,1536]{1,0:T(8,128)(2,1)S(1)} collective-permute-done((bf16[32,1536]{1,0:T(8,128)(2,1)S(1)}, bf16[32,1536]{1,0:T(8,128)(2,1)S(1)}, u32[]{:S(2)}, u32[]{:S(2)}) %collective-permute-start.6) | collective-permute-done | bytes 98336 | tf_op jit(solution)/shard_map/ppermute | solution.py:25
  28.9 4.9 %collective-permute-done.4.refs_3_.refs_6_.refs_1_ = bf16[160,1536]{1,0:T(8,128)(2,1)S(1)} collective-permute-done((bf16[160,1536]{1,0:T(8,128)(2,1)S(1)}, bf16[160,1536]{1,0:T(8,128)(2,1)S(1)}, u32[]{:S(2)}, u32[]{:S(2)}) %collective-permute-start.4) | collective-permute-done | bytes 491552 | tf_op jit(solution)/shard_map/ppermute | solution.py:25
  33.8 0.1 shard_map.62
  33.9 0.1 collective-permute-start.8
  33.9 0.0 copy-start.4
  33.9 2.9 %shard_map.63 = (f32[768,512]{1,0:T(8,128)S(1)}, f32[12,512]{1,0:T(8,128)S(1)}, f32[12,512]{1,0:T(8,128)S(1)}) custom-call(bf16[512,768]{1,0:T(8,128)(2,1)S(1)} %bitcast.13, bf16[160,1536]{1,0:T(8,128)(2,1)S(1)} %collective-permute-done.4.refs_3_.refs_6_.refs_1_, bf16[32,1536]{1,0:T(8,128)(2,1)S(1)} %shard_map.59.refs_1_.refs_2_.refs_4_, ...), custom_call_target="tpu_custom_call" | custom-call | flops 1610612736 | bytes 2359296 | tf_op jit(solution)/shard_map/pallas_call | solution.py:335
  36.9 5.0 %shard_map.64 = bf16[512,768]{1,0:T(8,128)(2,1)} custom-call(bf16[512,768]{1,0:T(8,128)(2,1)S(1)} %bitcast.14, bf16[384,1536]{1,0:T(8,128)(2,1)S(1)} %collective-permute-done.8.refs_1_, f32[768,512]{1,0:T(8,128)S(1)} %get-tuple-element.32.refs_2_, f32[12,512]{1,0:T(8,128)S(1)} %get-tuple-element.33.refs_3_, f32[12,512]{1,0:T(8,128)S(1)} %get-tuple-element.34.refs_4_, ...), custom_call_target="tpu_custom_call" | custom-call | flops 2415919104 | bytes 2752512 | tf_op jit(solution)/shard_map/pallas_call | solution.py:335
  (18 shorter events, 0.1 us)
Async XLA Ops:
  0.0 10.3 %copy-start.1 = (bf16[1,512,768]{2,1,0:T(8,128)(2,1)S(1)}, bf16[1,512,768]{2,1,0:T(8,128)(2,1)}, u32[]{:S(2)}) copy-start(bf16[1,512,768]{2,1,0:T(8,128)(2,1)} %param.7) | copy-start | bytes 2359300
  0.0 10.3 %copy-start = (bf16[1,512,768]{2,1,0:T(8,128)(2,1)S(1)}, bf16[1,512,768]{2,1,0:T(8,128)(2,1)}, u32[]{:S(2)}) copy-start(bf16[1,512,768]{2,1,0:T(8,128)(2,1)} %param.6) | copy-start | bytes 2359300
  3.6 16.4 %collective-permute-start = (bf16[128,1536]{1,0:T(8,128)(2,1)}, bf16[128,1536]{1,0:T(8,128)(2,1)S(1)}, u32[]{:S(2)}, u32[]{:S(2)}) collective-permute-start(bf16[128,1536]{1,0:T(8,128)(2,1)} %get-tuple-element.20.refs_0_), channel_id=1, source_target_pairs={{0,8},{8,0},{16,24},{24,16},{1,9},{9,1},{17,25},{25,17},{2,10},{10... | collective-permute-start | bytes 1179656 | tf_op jit(solution)/shard_map/ppermute | solution.py:25
  6.6 18.6 %collective-permute-start.1 = (bf16[128,1536]{1,0:T(8,128)(2,1)}, bf16[128,1536]{1,0:T(8,128)(2,1)S(1)}, u32[]{:S(2)}, u32[]{:S(2)}) collective-permute-start(bf16[128,1536]{1,0:T(8,128)(2,1)} %get-tuple-element.20.refs_0_), channel_id=1, source_target_pairs={{0,16},{8,24},{16,0},{24,8},{1,17},{9,25},{17,1},{25,9},{2,18},{10... | collective-permute-start | bytes 1179656 | tf_op jit(solution)/shard_map/ppermute | solution.py:25
  8.2 6.2 %collective-permute-start.2 = (bf16[8,1536]{1,0:T(8,128)(2,1)}, bf16[8,1536]{1,0:T(8,128)(2,1)S(1)}, u32[]{:S(2)}, u32[]{:S(2)}) collective-permute-start(bf16[8,1536]{1,0:T(8,128)(2,1)} %get-tuple-element.21.refs_0_), channel_id=1, source_target_pairs={{0,2},{1,3},{2,0},{3,1},{4,6},{5,7},{6,4},{7,5},{8,10},{9,11},{10,... | collective-permute-start | bytes 73736 | tf_op jit(solution)/shard_map/ppermute | solution.py:25
  9.7 15.5 %collective-permute-start.7 = (bf16[128,1536]{1,0:T(8,128)(2,1)}, bf16[128,1536]{1,0:T(8,128)(2,1)S(1)}, u32[]{:S(2)}, u32[]{:S(2)}) collective-permute-start(bf16[128,1536]{1,0:T(8,128)(2,1)} %get-tuple-element.24), channel_id=1, source_target_pairs={{0,8},{8,0},{16,24},{24,16},{1,9},{9,1},{17,25},{25,17},{2,10},{10... | collective-permute-start | bytes 1179656 | tf_op jit(solution)/shard_map/ppermute | solution.py:25
  10.3 1.1 %copy-start.5 = (bf16[1,512,768]{2,1,0:T(8,128)(2,1)S(1)}, bf16[1,512,768]{2,1,0:T(8,128)(2,1)}, u32[]{:S(2)}) copy-start(bf16[1,512,768]{2,1,0:T(8,128)(2,1)} %param.5) | copy-start | bytes 2359300
  11.4 2.9 %copy-start.3 = (bf16[8,1536]{1,0:T(8,128)(2,1)S(1)}, bf16[8,1536]{1,0:T(8,128)(2,1)}, u32[]{:S(2)}) copy-start(bf16[8,1536]{1,0:T(8,128)(2,1)} %get-tuple-element.21.refs_0_) | copy-start | bytes 73732
  14.4 5.6 %collective-permute-start.3 = (bf16[16,1536]{1,0:T(8,128)(2,1)S(1)}, bf16[16,1536]{1,0:T(8,128)(2,1)S(1)}, u32[]{:S(2)}, u32[]{:S(2)}) collective-permute-start(bf16[16,1536]{1,0:T(8,128)(2,1)S(1)} %shard_map.57.refs_3_.refs_0_), channel_id=1, source_target_pairs={{0,4},{1,5},{2,6},{3,7},{4,0},{5,1},{6,2},{7,3},{8,12},{9,13},{10,... | collective-permute-start | bytes 147464 | tf_op jit(solution)/shard_map/ppermute | solution.py:25
  20.0 5.3 %copy-start.6 = (bf16[1,512,768]{2,1,0:T(8,128)(2,1)S(1)}, bf16[1,512,768]{2,1,0:T(8,128)(2,1)}, u32[]{:S(2)}) copy-start(bf16[1,512,768]{2,1,0:T(8,128)(2,1)} %param.5) | copy-start | bytes 2359300
  20.0 13.7 %collective-permute-start.4 = (bf16[160,1536]{1,0:T(8,128)(2,1)S(1)}, bf16[160,1536]{1,0:T(8,128)(2,1)S(1)}, u32[]{:S(2)}, u32[]{:S(2)}) collective-permute-start(bf16[160,1536]{1,0:T(8,128)(2,1)S(1)} %shard_map.60), channel_id=1, source_target_pairs={{0,16},{8,24},{16,0},{24,8},{1,17},{9,25},{17,1},{25,9},{2,18},{10... | collective-permute-start | bytes 1474568 | tf_op jit(solution)/shard_map/ppermute | solution.py:25
  20.6 8.2 %collective-permute-start.6 = (bf16[32,1536]{1,0:T(8,128)(2,1)S(1)}, bf16[32,1536]{1,0:T(8,128)(2,1)S(1)}, u32[]{:S(2)}, u32[]{:S(2)}) collective-permute-start(bf16[32,1536]{1,0:T(8,128)(2,1)S(1)} %shard_map.59.refs_1_.refs_2_.refs_4_), channel_id=1, source_target_pairs={{0,24},{8,16},{16,8},{24,0},{1,25},{9,17},{17,9},{25,1},{2,26},{10... | collective-permute-start | bytes 294920 | tf_op jit(solution)/shard_map/ppermute | solution.py:25
  23.1 5.8 %collective-permute-start.5 = (bf16[32,1536]{1,0:T(8,128)(2,1)S(1)}, bf16[32,1536]{1,0:T(8,128)(2,1)S(1)}, u32[]{:S(2)}, u32[]{:S(2)}) collective-permute-start(bf16[32,1536]{1,0:T(8,128)(2,1)S(1)} %shard_map.59.refs_1_.refs_2_.refs_4_), channel_id=1, source_target_pairs={{0,8},{8,0},{16,24},{24,16},{1,9},{9,1},{17,25},{25,17},{2,10},{10... | collective-permute-start | bytes 294920 | tf_op jit(solution)/shard_map/ppermute | solution.py:25
  25.2 8.6 %copy-start.2 = (bf16[128,1536]{1,0:T(8,128)(2,1)S(1)}, bf16[128,1536]{1,0:T(8,128)(2,1)}, u32[]{:S(2)}) copy-start(bf16[128,1536]{1,0:T(8,128)(2,1)} %get-tuple-element.20.refs_0_) | copy-start | bytes 1179652
  33.9 3.0 %collective-permute-start.8 = (bf16[384,1536]{1,0:T(8,128)(2,1)S(1)}, bf16[384,1536]{1,0:T(8,128)(2,1)S(1)}, u32[]{:S(2)}, u32[]{:S(2)}) collective-permute-start(bf16[384,1536]{1,0:T(8,128)(2,1)S(1)} %shard_map.62), channel_id=1, source_target_pairs={{0,1},{1,0},{2,3},{3,2},{4,5},{5,4},{6,7},{7,6},{8,9},{9,8},{10,11... | collective-permute-start | bytes 3538952 | tf_op jit(solution)/shard_map/ppermute | solution.py:25
  33.9 2.9 %copy-start.4 = (bf16[768,768]{1,0:T(8,128)(2,1)S(1)}, bf16[768,768]{1,0:T(8,128)(2,1)}, u32[]{:S(2)}) copy-start(bf16[768,768]{1,0:T(8,128)(2,1)} %refs_5_.1) | copy-start | bytes 3538948

commit v4 on v3

--- a/solution.py
+++ b/solution.py
@@ -18,7 +18,7 @@
 LOG2E = math.log2(math.e)
 VMEM_BYTES = 16 * 1024 * 1024
 JOIN_VMEM_BYTES = 8 * 1024 * 1024
-FETCH_VMEM_BYTES = 56 * 1024 * 1024
+FETCH_VMEM_BYTES = 60 * 1024 * 1024
 
 
 def across(block, axis, flip):
@@ -65,10 +65,7 @@
     tokens, width = key_rows.shape
 
     def kernel(select_hbm, key_hbm, value_hbm, *refs):
-        out_refs, (select_ref, row_ref, moved_ref, sems) = (
-            refs[: len(prefixes)],
-            refs[len(prefixes) :],
-        )
+        out_refs, (select_ref, row_ref, sems) = refs[: len(prefixes)], refs[len(prefixes) :]
         copies = [
             pltpu.make_async_copy(select_hbm, select_ref, sems.at[0]),
             pltpu.make_async_copy(key_hbm, row_ref.at[0], sems.at[1]),
@@ -77,24 +74,13 @@
         for copy in copies:
             copy.start()
         copies[0].wait()
-        stores = []
         for half in range(2):
             copies[1 + half].wait()
-            moved_ref[half] = jnp.dot(
+            moved = jnp.dot(
                 select_ref[...], row_ref[half], preferred_element_type=jnp.float32
             ).astype(jnp.bfloat16)
-            cols = slice(half * width, (half + 1) * width)
-            for (low, high), out_ref in zip(prefixes[:-1], out_refs):
-                stores.append(
-                    pltpu.make_async_copy(
-                        moved_ref.at[half, low:high], out_ref.at[:, cols], sems.at[3 + len(stores)]
-                    )
-                )
-                stores[-1].start()
-            low, high = prefixes[-1]
-            out_refs[-1][:, cols] = moved_ref[half, low : 2 * high, :][: high - low]
-        for store in stores:
-            store.wait()
+            for (low, high), out_ref in zip(prefixes, out_refs):
+                out_ref[:, half * width : (half + 1) * width] = moved[low:high]
 
     return pl.pallas_call(
         kernel,
@@ -102,13 +88,10 @@
             jax.ShapeDtypeStruct((high - low, 2 * width), jnp.bfloat16) for low, high in prefixes
         ],
         in_specs=[pl.BlockSpec(memory_space=pltpu.HBM)] * 3,
-        out_specs=[pl.BlockSpec(memory_space=pl.ANY)] * (len(prefixes) - 1)
-        + [pl.BlockSpec(memory_space=pltpu.VMEM)],
         scratch_shapes=[
             pltpu.VMEM(select.shape, jnp.bfloat16),
             pltpu.VMEM((2, tokens, width), jnp.bfloat16),
-            pltpu.VMEM((2, select.shape[0], width), jnp.bfloat16),
-            pltpu.SemaphoreType.DMA((3 + 2 * (len(prefixes) - 1),)),
+            pltpu.SemaphoreType.DMA((3,)),
         ],
         compiler_params=pltpu.CompilerParams(vmem_limit_bytes=FETCH_VMEM_BYTES),
         cost_estimate=pl.CostEstimate(
@@ -130,7 +113,7 @@
     row_runs = [(0, keys, 1)] if counts is None else runs(counts)
     scale = HEAD_DIM**-0.5 * LOG2E
     final = out_weight is not None
-    groups = max(len(states), 1)
+    groups = 2 if final else max(len(states), 1)
 
     def kernel(*refs):
         refs = list(refs)
@@ -144,20 +127,15 @@
             refs.pop(1 if final else 0)
         if final:
             weight_ref, out_hbm = refs.pop(0), refs.pop(0)
-            attended_ref, out_ref, result_ref, sems = refs[-4:]
+            attended_ref, out_ref, result_ref, sum_ref, sems = refs[-5:]
         else:
             numer_out, peak_out, total_out = [refs.pop(0) for _ in range(3)]
         score_ref, value_ref, key_ref, turned_ref = [refs.pop(0) for _ in range(4)]
+        ones = jnp.ones((16, padded), jnp.bfloat16)
         if row_strides is not None:
-            offset_ref = refs.pop(0)
-            row = lax.broadcasted_iota(jnp.int32, (keys, LANES), 0)
-            rank = sum((row & (s - 1) == 0).astype(jnp.int32) for s in row_strides)
-            offsets = jnp.zeros((keys, LANES), jnp.float32)
-            for times in range(1, len(row_strides) + 1):
-                offsets = jnp.where(rank == times, math.log2(1 + times), offsets)
-            offset_ref[...] = offsets
-
-        ones = jnp.ones((16, padded), jnp.bfloat16)
+            row = lax.broadcasted_iota(jnp.int32, (16, padded), 1)
+            times = sum((row & (s - 1) == 0).astype(jnp.int32) for s in [1] + row_strides)
+            ones = times.astype(jnp.float32).astype(jnp.bfloat16)
         key_chunks = [(low, min(KEY_CHUNK, keys - low)) for low in range(0, keys, KEY_CHUNK)]
         value_chunks = [(low, min(CHUNK, padded - low)) for low in range(0, padded, CHUNK)]
 
@@ -197,11 +175,7 @@
                 first, last = max(first, low), min(last, high)
                 if first < last:
                     offset = peak - math.log2(times)
-                    power = score_ref[half, first:last, :] * scale - offset
-                    if row_strides is not None:
-                        extra = offset_ref[first:last, :]
-                        power = power + jnp.concatenate([extra] * (tokens // LANES), axis=1)
-                    pieces.append(jnp.exp2(power))
+                    pieces.append(jnp.exp2(score_ref[half, first:last, :] * scale - offset))
             if low + size > keys:
                 pieces.append(jnp.zeros((low + size - keys, tokens), jnp.float32))
             probs = (pieces[0] if len(pieces) == 1 else jnp.concatenate(pieces, axis=0)).astype(
@@ -212,13 +186,13 @@
             )
             return product if gathered is None else gathered + product
 
-        def one_group(first_pair, last_pair, earlier):
+        def one_group(first_pair, last_pair, earlier, first_state):
             def local_rows(pair, half):
-                start = (pair - first_pair) * PAIR + half * HEAD_DIM
+                start = (pair - first_state) * PAIR + half * HEAD_DIM
                 return pl.ds(pl.multiple_of(start, HEAD_DIM), HEAD_DIM)
 
             def local_head(pair, half):
-                return pl.ds(2 * (pair - first_pair) + half, 1)
+                return pl.ds(2 * (pair - first_state) + half, 1)
 
             def finish(pair, half, gathered, peak, before):
                 numer, total = gathered[:HEAD_DIM], gathered[HEAD_DIM : HEAD_DIM + 1]
@@ -270,6 +244,8 @@
                 if padded > keys:
                     value_ref[keys:, :] = jnp.zeros((padded - keys, PAIR), jnp.bfloat16)
                 values_t = value_ref[...].T
+                if row_strides is not None:
+                    values_t = values_t * ones[:1]
                 running = overlap(pair, 0, running, values_t, pair, 1)
                 later = jnp.minimum(pair + 1, last_pair - 1)
                 return overlap(pair, 1, running, values_t, later, 0)
@@ -282,17 +258,28 @@
             lax.fori_loop(first_pair, last_pair, pair_step, running, unroll=UNROLL)
 
         for group in range(groups):
+            low, high = group * pairs // groups, (group + 1) * pairs // groups
+            shared = len(states) == 1
             one_group(
-                group * pairs // groups,
-                (group + 1) * pairs // groups,
-                state_refs[group] if states else None,
+                low, high, state_refs[0 if shared else group] if states else None, 0 if shared else low
             )
+            if final and group == 0:
+                sum_ref[...] = jnp.dot(
+                    out_ref[:, : high * PAIR],
+                    weight_ref[: high * PAIR, :],
+                    preferred_element_type=jnp.float32,
+                )
         if final:
-            copies = []
+            copies, split = [], pairs // groups * PAIR
             for at, low in enumerate(range(0, tokens, LANES)):
                 rows = slice(low, low + LANES)
-                result_ref[rows, :] = jnp.dot(
-                    out_ref[rows, :], weight_ref[...], preferred_element_type=jnp.float32
+                result_ref[rows, :] = (
+                    sum_ref[rows, :]
+                    + jnp.dot(
+                        out_ref[rows, split:],
+                        weight_ref[split:, :],
+                        preferred_element_type=jnp.float32,
+                    )
                 ).astype(jnp.bfloat16)
                 copies.append(
                     pltpu.make_async_copy(result_ref.at[rows], out_hbm.at[rows], sems.at[at])
@@ -315,11 +302,10 @@
         pltpu.VMEM((padded, PAIR), jnp.bfloat16),
         pltpu.VMEM((PAIR, tokens), jnp.bfloat16),
     ]
-    if row_strides is not None:
-        scratch.append(pltpu.VMEM((keys, LANES), jnp.float32))
     if final:
         scratch.append(pltpu.VMEM((2, HEAD_DIM, tokens), jnp.bfloat16))
         scratch += [pltpu.VMEM((tokens, width), jnp.bfloat16)] * 2
+        scratch.append(pltpu.VMEM((tokens, width), jnp.float32))
         scratch.append(pltpu.SemaphoreType.DMA((tokens // LANES,)))
     operands = [queries]
     for block, whole in zip(sets, joined):

time: 42.2 us -> 41.8 us (level)
    pallas_call x1, Pallas kernels: 3.62 us -> 3.08 us  [order_rows(): pl.pallas_call(kernel, out_shape=[jax.ShapeDtypeStruct((high - low, 2 * w...]
  transfers between devices with their start and end apart: 9 -> 9, of which waited for: 3 -> 4; matrix products, arithmetic and copies ran while one was open for 0% -> 0% of each run, Pallas kernels for 28% -> 27%
where the time goes in v4:
time: 41.8 us; the launch traced here: 41.7 us
  Pallas kernels  20.1 us (48%)
  starting transfers between devices  12.9 us (31%)
  waiting for transfers between devices  7.24 us (17%)
  local copies, waits for them, and re-layouts  1.16 us (3%)
    pallas_call x5, Pallas kernels, attend(): pl.pallas_call(kernel, out_shape=out_shape, in_specs=specs, **{'out_specs...  16.9 us
    ppermute x9, starting transfers between devices, across(): lax.ppermute(block, axis, [(i, i ^ flip) for i in range(lax.axis_size(axi...  12.9 us
    ppermute x9, waiting for transfers between devices, across(): lax.ppermute(block, axis, [(i, i ^ flip) for i in range(lax.axis_size(axi...  7.24 us
    pallas_call x1, Pallas kernels, order_rows(): pl.pallas_call(kernel, out_shape=[jax.ShapeDtypeStruct((high - low, 2 * w...  3.08 us
    unnamed x14, local copies, waits for them, and re-layouts  1.16 us
  transfers between devices with their start and end apart: 9, of which 4 were waited for; matrix products, arithmetic and copies ran while one was open for 0% of the time, Pallas kernels for 27%

profile of v4, /device:TPU:0, one launch (start us, length us, event | category | flops | bytes accessed | tf_op | source)
XLA Modules:
  0.0 41.7 jit_solution(13192163803046453262)
XLA Ops:
  0.0 3.1 %shard_map.55 = (bf16[128,1536]{1,0:T(8,128)(2,1)}, bf16[128,1536]{1,0:T(8,128)(2,1)}, bf16[8,1536]{1,0:T(8,128)(2,1)}) custom-call(bf16[256,512]{1,0:T(8,128)(2,1)} %constant.2.clone.select_hbm, bf16[512,768]{1,0:T(8,128)(2,1)} %bitcast.4, bf16[512,768]{1,0:T(8,128)(2,1)} %bitcast.7), custom_call_target="tpu_custom_call" | custom-call | flops 402653184 | bytes 2359296 | tf_op jit(solution)/shard_map/pallas_call | solution.py:85
  3.1 3.0 %collective-permute-start = (bf16[128,1536]{1,0:T(8,128)(2,1)}, bf16[128,1536]{1,0:T(8,128)(2,1)S(1)}, u32[]{:S(2)}, u32[]{:S(2)}) collective-permute-start(bf16[128,1536]{1,0:T(8,128)(2,1)} %get-tuple-element.20.refs_0_), channel_id=1, source_target_pairs={{0,8},{8,0},{16,24},{24,16},{1,9},{9,1},{17,25},{25,17},{2,10},{10... | collective-permute-start | bytes 1179656 | tf_op jit(solution)/shard_map/ppermute | solution.py:25
  6.1 1.5 %collective-permute-start.1 = (bf16[128,1536]{1,0:T(8,128)(2,1)}, bf16[128,1536]{1,0:T(8,128)(2,1)S(1)}, u32[]{:S(2)}, u32[]{:S(2)}) collective-permute-start(bf16[128,1536]{1,0:T(8,128)(2,1)} %get-tuple-element.20.refs_0_), channel_id=1, source_target_pairs={{0,16},{8,24},{16,0},{24,8},{1,17},{9,25},{17,1},{25,9},{2,18},{10... | collective-permute-start | bytes 1179656 | tf_op jit(solution)/shard_map/ppermute | solution.py:25
  7.6 1.6 %collective-permute-start.2 = (bf16[8,1536]{1,0:T(8,128)(2,1)}, bf16[8,1536]{1,0:T(8,128)(2,1)S(1)}, u32[]{:S(2)}, u32[]{:S(2)}) collective-permute-start(bf16[8,1536]{1,0:T(8,128)(2,1)} %get-tuple-element.21.refs_0_), channel_id=1, source_target_pairs={{0,2},{1,3},{2,0},{3,1},{4,6},{5,7},{6,4},{7,5},{8,10},{9,11},{10,... | collective-permute-start | bytes 73736 | tf_op jit(solution)/shard_map/ppermute | solution.py:25
  9.2 0.5 %collective-permute-start.7 = (bf16[128,1536]{1,0:T(8,128)(2,1)}, bf16[128,1536]{1,0:T(8,128)(2,1)S(1)}, u32[]{:S(2)}, u32[]{:S(2)}) collective-permute-start(bf16[128,1536]{1,0:T(8,128)(2,1)} %get-tuple-element.24), channel_id=1, source_target_pairs={{0,8},{8,0},{16,24},{24,16},{1,9},{9,1},{17,25},{25,17},{2,10},{10... | collective-permute-start | bytes 1179656 | tf_op jit(solution)/shard_map/ppermute | solution.py:25
  9.7 1.1 %copy-done.5 = bf16[1,512,768]{2,1,0:T(8,128)(2,1)S(1)} copy-done((bf16[1,512,768]{2,1,0:T(8,128)(2,1)S(1)}, bf16[1,512,768]{2,1,0:T(8,128)(2,1)}, u32[]{:S(2)}) %copy-start.5) | copy-done | bytes 786456
  10.9 2.7 %shard_map.56 = (f32[384,512]{1,0:T(8,128)S(1)}, f32[6,512]{1,0:T(8,128)S(1)}, f32[6,512]{1,0:T(8,128)S(1)}) custom-call(bf16[512,768]{1,0:T(8,128)(2,1)S(1)} %bitcast.10, bf16[512,768]{1,0:T(8,128)(2,1)S(1)} %bitcast.5, bf16[512,768]{1,0:T(8,128)(2,1)S(1)} %bitcast.8), custom_call_target="tpu_custom_call" | custom-call | flops 1610612736 | bytes 1572864 | tf_op jit(solution)/shard_map/pallas_call | solution.py:321
  13.5 0.0 collective-permute-done.2.refs_1_
  13.6 2.7 %collective-permute-start.3 = (bf16[16,1536]{1,0:T(8,128)(2,1)S(1)}, bf16[16,1536]{1,0:T(8,128)(2,1)S(1)}, u32[]{:S(2)}, u32[]{:S(2)}) collective-permute-start(bf16[16,1536]{1,0:T(8,128)(2,1)S(1)} %shard_map.57.refs_3_.refs_0_), channel_id=1, source_target_pairs={{0,4},{1,5},{2,6},{3,7},{4,0},{5,1},{6,2},{7,3},{8,12},{9,13},{10,... | collective-permute-start | bytes 147464 | tf_op jit(solution)/shard_map/ppermute | solution.py:25
  16.2 2.7 %shard_map.58 = (f32[384,512]{1,0:T(8,128)S(1)}, f32[6,512]{1,0:T(8,128)S(1)}, f32[6,512]{1,0:T(8,128)S(1)}) custom-call(bf16[512,768]{1,0:T(8,128)(2,1)S(1)} %bitcast.11, bf16[512,768]{1,0:T(8,128)(2,1)S(1)} %bitcast.6, bf16[512,768]{1,0:T(8,128)(2,1)S(1)} %bitcast.9, bf16[16,1536]{1,0:T(8,128)(2,1)S(1)} %shard_map.57.refs_3_.refs_0_), custom_call_target="tpu_custom_call" | custom-call | flops 1610612736 | bytes 1572864 | tf_op jit(solution)/shard_map/pallas_call | solution.py:321
  18.9 0.0 copy-start.6
  18.9 0.1 collective-permute-done.3.refs_1_
  19.1 0.5 %collective-permute-start.4 = (bf16[160,1536]{1,0:T(8,128)(2,1)S(1)}, bf16[160,1536]{1,0:T(8,128)(2,1)S(1)}, u32[]{:S(2)}, u32[]{:S(2)}) collective-permute-start(bf16[160,1536]{1,0:T(8,128)(2,1)S(1)} %shard_map.60), channel_id=1, source_target_pairs={{0,16},{8,24},{16,0},{24,8},{1,17},{9,25},{17,1},{25,9},{2,18},{10... | collective-permute-start | bytes 1474568 | tf_op jit(solution)/shard_map/ppermute | solution.py:25
  19.6 2.6 %collective-permute-start.6 = (bf16[32,1536]{1,0:T(8,128)(2,1)S(1)}, bf16[32,1536]{1,0:T(8,128)(2,1)S(1)}, u32[]{:S(2)}, u32[]{:S(2)}) collective-permute-start(bf16[32,1536]{1,0:T(8,128)(2,1)S(1)} %shard_map.59.refs_1_.refs_2_.refs_4_), channel_id=1, source_target_pairs={{0,24},{8,16},{16,8},{24,0},{1,25},{9,17},{17,9},{25,1},{2,26},{10... | collective-permute-start | bytes 294920 | tf_op jit(solution)/shard_map/ppermute | solution.py:25
  22.1 0.5 %collective-permute-start.5 = (bf16[32,1536]{1,0:T(8,128)(2,1)S(1)}, bf16[32,1536]{1,0:T(8,128)(2,1)S(1)}, u32[]{:S(2)}, u32[]{:S(2)}) collective-permute-start(bf16[32,1536]{1,0:T(8,128)(2,1)S(1)} %shard_map.59.refs_1_.refs_2_.refs_4_), channel_id=1, source_target_pairs={{0,8},{8,0},{16,24},{24,16},{1,9},{9,1},{17,25},{25,17},{2,10},{10... | collective-permute-start | bytes 294920 | tf_op jit(solution)/shard_map/ppermute | solution.py:25
  22.7 2.0 %collective-permute-done.7.refs_2_ = bf16[128,1536]{1,0:T(8,128)(2,1)S(1)} collective-permute-done((bf16[128,1536]{1,0:T(8,128)(2,1)}, bf16[128,1536]{1,0:T(8,128)(2,1)S(1)}, u32[]{:S(2)}, u32[]{:S(2)}) %collective-permute-start.7) | collective-permute-done | bytes 393248 | tf_op jit(solution)/shard_map/ppermute | solution.py:25
  24.7 2.9 %shard_map.61 = (f32[768,512]{1,0:T(8,128)S(1)}, f32[12,512]{1,0:T(8,128)S(1)}, f32[12,512]{1,0:T(8,128)S(1)}) custom-call(bf16[512,768]{1,0:T(8,128)(2,1)S(1)} %bitcast.12, bf16[128,1536]{1,0:T(8,128)(2,1)S(1)} %collective-permute-done.refs_0_.refs_1_, bf16[128,1536]{1,0:T(8,128)(2,1)S(1)} %collective-permute-done.7.refs_2_, ...), custom_call_target="tpu_custom_call" | custom-call | flops 2415919104 | bytes 2752512 | tf_op jit(solution)/shard_map/pallas_call | solution.py:321
  27.6 0.7 %collective-permute-done.6.refs_7_.refs_4_ = bf16[32,1536]{1,0:T(8,128)(2,1)S(1)} collective-permute-done((bf16[32,1536]{1,0:T(8,128)(2,1)S(1)}, bf16[32,1536]{1,0:T(8,128)(2,1)S(1)}, u32[]{:S(2)}, u32[]{:S(2)}) %collective-permute-start.6) | collective-permute-done | bytes 98336 | tf_op jit(solution)/shard_map/ppermute | solution.py:25
  28.3 4.4 %collective-permute-done.4.refs_3_.refs_6_.refs_1_ = bf16[160,1536]{1,0:T(8,128)(2,1)S(1)} collective-permute-done((bf16[160,1536]{1,0:T(8,128)(2,1)S(1)}, bf16[160,1536]{1,0:T(8,128)(2,1)S(1)}, u32[]{:S(2)}, u32[]{:S(2)}) %collective-permute-start.4) | collective-permute-done | bytes 491552 | tf_op jit(solution)/shard_map/ppermute | solution.py:25
  32.7 0.1 shard_map.62
  32.8 0.1 collective-permute-start.8
  32.9 0.0 copy-start.4
  32.9 2.9 %shard_map.63 = (f32[768,512]{1,0:T(8,128)S(1)}, f32[12,512]{1,0:T(8,128)S(1)}, f32[12,512]{1,0:T(8,128)S(1)}) custom-call(bf16[512,768]{1,0:T(8,128)(2,1)S(1)} %bitcast.13, bf16[160,1536]{1,0:T(8,128)(2,1)S(1)} %collective-permute-done.4.refs_3_.refs_6_.refs_1_, bf16[32,1536]{1,0:T(8,128)(2,1)S(1)} %shard_map.59.refs_1_.refs_2_.refs_4_, ...), custom_call_target="tpu_custom_call" | custom-call | flops 1610612736 | bytes 2359296 | tf_op jit(solution)/shard_map/pallas_call | solution.py:321
  35.9 5.7 %shard_map.64 = bf16[512,768]{1,0:T(8,128)(2,1)} custom-call(bf16[512,768]{1,0:T(8,128)(2,1)S(1)} %bitcast.14, bf16[384,1536]{1,0:T(8,128)(2,1)S(1)} %collective-permute-done.8.refs_1_, f32[768,512]{1,0:T(8,128)S(1)} %get-tuple-element.32.refs_2_, f32[12,512]{1,0:T(8,128)S(1)} %get-tuple-element.33.refs_3_, f32[12,512]{1,0:T(8,128)S(1)} %get-tuple-element.34.refs_4_, ...), custom_call_target="tpu_custom_call" | custom-call | flops 2415919104 | bytes 2752512 | tf_op jit(solution)/shard_map/pallas_call | solution.py:321
  (18 shorter events, 0.1 us)
Async XLA Ops:
  0.0 9.7 %copy-start.1 = (bf16[1,512,768]{2,1,0:T(8,128)(2,1)S(1)}, bf16[1,512,768]{2,1,0:T(8,128)(2,1)}, u32[]{:S(2)}) copy-start(bf16[1,512,768]{2,1,0:T(8,128)(2,1)} %param.7) | copy-start | bytes 2359300
  0.0 9.7 %copy-start = (bf16[1,512,768]{2,1,0:T(8,128)(2,1)S(1)}, bf16[1,512,768]{2,1,0:T(8,128)(2,1)}, u32[]{:S(2)}) copy-start(bf16[1,512,768]{2,1,0:T(8,128)(2,1)} %param.6) | copy-start | bytes 2359300
  3.1 16.0 %collective-permute-start = (bf16[128,1536]{1,0:T(8,128)(2,1)}, bf16[128,1536]{1,0:T(8,128)(2,1)S(1)}, u32[]{:S(2)}, u32[]{:S(2)}) collective-permute-start(bf16[128,1536]{1,0:T(8,128)(2,1)} %get-tuple-element.20.refs_0_), channel_id=1, source_target_pairs={{0,8},{8,0},{16,24},{24,16},{1,9},{9,1},{17,25},{25,17},{2,10},{10... | collective-permute-start | bytes 1179656 | tf_op jit(solution)/shard_map/ppermute | solution.py:25
  6.1 18.6 %collective-permute-start.1 = (bf16[128,1536]{1,0:T(8,128)(2,1)}, bf16[128,1536]{1,0:T(8,128)(2,1)S(1)}, u32[]{:S(2)}, u32[]{:S(2)}) collective-permute-start(bf16[128,1536]{1,0:T(8,128)(2,1)} %get-tuple-element.20.refs_0_), channel_id=1, source_target_pairs={{0,16},{8,24},{16,0},{24,8},{1,17},{9,25},{17,1},{25,9},{2,18},{10... | collective-permute-start | bytes 1179656 | tf_op jit(solution)/shard_map/ppermute | solution.py:25
  7.6 5.9 %collective-permute-start.2 = (bf16[8,1536]{1,0:T(8,128)(2,1)}, bf16[8,1536]{1,0:T(8,128)(2,1)S(1)}, u32[]{:S(2)}, u32[]{:S(2)}) collective-permute-start(bf16[8,1536]{1,0:T(8,128)(2,1)} %get-tuple-element.21.refs_0_), channel_id=1, source_target_pairs={{0,2},{1,3},{2,0},{3,1},{4,6},{5,7},{6,4},{7,5},{8,10},{9,11},{10,... | collective-permute-start | bytes 73736 | tf_op jit(solution)/shard_map/ppermute | solution.py:25
  9.2 15.5 %collective-permute-start.7 = (bf16[128,1536]{1,0:T(8,128)(2,1)}, bf16[128,1536]{1,0:T(8,128)(2,1)S(1)}, u32[]{:S(2)}, u32[]{:S(2)}) collective-permute-start(bf16[128,1536]{1,0:T(8,128)(2,1)} %get-tuple-element.24), channel_id=1, source_target_pairs={{0,8},{8,0},{16,24},{24,16},{1,9},{9,1},{17,25},{25,17},{2,10},{10... | collective-permute-start | bytes 1179656 | tf_op jit(solution)/shard_map/ppermute | solution.py:25
  9.7 1.1 %copy-start.5 = (bf16[1,512,768]{2,1,0:T(8,128)(2,1)S(1)}, bf16[1,512,768]{2,1,0:T(8,128)(2,1)}, u32[]{:S(2)}) copy-start(bf16[1,512,768]{2,1,0:T(8,128)(2,1)} %param.5) | copy-start | bytes 2359300
  10.9 2.7 %copy-start.3 = (bf16[8,1536]{1,0:T(8,128)(2,1)S(1)}, bf16[8,1536]{1,0:T(8,128)(2,1)}, u32[]{:S(2)}) copy-start(bf16[8,1536]{1,0:T(8,128)(2,1)} %get-tuple-element.21.refs_0_) | copy-start | bytes 73732
  13.6 5.5 %collective-permute-start.3 = (bf16[16,1536]{1,0:T(8,128)(2,1)S(1)}, bf16[16,1536]{1,0:T(8,128)(2,1)S(1)}, u32[]{:S(2)}, u32[]{:S(2)}) collective-permute-start(bf16[16,1536]{1,0:T(8,128)(2,1)S(1)} %shard_map.57.refs_3_.refs_0_), channel_id=1, source_target_pairs={{0,4},{1,5},{2,6},{3,7},{4,0},{5,1},{6,2},{7,3},{8,12},{9,13},{10,... | collective-permute-start | bytes 147464 | tf_op jit(solution)/shard_map/ppermute | solution.py:25
  18.9 5.8 %copy-start.6 = (bf16[1,512,768]{2,1,0:T(8,128)(2,1)S(1)}, bf16[1,512,768]{2,1,0:T(8,128)(2,1)}, u32[]{:S(2)}) copy-start(bf16[1,512,768]{2,1,0:T(8,128)(2,1)} %param.5) | copy-start | bytes 2359300
  19.1 13.6 %collective-permute-start.4 = (bf16[160,1536]{1,0:T(8,128)(2,1)S(1)}, bf16[160,1536]{1,0:T(8,128)(2,1)S(1)}, u32[]{:S(2)}, u32[]{:S(2)}) collective-permute-start(bf16[160,1536]{1,0:T(8,128)(2,1)S(1)} %shard_map.60), channel_id=1, source_target_pairs={{0,16},{8,24},{16,0},{24,8},{1,17},{9,25},{17,1},{25,9},{2,18},{10... | collective-permute-start | bytes 1474568 | tf_op jit(solution)/shard_map/ppermute | solution.py:25
  19.6 8.7 %collective-permute-start.6 = (bf16[32,1536]{1,0:T(8,128)(2,1)S(1)}, bf16[32,1536]{1,0:T(8,128)(2,1)S(1)}, u32[]{:S(2)}, u32[]{:S(2)}) collective-permute-start(bf16[32,1536]{1,0:T(8,128)(2,1)S(1)} %shard_map.59.refs_1_.refs_2_.refs_4_), channel_id=1, source_target_pairs={{0,24},{8,16},{16,8},{24,0},{1,25},{9,17},{17,9},{25,1},{2,26},{10... | collective-permute-start | bytes 294920 | tf_op jit(solution)/shard_map/ppermute | solution.py:25
  22.1 6.2 %collective-permute-start.5 = (bf16[32,1536]{1,0:T(8,128)(2,1)S(1)}, bf16[32,1536]{1,0:T(8,128)(2,1)S(1)}, u32[]{:S(2)}, u32[]{:S(2)}) collective-permute-start(bf16[32,1536]{1,0:T(8,128)(2,1)S(1)} %shard_map.59.refs_1_.refs_2_.refs_4_), channel_id=1, source_target_pairs={{0,8},{8,0},{16,24},{24,16},{1,9},{9,1},{17,25},{25,17},{2,10},{10... | collective-permute-start | bytes 294920 | tf_op jit(solution)/shard_map/ppermute | solution.py:25
  24.7 8.1 %copy-start.2 = (bf16[128,1536]{1,0:T(8,128)(2,1)S(1)}, bf16[128,1536]{1,0:T(8,128)(2,1)}, u32[]{:S(2)}) copy-start(bf16[128,1536]{1,0:T(8,128)(2,1)} %get-tuple-element.20.refs_0_) | copy-start | bytes 1179652
  32.8 3.0 %collective-permute-start.8 = (bf16[384,1536]{1,0:T(8,128)(2,1)S(1)}, bf16[384,1536]{1,0:T(8,128)(2,1)S(1)}, u32[]{:S(2)}, u32[]{:S(2)}) collective-permute-start(bf16[384,1536]{1,0:T(8,128)(2,1)S(1)} %shard_map.62), channel_id=1, source_target_pairs={{0,1},{1,0},{2,3},{3,2},{4,5},{5,4},{6,7},{7,6},{8,9},{9,8},{10,11... | collective-permute-start | bytes 3538952 | tf_op jit(solution)/shard_map/ppermute | solution.py:25
  32.9 2.9 %copy-start.4 = (bf16[768,768]{1,0:T(8,128)(2,1)S(1)}, bf16[768,768]{1,0:T(8,128)(2,1)}, u32[]{:S(2)}) copy-start(bf16[768,768]{1,0:T(8,128)(2,1)} %refs_5_.1) | copy-start | bytes 3538948

commit v5 on v4

--- a/solution.py
+++ b/solution.py
@@ -14,6 +14,8 @@
 CHUNK = 256
 KEY_CHUNK = 512
 UNROLL = 3
+OWN_PARTS = 3
+PIECES = 4
 LANES = 128
 LOG2E = math.log2(math.e)
 VMEM_BYTES = 16 * 1024 * 1024
@@ -61,21 +63,37 @@
     return [tuple(entry) for entry in found]
 
 
+def row_copies(source, target, sems):
+    count = source.shape[0] // PIECES
+    copies = []
+    for at in range(PIECES):
+        rows = pl.ds(at * count, count)
+        copies.append(pltpu.make_async_copy(source.at[rows], target.at[rows], sems.at[at]))
+        copies[-1].start()
+    return copies
+
+
+def fetch_rows(source, target, sems):
+    for copy in row_copies(source, target, sems):
+        copy.wait()
+
+
 def order_rows(select, key_rows, values, prefixes):
     tokens, width = key_rows.shape
 
     def kernel(select_hbm, key_hbm, value_hbm, *refs):
         out_refs, (select_ref, row_ref, sems) = refs[: len(prefixes)], refs[len(prefixes) :]
+        sources = (select_hbm, key_hbm, value_hbm)
+        targets = (select_ref, row_ref.at[0], row_ref.at[1])
         copies = [
-            pltpu.make_async_copy(select_hbm, select_ref, sems.at[0]),
-            pltpu.make_async_copy(key_hbm, row_ref.at[0], sems.at[1]),
-            pltpu.make_async_copy(value_hbm, row_ref.at[1], sems.at[2]),
+            row_copies(source, target, sems.at[at])
+            for at, (source, target) in enumerate(zip(sources, targets))
         ]
-        for copy in copies:
-            copy.start()
-        copies[0].wait()
+        for copy in copies[0]:
+            copy.wait()
         for half in range(2):
-            copies[1 + half].wait()
+            for copy in copies[1 + half]:
+                copy.wait()
             moved = jnp.dot(
                 select_ref[...], row_ref[half], preferred_element_type=jnp.float32
             ).astype(jnp.bfloat16)
@@ -91,7 +109,7 @@
         scratch_shapes=[
             pltpu.VMEM(select.shape, jnp.bfloat16),
             pltpu.VMEM((2, tokens, width), jnp.bfloat16),
-            pltpu.SemaphoreType.DMA((3,)),
+            pltpu.SemaphoreType.DMA((3, PIECES)),
         ],
         compiler_params=pltpu.CompilerParams(vmem_limit_bytes=FETCH_VMEM_BYTES),
         cost_estimate=pl.CostEstimate(
@@ -113,7 +131,7 @@
     row_runs = [(0, keys, 1)] if counts is None else runs(counts)
     scale = HEAD_DIM**-0.5 * LOG2E
     final = out_weight is not None
-    groups = 2 if final else max(len(states), 1)
+    groups = max(len(states), 1)
 
     def kernel(*refs):
         refs = list(refs)
@@ -127,7 +145,7 @@
             refs.pop(1 if final else 0)
         if final:
             weight_ref, out_hbm = refs.pop(0), refs.pop(0)
-            attended_ref, out_ref, result_ref, sum_ref, sems = refs[-5:]
+            attended_ref, out_ref, result_ref, sems = refs[-4:]
         else:
             numer_out, peak_out, total_out = [refs.pop(0) for _ in range(3)]
         score_ref, value_ref, key_ref, turned_ref = [refs.pop(0) for _ in range(4)]
@@ -255,7 +273,7 @@
             running = None
             for chunk in key_chunks:
                 running = score(0, first_head, chunk, running)
-            lax.fori_loop(first_pair, last_pair, pair_step, running, unroll=UNROLL)
+            lax.fori_loop(first_pair, last_pair, pair_step, running, unroll=min(UNROLL, last_pair - first_pair))
 
         for group in range(groups):
             low, high = group * pairs // groups, (group + 1) * pairs // groups
@@ -263,23 +281,12 @@
             one_group(
                 low, high, state_refs[0 if shared else group] if states else None, 0 if shared else low
             )
-            if final and group == 0:
-                sum_ref[...] = jnp.dot(
-                    out_ref[:, : high * PAIR],
-                    weight_ref[: high * PAIR, :],
-                    preferred_element_type=jnp.float32,
-                )
         if final:
-            copies, split = [], pairs // groups * PAIR
+            copies = []
             for at, low in enumerate(range(0, tokens, LANES)):
                 rows = slice(low, low + LANES)
-                result_ref[rows, :] = (
-                    sum_ref[rows, :]
-                    + jnp.dot(
-                        out_ref[rows, split:],
-                        weight_ref[split:, :],
-                        preferred_element_type=jnp.float32,
-                    )
+                result_ref[rows, :] = jnp.dot(
+                    out_ref[rows, :], weight_ref[...], preferred_element_type=jnp.float32
                 ).astype(jnp.bfloat16)
                 copies.append(
                     pltpu.make_async_copy(result_ref.at[rows], out_hbm.at[rows], sems.at[at])
@@ -305,7 +312,6 @@
     if final:
         scratch.append(pltpu.VMEM((2, HEAD_DIM, tokens), jnp.bfloat16))
         scratch += [pltpu.VMEM((tokens, width), jnp.bfloat16)] * 2
-        scratch.append(pltpu.VMEM((tokens, width), jnp.float32))
         scratch.append(pltpu.SemaphoreType.DMA((tokens // LANES,)))
     operands = [queries]
     for block, whole in zip(sets, joined):
@@ -366,21 +372,19 @@
     held[1] = (across(first_a, "inner", 1), 0)
     own_set = [(own_keys, own_values)]
     own_states, moved, flip = [], far, 2
-    while flip < n_outer or len(own_states) < 2:
-        if flip < n_outer:
-            came = across(moved, "outer", flip)
-            flip *= 2
-        if len(own_states) < 2:
-            own_states.append(
-                attend(
-                    query_rows,
-                    own_set,
-                    row_strides=strides,
-                    part=(len(own_states), 2),
-                    wait=moved if own_states else None,
-                )
-            )
+
+    def own_part(wait):
+        part = (len(own_states), OWN_PARTS)
+        own_states.append(
+            attend(query_rows, own_set, row_strides=strides, part=part, wait=wait)
+        )
+
+    while flip < n_outer:
+        came = across(moved, "outer", flip)
+        if len(own_states) < OWN_PARTS - 1:
+            own_part(moved if own_states else None)
         moved = join_after([(moved, 0, moved.shape[0]), (came, 0, came.shape[0])], own_states[-1][1])
+        flip *= 2
     far = moved
     n_far = far.shape[0]
     fars = {0: (far, 0)}
@@ -388,14 +392,16 @@
     def first_rows(where, count):
         return (where[0], where[1], where[1] + count)
 
-    near_b = across(first_b, "inner", 1)
-    fars[1] = (across(far, "inner", 1), 0)
+    pieces = [first_rows((first_b, 0), sends[0] - sends[1]), first_rows(fars[0], n_far)]
+    near_b = across(join_after(pieces, far), "inner", 1)
+    fars[1] = (near_b, sends[0] - sends[1])
     own_done = far
 
     known = [0] + [1 << bit for bit in range(inner_bits)]
     late = [d for d in range(n_inner) if d not in known]
     last = sends[inner_bits]
-    late_sets, late_counts = [], []
+    late_sets = [near_b]
+    late_counts = [prefix_counts(0, sends[1], sends[0]), np.ones(n_far, np.int64)]
     for bit in range(1, inner_bits):
         count = sends[bit]
         others = range(1, 1 << bit)
@@ -409,15 +415,21 @@
         late_counts += [prefix_counts(bit, 0, count)] * len(others) + [np.ones(n_far, np.int64)]
     for d in late:
         fars[d] = (across(far, "inner", d), 0)
-    late_sets += [fars[d][0] for d in [0, 1] + late]
-    late_counts.append(np.ones(n_far * (2 + len(late)), np.int64))
-
-    early_sets = [held[1][0], near_b] + [held[d][0] for d in known[2:]]
-    early_counts = [prefix_counts(0, 0, sends[0])]
+    late_sets += [fars[d][0] for d in late]
+    late_counts.append(np.ones(n_far * len(late), np.int64))
+
+    moved = join_after([first_rows(held[d], last) for d in known], own_done)
+    early_core = across(moved, "outer", 1)
+    while len(own_states) < OWN_PARTS:
+        own_part(moved)
+
+    early_sets = [held[d][0] for d in known[1:]] + [early_core, far]
+    early_counts = [prefix_counts(0, 0, sends[1])]
     early_counts += [prefix_counts(bit, 0, sends[bit]) for bit in range(1, inner_bits)]
+    early_counts.append(np.ones(early_core.shape[0] + n_far, np.int64))
     state = attend(query_rows, early_sets, np.concatenate(early_counts), states=own_states)
 
-    pieces = [first_rows(held[d], last) for d in range(n_inner)]
+    pieces = [first_rows(held[d], last) for d in late]
     pieces += [first_rows(fars[d], n_far) for d in range(n_inner)]
     core = across(join_after(pieces, state[1]), "outer", 1)
     state = attend(query_rows, late_sets, np.concatenate(late_counts), states=[state])

time: 41.8 us -> 42.3 us (1.012)
  local copies, waits for them, and re-layouts: 1.16 us -> 1.95 us
  waiting for transfers between devices: 7.24 us -> 6.69 us
  Pallas kernels: 20.1 us -> 20.6 us
  starting transfers between devices: 12.9 us -> 12.4 us
    unnamed x14, local copies, waits for them, and re-layouts: 1.16 us -> 1.95 us
    ppermute x9, waiting for transfers between devices: 7.24 us -> 6.69 us  [across(): lax.ppermute(block, axis, [(i, i ^ flip) for i in range(lax.axis_size(axi...]
    ppermute x9, starting transfers between devices: 12.9 us -> 12.4 us  [across(): lax.ppermute(block, axis, [(i, i ^ flip) for i in range(lax.axis_size(axi...]
    pallas_call x5 -> x6, Pallas kernels: 16.9 us -> 17.2 us  [attend(): pl.pallas_call(kernel, out_shape=out_shape, in_specs=specs, **{'out_specs...]
  transfers between devices with their start and end apart: 9 -> 9, of which waited for: 4 -> 3; matrix products, arithmetic and copies ran while one was open for 0% -> 0% of each run, Pallas kernels for 27% -> 31%
where the time goes in v5:
time: 42.3 us; the launch traced here: 42 us
  Pallas kernels  20.6 us (49%)
  starting transfers between devices  12.4 us (29%)
  waiting for transfers between devices  6.69 us (16%)
  local copies, waits for them, and re-layouts  1.95 us (5%)
    pallas_call x6, Pallas kernels, attend(): pl.pallas_call(kernel, out_shape=out_shape, in_specs=specs, **{'out_specs...  17.2 us
    ppermute x9, starting transfers between devices, across(): lax.ppermute(block, axis, [(i, i ^ flip) for i in range(lax.axis_size(axi...  12.4 us
    ppermute x9, waiting for transfers between devices, across(): lax.ppermute(block, axis, [(i, i ^ flip) for i in range(lax.axis_size(axi...  6.69 us
    pallas_call x1, Pallas kernels, order_rows(): pl.pallas_call(kernel, out_shape=[jax.ShapeDtypeStruct((high - low, 2 * w...  3.25 us
    unnamed x14, local copies, waits for them, and re-layouts  1.95 us
  transfers between devices with their start and end apart: 9, of which 3 were waited for; matrix products, arithmetic and copies ran while one was open for 0% of the time, Pallas kernels for 31%

profile of v5, /device:TPU:0, one launch (start us, length us, event | category | flops | bytes accessed | tf_op | source)
XLA Modules:
  0.0 42.0 jit_solution(15074121915149832859)
XLA Ops:
  0.0 3.2 %shard_map.55 = (bf16[128,1536]{1,0:T(8,128)(2,1)}, bf16[128,1536]{1,0:T(8,128)(2,1)}, bf16[8,1536]{1,0:T(8,128)(2,1)}) custom-call(bf16[256,512]{1,0:T(8,128)(2,1)} %constant.2.clone.select_hbm, bf16[512,768]{1,0:T(8,128)(2,1)} %bitcast.4, bf16[512,768]{1,0:T(8,128)(2,1)} %bitcast.8), custom_call_target="tpu_custom_call" | custom-call | flops 402653184 | bytes 2359296 | tf_op jit(solution)/shard_map/pallas_call | solution.py:103
  3.3 3.0 %collective-permute-start = (bf16[128,1536]{1,0:T(8,128)(2,1)}, bf16[128,1536]{1,0:T(8,128)(2,1)S(1)}, u32[]{:S(2)}, u32[]{:S(2)}) collective-permute-start(bf16[128,1536]{1,0:T(8,128)(2,1)} %get-tuple-element.23.refs_0_), channel_id=1, source_target_pairs={{0,8},{8,0},{16,24},{24,16},{1,9},{9,1},{17,25},{25,17},{2,10},{10... | collective-permute-start | bytes 1179656 | tf_op jit(solution)/shard_map/ppermute | solution.py:27
  6.3 1.5 %collective-permute-start.6 = (bf16[128,1536]{1,0:T(8,128)(2,1)}, bf16[128,1536]{1,0:T(8,128)(2,1)S(1)}, u32[]{:S(2)}, u32[]{:S(2)}) collective-permute-start(bf16[128,1536]{1,0:T(8,128)(2,1)} %get-tuple-element.23.refs_0_), channel_id=1, source_target_pairs={{0,16},{8,24},{16,0},{24,8},{1,17},{9,25},{17,1},{25,9},{2,18},{10... | collective-permute-start | bytes 1179656 | tf_op jit(solution)/shard_map/ppermute | solution.py:27
  7.8 1.6 %collective-permute-start.1 = (bf16[8,1536]{1,0:T(8,128)(2,1)}, bf16[8,1536]{1,0:T(8,128)(2,1)S(1)}, u32[]{:S(2)}, u32[]{:S(2)}) collective-permute-start(bf16[8,1536]{1,0:T(8,128)(2,1)} %get-tuple-element.24.refs_0_), channel_id=1, source_target_pairs={{0,2},{1,3},{2,0},{3,1},{4,6},{5,7},{6,4},{7,5},{8,10},{9,11},{10,... | collective-permute-start | bytes 73736 | tf_op jit(solution)/shard_map/ppermute | solution.py:27
  9.4 1.1 %copy-done.3 = bf16[1,512,768]{2,1,0:T(8,128)(2,1)S(1)} copy-done((bf16[1,512,768]{2,1,0:T(8,128)(2,1)S(1)}, bf16[1,512,768]{2,1,0:T(8,128)(2,1)}, u32[]{:S(2)}) %copy-start.3) | copy-done | bytes 786456
  10.5 1.9 %shard_map.56 = (f32[256,512]{1,0:T(8,128)S(1)}, f32[4,512]{1,0:T(4,128)S(1)}, f32[4,512]{1,0:T(4,128)S(1)}) custom-call(bf16[512,768]{1,0:T(8,128)(2,1)S(1)} %bitcast.12, bf16[512,768]{1,0:T(8,128)(2,1)S(1)} %bitcast.5, bf16[512,768]{1,0:T(8,128)(2,1)S(1)} %bitcast.9), custom_call_target="tpu_custom_call" | custom-call | flops 1073741824 | bytes 1048576 | tf_op jit(solution)/shard_map/pallas_call | solution.py:327
  12.4 0.0 collective-permute-done.1.refs_1_
  12.4 0.0 copy-start.5
  12.4 2.7 %collective-permute-start.2 = (bf16[16,1536]{1,0:T(8,128)(2,1)S(1)}, bf16[16,1536]{1,0:T(8,128)(2,1)S(1)}, u32[]{:S(2)}, u32[]{:S(2)}) collective-permute-start(bf16[16,1536]{1,0:T(8,128)(2,1)S(1)} %shard_map.57.refs_3_.refs_0_), channel_id=1, source_target_pairs={{0,4},{1,5},{2,6},{3,7},{4,0},{5,1},{6,2},{7,3},{8,12},{9,13},{10,... | collective-permute-start | bytes 147464 | tf_op jit(solution)/shard_map/ppermute | solution.py:27
  15.1 1.9 %shard_map.58 = (f32[256,512]{1,0:T(8,128)S(1)}, f32[4,512]{1,0:T(4,128)S(1)}, f32[4,512]{1,0:T(4,128)S(1)}) custom-call(bf16[512,768]{1,0:T(8,128)(2,1)S(1)} %bitcast.13, bf16[512,768]{1,0:T(8,128)(2,1)S(1)} %bitcast.6, bf16[512,768]{1,0:T(8,128)(2,1)S(1)} %bitcast.10, bf16[16,1536]{1,0:T(8,128)(2,1)S(1)} %shard_map.57.refs_3_.refs_0_), custom_call_target="tpu_custom_call" | custom-call | flops 1073741824 | bytes 1048576 | tf_op jit(solution)/shard_map/pallas_call | solution.py:327
  16.9 0.5 %collective-permute-done.2.refs_1_ = bf16[16,1536]{1,0:T(8,128)(2,1)S(1)} collective-permute-done((bf16[16,1536]{1,0:T(8,128)(2,1)S(1)}, bf16[16,1536]{1,0:T(8,128)(2,1)S(1)}, u32[]{:S(2)}, u32[]{:S(2)}) %collective-permute-start.2) | collective-permute-done | bytes 49184 | tf_op jit(solution)/shard_map/ppermute | solution.py:27
  17.5 0.0 collective-permute-done.refs_0_.refs_1_
  17.6 0.1 collective-permute-start.7
  17.7 0.8 %copy-done.4 = bf16[128,1536]{1,0:T(8,128)(2,1)S(1)} copy-done((bf16[128,1536]{1,0:T(8,128)(2,1)S(1)}, bf16[128,1536]{1,0:T(8,128)(2,1)}, u32[]{:S(2)}) %copy-start.4) | copy-done | bytes 393240
  18.5 1.1 %collective-permute-start.4 = (bf16[160,1536]{1,0:T(8,128)(2,1)S(1)}, bf16[160,1536]{1,0:T(8,128)(2,1)S(1)}, u32[]{:S(2)}, u32[]{:S(2)}) collective-permute-start(bf16[160,1536]{1,0:T(8,128)(2,1)S(1)} %shard_map.61), channel_id=1, source_target_pairs={{0,8},{8,0},{16,24},{24,16},{1,9},{9,1},{17,25},{25,17},{2,10},{10... | collective-permute-start | bytes 1474568 | tf_op jit(solution)/shard_map/ppermute | solution.py:27
  19.7 2.4 %collective-permute-start.5 = (bf16[32,1536]{1,0:T(8,128)(2,1)S(1)}, bf16[32,1536]{1,0:T(8,128)(2,1)S(1)}, u32[]{:S(2)}, u32[]{:S(2)}) collective-permute-start(bf16[32,1536]{1,0:T(8,128)(2,1)S(1)} %shard_map.59.refs_1_.refs_2_.refs_4_), channel_id=1, source_target_pairs={{0,24},{8,16},{16,8},{24,0},{1,25},{9,17},{17,9},{25,1},{2,26},{10... | collective-permute-start | bytes 294920 | tf_op jit(solution)/shard_map/ppermute | solution.py:27
  22.1 1.9 %shard_map.63 = (f32[256,512]{1,0:T(8,128)S(1)}, f32[4,512]{1,0:T(4,128)S(1)}, f32[4,512]{1,0:T(4,128)S(1)}) custom-call(bf16[512,768]{1,0:T(8,128)(2,1)S(1)} %bitcast.14, bf16[512,768]{1,0:T(8,128)(2,1)S(1)} %bitcast.7, bf16[512,768]{1,0:T(8,128)(2,1)S(1)} %bitcast.11, bf16[192,1536]{1,0:T(8,128)(2,1)S(1)} %shard_map.62.refs_3_), custom_call_target="tpu_custom_call" | custom-call | flops 1073741824 | bytes 1048576 | tf_op jit(solution)/shard_map/pallas_call | solution.py:327
  24.0 4.2 %shard_map.64 = (f32[768,512]{1,0:T(8,128)S(1)}, f32[12,512]{1,0:T(8,128)S(1)}, f32[12,512]{1,0:T(8,128)S(1)}) custom-call(bf16[512,768]{1,0:T(8,128)(2,1)S(1)} %bitcast.15, bf16[128,1536]{1,0:T(8,128)(2,1)S(1)} %collective-permute-done.refs_0_.refs_1_, bf16[128,1536]{1,0:T(8,128)(2,1)S(1)} %collective-permute-done.6.refs_2_, ...), custom_call_target="tpu_custom_call" | custom-call | flops 3019898880 | bytes 3047424 | tf_op jit(solution)/shard_map/pallas_call | solution.py:327
  28.2 5.9 %collective-permute-done.5.refs_4_.refs_3_ = bf16[32,1536]{1,0:T(8,128)(2,1)S(1)} collective-permute-done((bf16[32,1536]{1,0:T(8,128)(2,1)S(1)}, bf16[32,1536]{1,0:T(8,128)(2,1)S(1)}, u32[]{:S(2)}, u32[]{:S(2)}) %collective-permute-start.5) | collective-permute-done | bytes 98336 | tf_op jit(solution)/shard_map/ppermute | solution.py:27
  34.1 0.2 collective-permute-done.3.refs_0_.refs_3_.refs_2_
  34.4 0.1 collective-permute-start.8
  34.4 0.0 copy-start
  34.5 3.3 %shard_map.66 = (f32[768,512]{1,0:T(8,128)S(1)}, f32[12,512]{1,0:T(8,128)S(1)}, f32[12,512]{1,0:T(8,128)S(1)}) custom-call(bf16[512,768]{1,0:T(8,128)(2,1)S(1)} %bitcast.16, bf16[160,1536]{1,0:T(8,128)(2,1)S(1)} %collective-permute-done.4.refs_2_.refs_1_, bf16[160,1536]{1,0:T(8,128)(2,1)S(1)} %collective-permute-done.3.refs_0_.refs_3_.refs_2_, ...), custom_call_target="tpu_custom_call" | custom-call | flops 2214592512 | bytes 2654208 | tf_op jit(solution)/shard_map/pallas_call | solution.py:327
  37.8 4.1 %shard_map.67 = bf16[512,768]{1,0:T(8,128)(2,1)} custom-call(bf16[512,768]{1,0:T(8,128)(2,1)S(1)} %bitcast.17, bf16[192,1536]{1,0:T(8,128)(2,1)S(1)} %collective-permute-done.8.refs_1_, f32[768,512]{1,0:T(8,128)S(1)} %get-tuple-element.38.refs_2_, f32[12,512]{1,0:T(8,128)S(1)} %get-tuple-element.39.refs_3_, f32[12,512]{1,0:T(8,128)S(1)} %get-tuple-element.40.refs_4_, ...), custom_call_target="tpu_custom_call" | custom-call | flops 1207959552 | bytes 2162688 | tf_op jit(solution)/shard_map/pallas_call | solution.py:327
  (21 shorter events, 0.2 us)
Async XLA Ops:
  0.0 9.4 %copy-start.1 = (bf16[1,512,768]{2,1,0:T(8,128)(2,1)S(1)}, bf16[1,512,768]{2,1,0:T(8,128)(2,1)}, u32[]{:S(2)}) copy-start(bf16[1,512,768]{2,1,0:T(8,128)(2,1)} %param.6) | copy-start | bytes 2359300
  0.0 9.4 %copy-start.2 = (bf16[1,512,768]{2,1,0:T(8,128)(2,1)S(1)}, bf16[1,512,768]{2,1,0:T(8,128)(2,1)}, u32[]{:S(2)}) copy-start(bf16[1,512,768]{2,1,0:T(8,128)(2,1)} %param.7) | copy-start | bytes 2359300
  3.3 14.3 %collective-permute-start = (bf16[128,1536]{1,0:T(8,128)(2,1)}, bf16[128,1536]{1,0:T(8,128)(2,1)S(1)}, u32[]{:S(2)}, u32[]{:S(2)}) collective-permute-start(bf16[128,1536]{1,0:T(8,128)(2,1)} %get-tuple-element.23.refs_0_), channel_id=1, source_target_pairs={{0,8},{8,0},{16,24},{24,16},{1,9},{9,1},{17,25},{25,17},{2,10},{10... | collective-permute-start | bytes 1179656 | tf_op jit(solution)/shard_map/ppermute | solution.py:27
  6.3 11.3 %collective-permute-start.6 = (bf16[128,1536]{1,0:T(8,128)(2,1)}, bf16[128,1536]{1,0:T(8,128)(2,1)S(1)}, u32[]{:S(2)}, u32[]{:S(2)}) collective-permute-start(bf16[128,1536]{1,0:T(8,128)(2,1)} %get-tuple-element.23.refs_0_), channel_id=1, source_target_pairs={{0,16},{8,24},{16,0},{24,8},{1,17},{9,25},{17,1},{25,9},{2,18},{10... | collective-permute-start | bytes 1179656 | tf_op jit(solution)/shard_map/ppermute | solution.py:27
  7.8 4.6 %collective-permute-start.1 = (bf16[8,1536]{1,0:T(8,128)(2,1)}, bf16[8,1536]{1,0:T(8,128)(2,1)S(1)}, u32[]{:S(2)}, u32[]{:S(2)}) collective-permute-start(bf16[8,1536]{1,0:T(8,128)(2,1)} %get-tuple-element.24.refs_0_), channel_id=1, source_target_pairs={{0,2},{1,3},{2,0},{3,1},{4,6},{5,7},{6,4},{7,5},{8,10},{9,11},{10,... | collective-permute-start | bytes 73736 | tf_op jit(solution)/shard_map/ppermute | solution.py:27
  9.4 1.1 %copy-start.3 = (bf16[1,512,768]{2,1,0:T(8,128)(2,1)S(1)}, bf16[1,512,768]{2,1,0:T(8,128)(2,1)}, u32[]{:S(2)}) copy-start(bf16[1,512,768]{2,1,0:T(8,128)(2,1)} %param.5) | copy-start | bytes 2359300
  10.5 1.9 %copy-start.6 = (bf16[8,1536]{1,0:T(8,128)(2,1)S(1)}, bf16[8,1536]{1,0:T(8,128)(2,1)}, u32[]{:S(2)}) copy-start(bf16[8,1536]{1,0:T(8,128)(2,1)} %get-tuple-element.24.refs_0_) | copy-start | bytes 73732
  12.4 5.2 %copy-start.5 = (bf16[128,1536]{1,0:T(8,128)(2,1)S(1)}, bf16[128,1536]{1,0:T(8,128)(2,1)}, u32[]{:S(2)}) copy-start(bf16[128,1536]{1,0:T(8,128)(2,1)} %get-tuple-element.23.refs_0_) | copy-start | bytes 1179652
  12.4 5.1 %collective-permute-start.2 = (bf16[16,1536]{1,0:T(8,128)(2,1)S(1)}, bf16[16,1536]{1,0:T(8,128)(2,1)S(1)}, u32[]{:S(2)}, u32[]{:S(2)}) collective-permute-start(bf16[16,1536]{1,0:T(8,128)(2,1)S(1)} %shard_map.57.refs_3_.refs_0_), channel_id=1, source_target_pairs={{0,4},{1,5},{2,6},{3,7},{4,0},{5,1},{6,2},{7,3},{8,12},{9,13},{10,... | collective-permute-start | bytes 147464 | tf_op jit(solution)/shard_map/ppermute | solution.py:27
  17.5 1.0 %copy-start.4 = (bf16[128,1536]{1,0:T(8,128)(2,1)S(1)}, bf16[128,1536]{1,0:T(8,128)(2,1)}, u32[]{:S(2)}) copy-start(bf16[128,1536]{1,0:T(8,128)(2,1)} %get-tuple-element.27.refs_0_) | copy-start | bytes 1179652
  17.6 6.3 %collective-permute-start.7 = (bf16[192,1536]{1,0:T(8,128)(2,1)S(1)}, bf16[192,1536]{1,0:T(8,128)(2,1)S(1)}, u32[]{:S(2)}, u32[]{:S(2)}) collective-permute-start(bf16[192,1536]{1,0:T(8,128)(2,1)S(1)} %shard_map.62.refs_3_), channel_id=1, source_target_pairs={{0,1},{1,0},{2,3},{3,2},{4,5},{5,4},{6,7},{7,6},{8,9},{9,8},{10,11... | collective-permute-start | bytes 1769480 | tf_op jit(solution)/shard_map/ppermute | solution.py:27
  18.5 15.5 %collective-permute-start.4 = (bf16[160,1536]{1,0:T(8,128)(2,1)S(1)}, bf16[160,1536]{1,0:T(8,128)(2,1)S(1)}, u32[]{:S(2)}, u32[]{:S(2)}) collective-permute-start(bf16[160,1536]{1,0:T(8,128)(2,1)S(1)} %shard_map.61), channel_id=1, source_target_pairs={{0,8},{8,0},{16,24},{24,16},{1,9},{9,1},{17,25},{25,17},{2,10},{10... | collective-permute-start | bytes 1474568 | tf_op jit(solution)/shard_map/ppermute | solution.py:27
  19.7 14.7 %collective-permute-start.3 = (bf16[160,1536]{1,0:T(8,128)(2,1)S(1)}, bf16[160,1536]{1,0:T(8,128)(2,1)S(1)}, u32[]{:S(2)}, u32[]{:S(2)}) collective-permute-start(bf16[160,1536]{1,0:T(8,128)(2,1)S(1)} %shard_map.60.refs_3_), channel_id=1, source_target_pairs={{0,16},{8,24},{16,0},{24,8},{1,17},{9,25},{17,1},{25,9},{2,18},{10... | collective-permute-start | bytes 1474568 | tf_op jit(solution)/shard_map/ppermute | solution.py:27
  19.7 14.4 %collective-permute-start.5 = (bf16[32,1536]{1,0:T(8,128)(2,1)S(1)}, bf16[32,1536]{1,0:T(8,128)(2,1)S(1)}, u32[]{:S(2)}, u32[]{:S(2)}) collective-permute-start(bf16[32,1536]{1,0:T(8,128)(2,1)S(1)} %shard_map.59.refs_1_.refs_2_.refs_4_), channel_id=1, source_target_pairs={{0,24},{8,16},{16,8},{24,0},{1,25},{9,17},{17,9},{25,1},{2,26},{10... | collective-permute-start | bytes 294920 | tf_op jit(solution)/shard_map/ppermute | solution.py:27
  34.4 3.4 %collective-permute-start.8 = (bf16[192,1536]{1,0:T(8,128)(2,1)S(1)}, bf16[192,1536]{1,0:T(8,128)(2,1)S(1)}, u32[]{:S(2)}, u32[]{:S(2)}) collective-permute-start(bf16[192,1536]{1,0:T(8,128)(2,1)S(1)} %shard_map.65), channel_id=1, source_target_pairs={{0,1},{1,0},{2,3},{3,2},{4,5},{5,4},{6,7},{7,6},{8,9},{9,8},{10,11... | collective-permute-start | bytes 1769480 | tf_op jit(solution)/shard_map/ppermute | solution.py:27
  34.4 3.4 %copy-start = (bf16[768,768]{1,0:T(8,128)(2,1)S(1)}, bf16[768,768]{1,0:T(8,128)(2,1)}, u32[]{:S(2)}) copy-start(bf16[768,768]{1,0:T(8,128)(2,1)} %refs_5_.1) | copy-start | bytes 3538948

commit v6 on v4

--- a/solution.py
+++ b/solution.py
@@ -13,7 +13,6 @@
 PAIR = 2 * HEAD_DIM
 CHUNK = 256
 KEY_CHUNK = 512
-UNROLL = 3
 LANES = 128
 LOG2E = math.log2(math.e)
 VMEM_BYTES = 16 * 1024 * 1024
@@ -113,7 +112,7 @@
     row_runs = [(0, keys, 1)] if counts is None else runs(counts)
     scale = HEAD_DIM**-0.5 * LOG2E
     final = out_weight is not None
-    groups = 2 if final else max(len(states), 1)
+    groups = max(len(states), 1)
 
     def kernel(*refs):
         refs = list(refs)
@@ -127,7 +126,7 @@
             refs.pop(1 if final else 0)
         if final:
             weight_ref, out_hbm = refs.pop(0), refs.pop(0)
-            attended_ref, out_ref, result_ref, sum_ref, sems = refs[-5:]
+            attended_ref, out_ref, result_ref, sems = refs[-4:]
         else:
             numer_out, peak_out, total_out = [refs.pop(0) for _ in range(3)]
         score_ref, value_ref, key_ref, turned_ref = [refs.pop(0) for _ in range(4)]
@@ -139,11 +138,8 @@
         key_chunks = [(low, min(KEY_CHUNK, keys - low)) for low in range(0, keys, KEY_CHUNK)]
         value_chunks = [(low, min(CHUNK, padded - low)) for low in range(0, padded, CHUNK)]
 
-        def column(pair):
-            return pl.multiple_of(pair * PAIR, PAIR)
-
         def columns(pair, shift=0):
-            return pl.ds(pl.multiple_of(base + shift + pair * PAIR, PAIR), PAIR)
+            return pl.ds(base + shift + pair * PAIR, PAIR)
 
         def head_queries(half):
             turned = turned_ref[...]
@@ -189,7 +185,7 @@
         def one_group(first_pair, last_pair, earlier, first_state):
             def local_rows(pair, half):
                 start = (pair - first_state) * PAIR + half * HEAD_DIM
-                return pl.ds(pl.multiple_of(start, HEAD_DIM), HEAD_DIM)
+                return pl.ds(start, HEAD_DIM)
 
             def local_head(pair, half):
                 return pl.ds(2 * (pair - first_state) + half, 1)
@@ -200,13 +196,12 @@
                     factor = jnp.exp2(before - peak)
                     numer = numer + factor * earlier[0][local_rows(pair, half), :]
                     total = total + factor * earlier[2][local_head(pair, half), :]
-                start = pl.multiple_of(column(pair) + half * HEAD_DIM, HEAD_DIM)
-                rows = pl.ds(start, HEAD_DIM)
+                rows = pl.ds(pair * PAIR + half * HEAD_DIM, HEAD_DIM)
                 if final:
                     attended_ref[half] = (numer * (1.0 / total)).astype(jnp.bfloat16)
                     if half == 1:
                         both = attended_ref[...].reshape(PAIR, tokens)
-                        out_ref[:, pl.ds(column(pair), PAIR)] = both.T
+                        out_ref[:, pl.ds(pair * PAIR, PAIR)] = both.T
                 else:
                     head = pl.ds(2 * pair + half, 1)
                     numer_out[rows, :] = numer
@@ -222,12 +217,13 @@
                 weighted = jnp.concatenate(
                     [values_t[half * HEAD_DIM : (half + 1) * HEAD_DIM], ones], axis=0
                 )
-                if next_half == 0:
+                ahead = next_pair < last_pair
+                if ahead and next_half == 0:
                     load(next_pair)
-                query_head = head_queries(next_half)
+                query_head = head_queries(next_half) if ahead else None
                 next_running, gathered = None, None
                 for step in range(max(len(key_chunks), len(value_chunks))):
-                    if step < len(key_chunks):
+                    if ahead and step < len(key_chunks):
                         next_running = score(
                             next_half, query_head, key_chunks[step], next_running
                         )
@@ -247,15 +243,15 @@
                 if row_strides is not None:
                     values_t = values_t * ones[:1]
                 running = overlap(pair, 0, running, values_t, pair, 1)
-                later = jnp.minimum(pair + 1, last_pair - 1)
-                return overlap(pair, 1, running, values_t, later, 0)
+                return overlap(pair, 1, running, values_t, pair + 1, 0)
 
             load(first_pair)
             first_head = head_queries(0)
             running = None
             for chunk in key_chunks:
                 running = score(0, first_head, chunk, running)
-            lax.fori_loop(first_pair, last_pair, pair_step, running, unroll=UNROLL)
+            for pair in range(first_pair, last_pair):
+                running = pair_step(pair, running)
 
         for group in range(groups):
             low, high = group * pairs // groups, (group + 1) * pairs // groups
@@ -263,23 +259,12 @@
             one_group(
                 low, high, state_refs[0 if shared else group] if states else None, 0 if shared else low
             )
-            if final and group == 0:
-                sum_ref[...] = jnp.dot(
-                    out_ref[:, : high * PAIR],
-                    weight_ref[: high * PAIR, :],
-                    preferred_element_type=jnp.float32,
-                )
         if final:
-            copies, split = [], pairs // groups * PAIR
+            copies = []
             for at, low in enumerate(range(0, tokens, LANES)):
                 rows = slice(low, low + LANES)
-                result_ref[rows, :] = (
-                    sum_ref[rows, :]
-                    + jnp.dot(
-                        out_ref[rows, split:],
-                        weight_ref[split:, :],
-                        preferred_element_type=jnp.float32,
-                    )
+                result_ref[rows, :] = jnp.dot(
+                    out_ref[rows, :], weight_ref[...], preferred_element_type=jnp.float32
                 ).astype(jnp.bfloat16)
                 copies.append(
                     pltpu.make_async_copy(result_ref.at[rows], out_hbm.at[rows], sems.at[at])
@@ -305,7 +290,6 @@
     if final:
         scratch.append(pltpu.VMEM((2, HEAD_DIM, tokens), jnp.bfloat16))
         scratch += [pltpu.VMEM((tokens, width), jnp.bfloat16)] * 2
-        scratch.append(pltpu.VMEM((tokens, width), jnp.float32))
         scratch.append(pltpu.SemaphoreType.DMA((tokens // LANES,)))
     operands = [queries]
     for block, whole in zip(sets, joined):

time: 41.8 us -> 41.1 us (0.983)
  Pallas kernels: 20.1 us -> 18.8 us
  waiting for transfers between devices: 7.24 us -> 7.81 us
    pallas_call x5, Pallas kernels: 16.9 us -> 15.6 us  [attend(): pl.pallas_call(kernel, out_shape=out_shape, in_specs=specs, **{'out_specs...]
    ppermute x9, waiting for transfers between devices: 7.24 us -> 7.81 us  [across(): lax.ppermute(block, axis, [(i, i ^ flip) for i in range(lax.axis_size(axi...]
  transfers between devices with their start and end apart: 9 -> 9, of which waited for: 4 -> 5; matrix products, arithmetic and copies ran while one was open for 0% -> 0% of each run, Pallas kernels for 27% -> 25%
where the time goes in v6:
time: 41.1 us; the launch traced here: 41 us
  Pallas kernels  18.8 us (46%)
  starting transfers between devices  12.9 us (31%)
  waiting for transfers between devices  7.81 us (19%)
  local copies, waits for them, and re-layouts  1.16 us (3%)
    pallas_call x5, Pallas kernels, attend(): pl.pallas_call(kernel, out_shape=out_shape, in_specs=specs, **{'out_specs...  15.6 us
    ppermute x9, starting transfers between devices, across(): lax.ppermute(block, axis, [(i, i ^ flip) for i in range(lax.axis_size(axi...  12.9 us
    ppermute x9, waiting for transfers between devices, across(): lax.ppermute(block, axis, [(i, i ^ flip) for i in range(lax.axis_size(axi...  7.81 us
    pallas_call x1, Pallas kernels, order_rows(): pl.pallas_call(kernel, out_shape=[jax.ShapeDtypeStruct((high - low, 2 * w...  3.08 us
    unnamed x14, local copies, waits for them, and re-layouts  1.16 us
  transfers between devices with their start and end apart: 9, of which 5 were waited for; matrix products, arithmetic and copies ran while one was open for 0% of the time, Pallas kernels for 25%

profile of v6, /device:TPU:0, one launch (start us, length us, event | category | flops | bytes accessed | tf_op | source)
XLA Modules:
  0.0 41.0 jit_solution(7049171437527189051)
XLA Ops:
  0.0 3.1 %shard_map.55 = (bf16[128,1536]{1,0:T(8,128)(2,1)}, bf16[128,1536]{1,0:T(8,128)(2,1)}, bf16[8,1536]{1,0:T(8,128)(2,1)}) custom-call(bf16[256,512]{1,0:T(8,128)(2,1)} %constant.2.clone.select_hbm, bf16[512,768]{1,0:T(8,128)(2,1)} %bitcast.4, bf16[512,768]{1,0:T(8,128)(2,1)} %bitcast.7), custom_call_target="tpu_custom_call" | custom-call | flops 402653184 | bytes 2359296 | tf_op jit(solution)/shard_map/pallas_call | solution.py:84
  3.1 3.0 %collective-permute-start = (bf16[128,1536]{1,0:T(8,128)(2,1)}, bf16[128,1536]{1,0:T(8,128)(2,1)S(1)}, u32[]{:S(2)}, u32[]{:S(2)}) collective-permute-start(bf16[128,1536]{1,0:T(8,128)(2,1)} %get-tuple-element.20.refs_0_), channel_id=1, source_target_pairs={{0,8},{8,0},{16,24},{24,16},{1,9},{9,1},{17,25},{25,17},{2,10},{10... | collective-permute-start | bytes 1179656 | tf_op jit(solution)/shard_map/ppermute | solution.py:24
  6.1 1.5 %collective-permute-start.1 = (bf16[128,1536]{1,0:T(8,128)(2,1)}, bf16[128,1536]{1,0:T(8,128)(2,1)S(1)}, u32[]{:S(2)}, u32[]{:S(2)}) collective-permute-start(bf16[128,1536]{1,0:T(8,128)(2,1)} %get-tuple-element.20.refs_0_), channel_id=1, source_target_pairs={{0,16},{8,24},{16,0},{24,8},{1,17},{9,25},{17,1},{25,9},{2,18},{10... | collective-permute-start | bytes 1179656 | tf_op jit(solution)/shard_map/ppermute | solution.py:24
  7.6 1.6 %collective-permute-start.2 = (bf16[8,1536]{1,0:T(8,128)(2,1)}, bf16[8,1536]{1,0:T(8,128)(2,1)S(1)}, u32[]{:S(2)}, u32[]{:S(2)}) collective-permute-start(bf16[8,1536]{1,0:T(8,128)(2,1)} %get-tuple-element.21.refs_0_), channel_id=1, source_target_pairs={{0,2},{1,3},{2,0},{3,1},{4,6},{5,7},{6,4},{7,5},{8,10},{9,11},{10,... | collective-permute-start | bytes 73736 | tf_op jit(solution)/shard_map/ppermute | solution.py:24
  9.2 0.5 %collective-permute-start.7 = (bf16[128,1536]{1,0:T(8,128)(2,1)}, bf16[128,1536]{1,0:T(8,128)(2,1)S(1)}, u32[]{:S(2)}, u32[]{:S(2)}) collective-permute-start(bf16[128,1536]{1,0:T(8,128)(2,1)} %get-tuple-element.24), channel_id=1, source_target_pairs={{0,8},{8,0},{16,24},{24,16},{1,9},{9,1},{17,25},{25,17},{2,10},{10... | collective-permute-start | bytes 1179656 | tf_op jit(solution)/shard_map/ppermute | solution.py:24
  9.7 1.1 %copy-done.5 = bf16[1,512,768]{2,1,0:T(8,128)(2,1)S(1)} copy-done((bf16[1,512,768]{2,1,0:T(8,128)(2,1)S(1)}, bf16[1,512,768]{2,1,0:T(8,128)(2,1)}, u32[]{:S(2)}) %copy-start.5) | copy-done | bytes 786456
  10.9 2.6 %shard_map.56 = (f32[384,512]{1,0:T(8,128)S(1)}, f32[6,512]{1,0:T(8,128)S(1)}, f32[6,512]{1,0:T(8,128)S(1)}) custom-call(bf16[512,768]{1,0:T(8,128)(2,1)S(1)} %bitcast.10, bf16[512,768]{1,0:T(8,128)(2,1)S(1)} %bitcast.5, bf16[512,768]{1,0:T(8,128)(2,1)S(1)} %bitcast.8), custom_call_target="tpu_custom_call" | custom-call | flops 1610612736 | bytes 1572864 | tf_op jit(solution)/shard_map/pallas_call | solution.py:305
  13.5 2.7 %collective-permute-start.3 = (bf16[16,1536]{1,0:T(8,128)(2,1)S(1)}, bf16[16,1536]{1,0:T(8,128)(2,1)S(1)}, u32[]{:S(2)}, u32[]{:S(2)}) collective-permute-start(bf16[16,1536]{1,0:T(8,128)(2,1)S(1)} %shard_map.57.refs_3_.refs_0_), channel_id=1, source_target_pairs={{0,4},{1,5},{2,6},{3,7},{4,0},{5,1},{6,2},{7,3},{8,12},{9,13},{10,... | collective-permute-start | bytes 147464 | tf_op jit(solution)/shard_map/ppermute | solution.py:24
  16.2 2.6 %shard_map.58 = (f32[384,512]{1,0:T(8,128)S(1)}, f32[6,512]{1,0:T(8,128)S(1)}, f32[6,512]{1,0:T(8,128)S(1)}) custom-call(bf16[512,768]{1,0:T(8,128)(2,1)S(1)} %bitcast.11, bf16[512,768]{1,0:T(8,128)(2,1)S(1)} %bitcast.6, bf16[512,768]{1,0:T(8,128)(2,1)S(1)} %bitcast.9, bf16[16,1536]{1,0:T(8,128)(2,1)S(1)} %shard_map.57.refs_3_.refs_0_), custom_call_target="tpu_custom_call" | custom-call | flops 1610612736 | bytes 1572864 | tf_op jit(solution)/shard_map/pallas_call | solution.py:305
  18.8 0.0 copy-start.6
  18.8 0.2 collective-permute-done.3.refs_1_
  19.0 0.4 collective-permute-start.4
  19.4 2.6 %collective-permute-start.6 = (bf16[32,1536]{1,0:T(8,128)(2,1)S(1)}, bf16[32,1536]{1,0:T(8,128)(2,1)S(1)}, u32[]{:S(2)}, u32[]{:S(2)}) collective-permute-start(bf16[32,1536]{1,0:T(8,128)(2,1)S(1)} %shard_map.59.refs_1_.refs_2_.refs_4_), channel_id=1, source_target_pairs={{0,24},{8,16},{16,8},{24,0},{1,25},{9,17},{17,9},{25,1},{2,26},{10... | collective-permute-start | bytes 294920 | tf_op jit(solution)/shard_map/ppermute | solution.py:24
  22.1 0.5 %collective-permute-start.5 = (bf16[32,1536]{1,0:T(8,128)(2,1)S(1)}, bf16[32,1536]{1,0:T(8,128)(2,1)S(1)}, u32[]{:S(2)}, u32[]{:S(2)}) collective-permute-start(bf16[32,1536]{1,0:T(8,128)(2,1)S(1)} %shard_map.59.refs_1_.refs_2_.refs_4_), channel_id=1, source_target_pairs={{0,8},{8,0},{16,24},{24,16},{1,9},{9,1},{17,25},{25,17},{2,10},{10... | collective-permute-start | bytes 294920 | tf_op jit(solution)/shard_map/ppermute | solution.py:24
  22.6 2.1 %collective-permute-done.7.refs_2_ = bf16[128,1536]{1,0:T(8,128)(2,1)S(1)} collective-permute-done((bf16[128,1536]{1,0:T(8,128)(2,1)}, bf16[128,1536]{1,0:T(8,128)(2,1)S(1)}, u32[]{:S(2)}, u32[]{:S(2)}) %collective-permute-start.7) | collective-permute-done | bytes 393248 | tf_op jit(solution)/shard_map/ppermute | solution.py:24
  24.7 2.9 %shard_map.61 = (f32[768,512]{1,0:T(8,128)S(1)}, f32[12,512]{1,0:T(8,128)S(1)}, f32[12,512]{1,0:T(8,128)S(1)}) custom-call(bf16[512,768]{1,0:T(8,128)(2,1)S(1)} %bitcast.12, bf16[128,1536]{1,0:T(8,128)(2,1)S(1)} %collective-permute-done.refs_0_.refs_1_, bf16[128,1536]{1,0:T(8,128)(2,1)S(1)} %collective-permute-done.7.refs_2_, ...), custom_call_target="tpu_custom_call" | custom-call | flops 2415919104 | bytes 2752512 | tf_op jit(solution)/shard_map/pallas_call | solution.py:305
  27.6 0.7 %collective-permute-done.6.refs_7_.refs_4_ = bf16[32,1536]{1,0:T(8,128)(2,1)S(1)} collective-permute-done((bf16[32,1536]{1,0:T(8,128)(2,1)S(1)}, bf16[32,1536]{1,0:T(8,128)(2,1)S(1)}, u32[]{:S(2)}, u32[]{:S(2)}) %collective-permute-start.6) | collective-permute-done | bytes 98336 | tf_op jit(solution)/shard_map/ppermute | solution.py:24
  28.3 4.3 %collective-permute-done.4.refs_3_.refs_6_.refs_1_ = bf16[160,1536]{1,0:T(8,128)(2,1)S(1)} collective-permute-done((bf16[160,1536]{1,0:T(8,128)(2,1)S(1)}, bf16[160,1536]{1,0:T(8,128)(2,1)S(1)}, u32[]{:S(2)}, u32[]{:S(2)}) %collective-permute-start.4) | collective-permute-done | bytes 491552 | tf_op jit(solution)/shard_map/ppermute | solution.py:24
  32.6 0.1 shard_map.62
  32.7 0.1 collective-permute-start.8
  32.7 0.0 copy-start.4
  32.8 2.3 %shard_map.63 = (f32[768,512]{1,0:T(8,128)S(1)}, f32[12,512]{1,0:T(8,128)S(1)}, f32[12,512]{1,0:T(8,128)S(1)}) custom-call(bf16[512,768]{1,0:T(8,128)(2,1)S(1)} %bitcast.13, bf16[160,1536]{1,0:T(8,128)(2,1)S(1)} %collective-permute-done.4.refs_3_.refs_6_.refs_1_, bf16[32,1536]{1,0:T(8,128)(2,1)S(1)} %shard_map.59.refs_1_.refs_2_.refs_4_, ...), custom_call_target="tpu_custom_call" | custom-call | flops 1610612736 | bytes 2359296 | tf_op jit(solution)/shard_map/pallas_call | solution.py:305
  35.1 0.5 %collective-permute-done.8.refs_1_ = bf16[384,1536]{1,0:T(8,128)(2,1)S(1)} collective-permute-done((bf16[384,1536]{1,0:T(8,128)(2,1)S(1)}, bf16[384,1536]{1,0:T(8,128)(2,1)S(1)}, u32[]{:S(2)}, u32[]{:S(2)}) %collective-permute-start.8) | collective-permute-done | bytes 1179680 | tf_op jit(solution)/shard_map/ppermute | solution.py:24
  35.6 5.2 %shard_map.64 = bf16[512,768]{1,0:T(8,128)(2,1)} custom-call(bf16[512,768]{1,0:T(8,128)(2,1)S(1)} %bitcast.14, bf16[384,1536]{1,0:T(8,128)(2,1)S(1)} %collective-permute-done.8.refs_1_, f32[768,512]{1,0:T(8,128)S(1)} %get-tuple-element.32.refs_2_, f32[12,512]{1,0:T(8,128)S(1)} %get-tuple-element.33.refs_3_, f32[12,512]{1,0:T(8,128)S(1)} %get-tuple-element.34.refs_4_, ...), custom_call_target="tpu_custom_call" | custom-call | flops 2415919104 | bytes 2752512 | tf_op jit(solution)/shard_map/pallas_call | solution.py:305
  (18 shorter events, 0.1 us)
Async XLA Ops:
  0.0 9.7 %copy-start.1 = (bf16[1,512,768]{2,1,0:T(8,128)(2,1)S(1)}, bf16[1,512,768]{2,1,0:T(8,128)(2,1)}, u32[]{:S(2)}) copy-start(bf16[1,512,768]{2,1,0:T(8,128)(2,1)} %param.7) | copy-start | bytes 2359300
  0.0 9.7 %copy-start = (bf16[1,512,768]{2,1,0:T(8,128)(2,1)S(1)}, bf16[1,512,768]{2,1,0:T(8,128)(2,1)}, u32[]{:S(2)}) copy-start(bf16[1,512,768]{2,1,0:T(8,128)(2,1)} %param.6) | copy-start | bytes 2359300
  3.1 15.9 %collective-permute-start = (bf16[128,1536]{1,0:T(8,128)(2,1)}, bf16[128,1536]{1,0:T(8,128)(2,1)S(1)}, u32[]{:S(2)}, u32[]{:S(2)}) collective-permute-start(bf16[128,1536]{1,0:T(8,128)(2,1)} %get-tuple-element.20.refs_0_), channel_id=1, source_target_pairs={{0,8},{8,0},{16,24},{24,16},{1,9},{9,1},{17,25},{25,17},{2,10},{10... | collective-permute-start | bytes 1179656 | tf_op jit(solution)/shard_map/ppermute | solution.py:24
  6.1 18.6 %collective-permute-start.1 = (bf16[128,1536]{1,0:T(8,128)(2,1)}, bf16[128,1536]{1,0:T(8,128)(2,1)S(1)}, u32[]{:S(2)}, u32[]{:S(2)}) collective-permute-start(bf16[128,1536]{1,0:T(8,128)(2,1)} %get-tuple-element.20.refs_0_), channel_id=1, source_target_pairs={{0,16},{8,24},{16,0},{24,8},{1,17},{9,25},{17,1},{25,9},{2,18},{10... | collective-permute-start | bytes 1179656 | tf_op jit(solution)/shard_map/ppermute | solution.py:24
  7.6 5.9 %collective-permute-start.2 = (bf16[8,1536]{1,0:T(8,128)(2,1)}, bf16[8,1536]{1,0:T(8,128)(2,1)S(1)}, u32[]{:S(2)}, u32[]{:S(2)}) collective-permute-start(bf16[8,1536]{1,0:T(8,128)(2,1)} %get-tuple-element.21.refs_0_), channel_id=1, source_target_pairs={{0,2},{1,3},{2,0},{3,1},{4,6},{5,7},{6,4},{7,5},{8,10},{9,11},{10,... | collective-permute-start | bytes 73736 | tf_op jit(solution)/shard_map/ppermute | solution.py:24
  9.2 15.5 %collective-permute-start.7 = (bf16[128,1536]{1,0:T(8,128)(2,1)}, bf16[128,1536]{1,0:T(8,128)(2,1)S(1)}, u32[]{:S(2)}, u32[]{:S(2)}) collective-permute-start(bf16[128,1536]{1,0:T(8,128)(2,1)} %get-tuple-element.24), channel_id=1, source_target_pairs={{0,8},{8,0},{16,24},{24,16},{1,9},{9,1},{17,25},{25,17},{2,10},{10... | collective-permute-start | bytes 1179656 | tf_op jit(solution)/shard_map/ppermute | solution.py:24
  9.7 1.1 %copy-start.5 = (bf16[1,512,768]{2,1,0:T(8,128)(2,1)S(1)}, bf16[1,512,768]{2,1,0:T(8,128)(2,1)}, u32[]{:S(2)}) copy-start(bf16[1,512,768]{2,1,0:T(8,128)(2,1)} %param.5) | copy-start | bytes 2359300
  10.9 2.6 %copy-start.3 = (bf16[8,1536]{1,0:T(8,128)(2,1)S(1)}, bf16[8,1536]{1,0:T(8,128)(2,1)}, u32[]{:S(2)}) copy-start(bf16[8,1536]{1,0:T(8,128)(2,1)} %get-tuple-element.21.refs_0_) | copy-start | bytes 73732
  13.5 5.5 %collective-permute-start.3 = (bf16[16,1536]{1,0:T(8,128)(2,1)S(1)}, bf16[16,1536]{1,0:T(8,128)(2,1)S(1)}, u32[]{:S(2)}, u32[]{:S(2)}) collective-permute-start(bf16[16,1536]{1,0:T(8,128)(2,1)S(1)} %shard_map.57.refs_3_.refs_0_), channel_id=1, source_target_pairs={{0,4},{1,5},{2,6},{3,7},{4,0},{5,1},{6,2},{7,3},{8,12},{9,13},{10,... | collective-permute-start | bytes 147464 | tf_op jit(solution)/shard_map/ppermute | solution.py:24
  18.8 5.9 %copy-start.6 = (bf16[1,512,768]{2,1,0:T(8,128)(2,1)S(1)}, bf16[1,512,768]{2,1,0:T(8,128)(2,1)}, u32[]{:S(2)}) copy-start(bf16[1,512,768]{2,1,0:T(8,128)(2,1)} %param.5) | copy-start | bytes 2359300
  19.0 13.5 %collective-permute-start.4 = (bf16[160,1536]{1,0:T(8,128)(2,1)S(1)}, bf16[160,1536]{1,0:T(8,128)(2,1)S(1)}, u32[]{:S(2)}, u32[]{:S(2)}) collective-permute-start(bf16[160,1536]{1,0:T(8,128)(2,1)S(1)} %shard_map.60), channel_id=1, source_target_pairs={{0,16},{8,24},{16,0},{24,8},{1,17},{9,25},{17,1},{25,9},{2,18},{10... | collective-permute-start | bytes 1474568 | tf_op jit(solution)/shard_map/ppermute | solution.py:24
  19.4 8.9 %collective-permute-start.6 = (bf16[32,1536]{1,0:T(8,128)(2,1)S(1)}, bf16[32,1536]{1,0:T(8,128)(2,1)S(1)}, u32[]{:S(2)}, u32[]{:S(2)}) collective-permute-start(bf16[32,1536]{1,0:T(8,128)(2,1)S(1)} %shard_map.59.refs_1_.refs_2_.refs_4_), channel_id=1, source_target_pairs={{0,24},{8,16},{16,8},{24,0},{1,25},{9,17},{17,9},{25,1},{2,26},{10... | collective-permute-start | bytes 294920 | tf_op jit(solution)/shard_map/ppermute | solution.py:24
  22.1 6.3 %collective-permute-start.5 = (bf16[32,1536]{1,0:T(8,128)(2,1)S(1)}, bf16[32,1536]{1,0:T(8,128)(2,1)S(1)}, u32[]{:S(2)}, u32[]{:S(2)}) collective-permute-start(bf16[32,1536]{1,0:T(8,128)(2,1)S(1)} %shard_map.59.refs_1_.refs_2_.refs_4_), channel_id=1, source_target_pairs={{0,8},{8,0},{16,24},{24,16},{1,9},{9,1},{17,25},{25,17},{2,10},{10... | collective-permute-start | bytes 294920 | tf_op jit(solution)/shard_map/ppermute | solution.py:24
  24.7 7.9 %copy-start.2 = (bf16[128,1536]{1,0:T(8,128)(2,1)S(1)}, bf16[128,1536]{1,0:T(8,128)(2,1)}, u32[]{:S(2)}) copy-start(bf16[128,1536]{1,0:T(8,128)(2,1)} %get-tuple-element.20.refs_0_) | copy-start | bytes 1179652
  32.7 2.9 %collective-permute-start.8 = (bf16[384,1536]{1,0:T(8,128)(2,1)S(1)}, bf16[384,1536]{1,0:T(8,128)(2,1)S(1)}, u32[]{:S(2)}, u32[]{:S(2)}) collective-permute-start(bf16[384,1536]{1,0:T(8,128)(2,1)S(1)} %shard_map.62), channel_id=1, source_target_pairs={{0,1},{1,0},{2,3},{3,2},{4,5},{5,4},{6,7},{7,6},{8,9},{9,8},{10,11... | collective-permute-start | bytes 3538952 | tf_op jit(solution)/shard_map/ppermute | solution.py:24
  32.7 2.8 %copy-start.4 = (bf16[768,768]{1,0:T(8,128)(2,1)S(1)}, bf16[768,768]{1,0:T(8,128)(2,1)}, u32[]{:S(2)}) copy-start(bf16[768,768]{1,0:T(8,128)(2,1)} %refs_5_.1) | copy-start | bytes 3538948

commit v7 on v6

--- a/solution.py
+++ b/solution.py
@@ -125,8 +125,8 @@
         if wait is not None:
             refs.pop(1 if final else 0)
         if final:
-            weight_ref, out_hbm = refs.pop(0), refs.pop(0)
-            attended_ref, out_ref, result_ref, sems = refs[-4:]
+            weight_ref, out_ref = refs.pop(0), refs.pop(0)
+            attended_ref, row_ref = refs[-2:]
         else:
             numer_out, peak_out, total_out = [refs.pop(0) for _ in range(3)]
         score_ref, value_ref, key_ref, turned_ref = [refs.pop(0) for _ in range(4)]
@@ -201,7 +201,7 @@
                     attended_ref[half] = (numer * (1.0 / total)).astype(jnp.bfloat16)
                     if half == 1:
                         both = attended_ref[...].reshape(PAIR, tokens)
-                        out_ref[:, pl.ds(pair * PAIR, PAIR)] = both.T
+                        row_ref[:, pl.ds(pair * PAIR, PAIR)] = both.T
                 else:
                     head = pl.ds(2 * pair + half, 1)
                     numer_out[rows, :] = numer
@@ -260,18 +260,9 @@
                 low, high, state_refs[0 if shared else group] if states else None, 0 if shared else low
             )
         if final:
-            copies = []
-            for at, low in enumerate(range(0, tokens, LANES)):
-                rows = slice(low, low + LANES)
-                result_ref[rows, :] = jnp.dot(
-                    out_ref[rows, :], weight_ref[...], preferred_element_type=jnp.float32
-                ).astype(jnp.bfloat16)
-                copies.append(
-                    pltpu.make_async_copy(result_ref.at[rows], out_hbm.at[rows], sems.at[at])
-                )
-                copies[-1].start()
-            for copy in copies:
-                copy.wait()
+            out_ref[...] = jnp.dot(
+                row_ref[...], weight_ref[...], preferred_element_type=jnp.float32
+            ).astype(jnp.bfloat16)
 
     if final:
         out_shape = jax.ShapeDtypeStruct((tokens, width), jnp.bfloat16)
@@ -289,8 +280,7 @@
     ]
     if final:
         scratch.append(pltpu.VMEM((2, HEAD_DIM, tokens), jnp.bfloat16))
-        scratch += [pltpu.VMEM((tokens, width), jnp.bfloat16)] * 2
-        scratch.append(pltpu.SemaphoreType.DMA((tokens // LANES,)))
+        scratch.append(pltpu.VMEM((tokens, width), jnp.bfloat16))
     operands = [queries]
     for block, whole in zip(sets, joined):
         operands += [block] if whole else list(block)
@@ -306,7 +296,6 @@
         kernel,
         out_shape=out_shape,
         in_specs=specs,
-        **({"out_specs": pl.BlockSpec(memory_space=pl.ANY)} if final else {}),
         scratch_shapes=scratch,
         compiler_params=pltpu.CompilerParams(
             vmem_limit_bytes=VMEM_BYTES

time: 41.1 us -> 41.1 us (level)
  no operation moved by 1% of the time
where the time goes in v7:
time: 41.1 us; the launch traced here: 40.9 us
  Pallas kernels  18.9 us (46%)
  starting transfers between devices  12.9 us (31%)
  waiting for transfers between devices  7.81 us (19%)
  local copies, waits for them, and re-layouts  1.16 us (3%)
    pallas_call x5, Pallas kernels, attend(): pl.pallas_call(kernel, out_shape=out_shape, in_specs=specs, scratch_shape...  15.7 us
    ppermute x9, starting transfers between devices, across(): lax.ppermute(block, axis, [(i, i ^ flip) for i in range(lax.axis_size(axi...  12.9 us
    ppermute x9, waiting for transfers between devices, across(): lax.ppermute(block, axis, [(i, i ^ flip) for i in range(lax.axis_size(axi...  7.81 us
    pallas_call x1, Pallas kernels, order_rows(): pl.pallas_call(kernel, out_shape=[jax.ShapeDtypeStruct((high - low, 2 * w...  3.08 us
    unnamed x14, local copies, waits for them, and re-layouts  1.16 us
  transfers between devices with their start and end apart: 9, of which 5 were waited for; matrix products, arithmetic and copies ran while one was open for 0% of the time, Pallas kernels for 25%

profile of v7, /device:TPU:0, one launch (start us, length us, event | category | flops | bytes accessed | tf_op | source)
XLA Modules:
  0.0 40.9 jit_solution(10974880589174057595)
XLA Ops:
  0.0 3.1 %shard_map.55 = (bf16[128,1536]{1,0:T(8,128)(2,1)}, bf16[128,1536]{1,0:T(8,128)(2,1)}, bf16[8,1536]{1,0:T(8,128)(2,1)}) custom-call(bf16[256,512]{1,0:T(8,128)(2,1)} %constant.2.clone.select_hbm, bf16[512,768]{1,0:T(8,128)(2,1)} %bitcast.4, bf16[512,768]{1,0:T(8,128)(2,1)} %bitcast.7), custom_call_target="tpu_custom_call" | custom-call | flops 402653184 | bytes 2359296 | tf_op jit(solution)/shard_map/pallas_call | solution.py:84
  3.1 3.0 %collective-permute-start = (bf16[128,1536]{1,0:T(8,128)(2,1)}, bf16[128,1536]{1,0:T(8,128)(2,1)S(1)}, u32[]{:S(2)}, u32[]{:S(2)}) collective-permute-start(bf16[128,1536]{1,0:T(8,128)(2,1)} %get-tuple-element.20.refs_0_), channel_id=1, source_target_pairs={{0,8},{8,0},{16,24},{24,16},{1,9},{9,1},{17,25},{25,17},{2,10},{10... | collective-permute-start | bytes 1179656 | tf_op jit(solution)/shard_map/ppermute | solution.py:24
  6.1 1.5 %collective-permute-start.1 = (bf16[128,1536]{1,0:T(8,128)(2,1)}, bf16[128,1536]{1,0:T(8,128)(2,1)S(1)}, u32[]{:S(2)}, u32[]{:S(2)}) collective-permute-start(bf16[128,1536]{1,0:T(8,128)(2,1)} %get-tuple-element.20.refs_0_), channel_id=1, source_target_pairs={{0,16},{8,24},{16,0},{24,8},{1,17},{9,25},{17,1},{25,9},{2,18},{10... | collective-permute-start | bytes 1179656 | tf_op jit(solution)/shard_map/ppermute | solution.py:24
  7.6 1.6 %collective-permute-start.2 = (bf16[8,1536]{1,0:T(8,128)(2,1)}, bf16[8,1536]{1,0:T(8,128)(2,1)S(1)}, u32[]{:S(2)}, u32[]{:S(2)}) collective-permute-start(bf16[8,1536]{1,0:T(8,128)(2,1)} %get-tuple-element.21.refs_0_), channel_id=1, source_target_pairs={{0,2},{1,3},{2,0},{3,1},{4,6},{5,7},{6,4},{7,5},{8,10},{9,11},{10,... | collective-permute-start | bytes 73736 | tf_op jit(solution)/shard_map/ppermute | solution.py:24
  9.2 0.5 %collective-permute-start.7 = (bf16[128,1536]{1,0:T(8,128)(2,1)}, bf16[128,1536]{1,0:T(8,128)(2,1)S(1)}, u32[]{:S(2)}, u32[]{:S(2)}) collective-permute-start(bf16[128,1536]{1,0:T(8,128)(2,1)} %get-tuple-element.24), channel_id=1, source_target_pairs={{0,8},{8,0},{16,24},{24,16},{1,9},{9,1},{17,25},{25,17},{2,10},{10... | collective-permute-start | bytes 1179656 | tf_op jit(solution)/shard_map/ppermute | solution.py:24
  9.7 1.1 %copy-done.5 = bf16[1,512,768]{2,1,0:T(8,128)(2,1)S(1)} copy-done((bf16[1,512,768]{2,1,0:T(8,128)(2,1)S(1)}, bf16[1,512,768]{2,1,0:T(8,128)(2,1)}, u32[]{:S(2)}) %copy-start.5) | copy-done | bytes 786456
  10.9 2.6 %shard_map.56 = (f32[384,512]{1,0:T(8,128)S(1)}, f32[6,512]{1,0:T(8,128)S(1)}, f32[6,512]{1,0:T(8,128)S(1)}) custom-call(bf16[512,768]{1,0:T(8,128)(2,1)S(1)} %bitcast.10, bf16[512,768]{1,0:T(8,128)(2,1)S(1)} %bitcast.5, bf16[512,768]{1,0:T(8,128)(2,1)S(1)} %bitcast.8), custom_call_target="tpu_custom_call" | custom-call | flops 1610612736 | bytes 1572864 | tf_op jit(solution)/shard_map/pallas_call | solution.py:295
  13.5 2.7 %collective-permute-start.3 = (bf16[16,1536]{1,0:T(8,128)(2,1)S(1)}, bf16[16,1536]{1,0:T(8,128)(2,1)S(1)}, u32[]{:S(2)}, u32[]{:S(2)}) collective-permute-start(bf16[16,1536]{1,0:T(8,128)(2,1)S(1)} %shard_map.57.refs_3_.refs_0_), channel_id=1, source_target_pairs={{0,4},{1,5},{2,6},{3,7},{4,0},{5,1},{6,2},{7,3},{8,12},{9,13},{10,... | collective-permute-start | bytes 147464 | tf_op jit(solution)/shard_map/ppermute | solution.py:24
  16.2 2.6 %shard_map.58 = (f32[384,512]{1,0:T(8,128)S(1)}, f32[6,512]{1,0:T(8,128)S(1)}, f32[6,512]{1,0:T(8,128)S(1)}) custom-call(bf16[512,768]{1,0:T(8,128)(2,1)S(1)} %bitcast.11, bf16[512,768]{1,0:T(8,128)(2,1)S(1)} %bitcast.6, bf16[512,768]{1,0:T(8,128)(2,1)S(1)} %bitcast.9, bf16[16,1536]{1,0:T(8,128)(2,1)S(1)} %shard_map.57.refs_3_.refs_0_), custom_call_target="tpu_custom_call" | custom-call | flops 1610612736 | bytes 1572864 | tf_op jit(solution)/shard_map/pallas_call | solution.py:295
  18.8 0.0 copy-start.6
  18.8 0.2 collective-permute-done.3.refs_1_
  19.0 0.4 collective-permute-start.4
  19.4 2.6 %collective-permute-start.6 = (bf16[32,1536]{1,0:T(8,128)(2,1)S(1)}, bf16[32,1536]{1,0:T(8,128)(2,1)S(1)}, u32[]{:S(2)}, u32[]{:S(2)}) collective-permute-start(bf16[32,1536]{1,0:T(8,128)(2,1)S(1)} %shard_map.59.refs_1_.refs_2_.refs_4_), channel_id=1, source_target_pairs={{0,24},{8,16},{16,8},{24,0},{1,25},{9,17},{17,9},{25,1},{2,26},{10... | collective-permute-start | bytes 294920 | tf_op jit(solution)/shard_map/ppermute | solution.py:24
  22.1 0.5 %collective-permute-start.5 = (bf16[32,1536]{1,0:T(8,128)(2,1)S(1)}, bf16[32,1536]{1,0:T(8,128)(2,1)S(1)}, u32[]{:S(2)}, u32[]{:S(2)}) collective-permute-start(bf16[32,1536]{1,0:T(8,128)(2,1)S(1)} %shard_map.59.refs_1_.refs_2_.refs_4_), channel_id=1, source_target_pairs={{0,8},{8,0},{16,24},{24,16},{1,9},{9,1},{17,25},{25,17},{2,10},{10... | collective-permute-start | bytes 294920 | tf_op jit(solution)/shard_map/ppermute | solution.py:24
  22.6 2.1 %collective-permute-done.7.refs_2_ = bf16[128,1536]{1,0:T(8,128)(2,1)S(1)} collective-permute-done((bf16[128,1536]{1,0:T(8,128)(2,1)}, bf16[128,1536]{1,0:T(8,128)(2,1)S(1)}, u32[]{:S(2)}, u32[]{:S(2)}) %collective-permute-start.7) | collective-permute-done | bytes 393248 | tf_op jit(solution)/shard_map/ppermute | solution.py:24
  24.7 2.9 %shard_map.61 = (f32[768,512]{1,0:T(8,128)S(1)}, f32[12,512]{1,0:T(8,128)S(1)}, f32[12,512]{1,0:T(8,128)S(1)}) custom-call(bf16[512,768]{1,0:T(8,128)(2,1)S(1)} %bitcast.12, bf16[128,1536]{1,0:T(8,128)(2,1)S(1)} %collective-permute-done.refs_0_.refs_1_, bf16[128,1536]{1,0:T(8,128)(2,1)S(1)} %collective-permute-done.7.refs_2_, ...), custom_call_target="tpu_custom_call" | custom-call | flops 2415919104 | bytes 2752512 | tf_op jit(solution)/shard_map/pallas_call | solution.py:295
  27.6 0.7 %collective-permute-done.6.refs_7_.refs_4_ = bf16[32,1536]{1,0:T(8,128)(2,1)S(1)} collective-permute-done((bf16[32,1536]{1,0:T(8,128)(2,1)S(1)}, bf16[32,1536]{1,0:T(8,128)(2,1)S(1)}, u32[]{:S(2)}, u32[]{:S(2)}) %collective-permute-start.6) | collective-permute-done | bytes 98336 | tf_op jit(solution)/shard_map/ppermute | solution.py:24
  28.3 4.3 %collective-permute-done.4.refs_3_.refs_6_.refs_1_ = bf16[160,1536]{1,0:T(8,128)(2,1)S(1)} collective-permute-done((bf16[160,1536]{1,0:T(8,128)(2,1)S(1)}, bf16[160,1536]{1,0:T(8,128)(2,1)S(1)}, u32[]{:S(2)}, u32[]{:S(2)}) %collective-permute-start.4) | collective-permute-done | bytes 491552 | tf_op jit(solution)/shard_map/ppermute | solution.py:24
  32.6 0.1 shard_map.62
  32.7 0.1 collective-permute-start.8
  32.7 0.0 copy-start.4
  32.8 2.3 %shard_map.63 = (f32[768,512]{1,0:T(8,128)S(1)}, f32[12,512]{1,0:T(8,128)S(1)}, f32[12,512]{1,0:T(8,128)S(1)}) custom-call(bf16[512,768]{1,0:T(8,128)(2,1)S(1)} %bitcast.13, bf16[160,1536]{1,0:T(8,128)(2,1)S(1)} %collective-permute-done.4.refs_3_.refs_6_.refs_1_, bf16[32,1536]{1,0:T(8,128)(2,1)S(1)} %shard_map.59.refs_1_.refs_2_.refs_4_, ...), custom_call_target="tpu_custom_call" | custom-call | flops 1610612736 | bytes 2359296 | tf_op jit(solution)/shard_map/pallas_call | solution.py:295
  35.1 0.5 %collective-permute-done.8.refs_1_ = bf16[384,1536]{1,0:T(8,128)(2,1)S(1)} collective-permute-done((bf16[384,1536]{1,0:T(8,128)(2,1)S(1)}, bf16[384,1536]{1,0:T(8,128)(2,1)S(1)}, u32[]{:S(2)}, u32[]{:S(2)}) %collective-permute-start.8) | collective-permute-done | bytes 1179680 | tf_op jit(solution)/shard_map/ppermute | solution.py:24
  35.6 5.3 %shard_map.64 = bf16[512,768]{1,0:T(8,128)(2,1)} custom-call(bf16[512,768]{1,0:T(8,128)(2,1)S(1)} %bitcast.14, bf16[384,1536]{1,0:T(8,128)(2,1)S(1)} %collective-permute-done.8.refs_1_, f32[768,512]{1,0:T(8,128)S(1)} %get-tuple-element.32.refs_2_, f32[12,512]{1,0:T(8,128)S(1)} %get-tuple-element.33.refs_3_, f32[12,512]{1,0:T(8,128)S(1)} %get-tuple-element.34.refs_4_, ...), custom_call_target="tpu_custom_call" | custom-call | flops 2415919104 | bytes 2752512 | tf_op jit(solution)/shard_map/pallas_call | solution.py:295
  (18 shorter events, 0.1 us)
Async XLA Ops:
  0.0 9.7 %copy-start.1 = (bf16[1,512,768]{2,1,0:T(8,128)(2,1)S(1)}, bf16[1,512,768]{2,1,0:T(8,128)(2,1)}, u32[]{:S(2)}) copy-start(bf16[1,512,768]{2,1,0:T(8,128)(2,1)} %param.7) | copy-start | bytes 2359300
  0.0 9.7 %copy-start = (bf16[1,512,768]{2,1,0:T(8,128)(2,1)S(1)}, bf16[1,512,768]{2,1,0:T(8,128)(2,1)}, u32[]{:S(2)}) copy-start(bf16[1,512,768]{2,1,0:T(8,128)(2,1)} %param.6) | copy-start | bytes 2359300
  3.1 15.9 %collective-permute-start = (bf16[128,1536]{1,0:T(8,128)(2,1)}, bf16[128,1536]{1,0:T(8,128)(2,1)S(1)}, u32[]{:S(2)}, u32[]{:S(2)}) collective-permute-start(bf16[128,1536]{1,0:T(8,128)(2,1)} %get-tuple-element.20.refs_0_), channel_id=1, source_target_pairs={{0,8},{8,0},{16,24},{24,16},{1,9},{9,1},{17,25},{25,17},{2,10},{10... | collective-permute-start | bytes 1179656 | tf_op jit(solution)/shard_map/ppermute | solution.py:24
  6.1 18.6 %collective-permute-start.1 = (bf16[128,1536]{1,0:T(8,128)(2,1)}, bf16[128,1536]{1,0:T(8,128)(2,1)S(1)}, u32[]{:S(2)}, u32[]{:S(2)}) collective-permute-start(bf16[128,1536]{1,0:T(8,128)(2,1)} %get-tuple-element.20.refs_0_), channel_id=1, source_target_pairs={{0,16},{8,24},{16,0},{24,8},{1,17},{9,25},{17,1},{25,9},{2,18},{10... | collective-permute-start | bytes 1179656 | tf_op jit(solution)/shard_map/ppermute | solution.py:24
  7.6 5.9 %collective-permute-start.2 = (bf16[8,1536]{1,0:T(8,128)(2,1)}, bf16[8,1536]{1,0:T(8,128)(2,1)S(1)}, u32[]{:S(2)}, u32[]{:S(2)}) collective-permute-start(bf16[8,1536]{1,0:T(8,128)(2,1)} %get-tuple-element.21.refs_0_), channel_id=1, source_target_pairs={{0,2},{1,3},{2,0},{3,1},{4,6},{5,7},{6,4},{7,5},{8,10},{9,11},{10,... | collective-permute-start | bytes 73736 | tf_op jit(solution)/shard_map/ppermute | solution.py:24
  9.2 15.5 %collective-permute-start.7 = (bf16[128,1536]{1,0:T(8,128)(2,1)}, bf16[128,1536]{1,0:T(8,128)(2,1)S(1)}, u32[]{:S(2)}, u32[]{:S(2)}) collective-permute-start(bf16[128,1536]{1,0:T(8,128)(2,1)} %get-tuple-element.24), channel_id=1, source_target_pairs={{0,8},{8,0},{16,24},{24,16},{1,9},{9,1},{17,25},{25,17},{2,10},{10... | collective-permute-start | bytes 1179656 | tf_op jit(solution)/shard_map/ppermute | solution.py:24
  9.7 1.1 %copy-start.5 = (bf16[1,512,768]{2,1,0:T(8,128)(2,1)S(1)}, bf16[1,512,768]{2,1,0:T(8,128)(2,1)}, u32[]{:S(2)}) copy-start(bf16[1,512,768]{2,1,0:T(8,128)(2,1)} %param.5) | copy-start | bytes 2359300
  10.9 2.6 %copy-start.3 = (bf16[8,1536]{1,0:T(8,128)(2,1)S(1)}, bf16[8,1536]{1,0:T(8,128)(2,1)}, u32[]{:S(2)}) copy-start(bf16[8,1536]{1,0:T(8,128)(2,1)} %get-tuple-element.21.refs_0_) | copy-start | bytes 73732
  13.5 5.5 %collective-permute-start.3 = (bf16[16,1536]{1,0:T(8,128)(2,1)S(1)}, bf16[16,1536]{1,0:T(8,128)(2,1)S(1)}, u32[]{:S(2)}, u32[]{:S(2)}) collective-permute-start(bf16[16,1536]{1,0:T(8,128)(2,1)S(1)} %shard_map.57.refs_3_.refs_0_), channel_id=1, source_target_pairs={{0,4},{1,5},{2,6},{3,7},{4,0},{5,1},{6,2},{7,3},{8,12},{9,13},{10,... | collective-permute-start | bytes 147464 | tf_op jit(solution)/shard_map/ppermute | solution.py:24
  18.8 5.9 %copy-start.6 = (bf16[1,512,768]{2,1,0:T(8,128)(2,1)S(1)}, bf16[1,512,768]{2,1,0:T(8,128)(2,1)}, u32[]{:S(2)}) copy-start(bf16[1,512,768]{2,1,0:T(8,128)(2,1)} %param.5) | copy-start | bytes 2359300
  19.0 13.5 %collective-permute-start.4 = (bf16[160,1536]{1,0:T(8,128)(2,1)S(1)}, bf16[160,1536]{1,0:T(8,128)(2,1)S(1)}, u32[]{:S(2)}, u32[]{:S(2)}) collective-permute-start(bf16[160,1536]{1,0:T(8,128)(2,1)S(1)} %shard_map.60), channel_id=1, source_target_pairs={{0,16},{8,24},{16,0},{24,8},{1,17},{9,25},{17,1},{25,9},{2,18},{10... | collective-permute-start | bytes 1474568 | tf_op jit(solution)/shard_map/ppermute | solution.py:24
  19.4 8.9 %collective-permute-start.6 = (bf16[32,1536]{1,0:T(8,128)(2,1)S(1)}, bf16[32,1536]{1,0:T(8,128)(2,1)S(1)}, u32[]{:S(2)}, u32[]{:S(2)}) collective-permute-start(bf16[32,1536]{1,0:T(8,128)(2,1)S(1)} %shard_map.59.refs_1_.refs_2_.refs_4_), channel_id=1, source_target_pairs={{0,24},{8,16},{16,8},{24,0},{1,25},{9,17},{17,9},{25,1},{2,26},{10... | collective-permute-start | bytes 294920 | tf_op jit(solution)/shard_map/ppermute | solution.py:24
  22.1 6.3 %collective-permute-start.5 = (bf16[32,1536]{1,0:T(8,128)(2,1)S(1)}, bf16[32,1536]{1,0:T(8,128)(2,1)S(1)}, u32[]{:S(2)}, u32[]{:S(2)}) collective-permute-start(bf16[32,1536]{1,0:T(8,128)(2,1)S(1)} %shard_map.59.refs_1_.refs_2_.refs_4_), channel_id=1, source_target_pairs={{0,8},{8,0},{16,24},{24,16},{1,9},{9,1},{17,25},{25,17},{2,10},{10... | collective-permute-start | bytes 294920 | tf_op jit(solution)/shard_map/ppermute | solution.py:24
  24.7 7.9 %copy-start.2 = (bf16[128,1536]{1,0:T(8,128)(2,1)S(1)}, bf16[128,1536]{1,0:T(8,128)(2,1)}, u32[]{:S(2)}) copy-start(bf16[128,1536]{1,0:T(8,128)(2,1)} %get-tuple-element.20.refs_0_) | copy-start | bytes 1179652
  32.7 2.9 %collective-permute-start.8 = (bf16[384,1536]{1,0:T(8,128)(2,1)S(1)}, bf16[384,1536]{1,0:T(8,128)(2,1)S(1)}, u32[]{:S(2)}, u32[]{:S(2)}) collective-permute-start(bf16[384,1536]{1,0:T(8,128)(2,1)S(1)} %shard_map.62), channel_id=1, source_target_pairs={{0,1},{1,0},{2,3},{3,2},{4,5},{5,4},{6,7},{7,6},{8,9},{9,8},{10,11... | collective-permute-start | bytes 3538952 | tf_op jit(solution)/shard_map/ppermute | solution.py:24
  32.7 2.8 %copy-start.4 = (bf16[768,768]{1,0:T(8,128)(2,1)S(1)}, bf16[768,768]{1,0:T(8,128)(2,1)}, u32[]{:S(2)}) copy-start(bf16[768,768]{1,0:T(8,128)(2,1)} %refs_5_.1) | copy-start | bytes 3538948

commit v8 on v6

--- a/solution.py
+++ b/solution.py
@@ -260,16 +260,21 @@
                 low, high, state_refs[0 if shared else group] if states else None, 0 if shared else low
             )
         if final:
-            copies = []
-            for at, low in enumerate(range(0, tokens, LANES)):
-                rows = slice(low, low + LANES)
-                result_ref[rows, :] = jnp.dot(
-                    out_ref[rows, :], weight_ref[...], preferred_element_type=jnp.float32
+            copies, step = [], tokens // 2
+            for low in range(0, tokens, step):
+                result_ref[low : low + step, :] = jnp.dot(
+                    out_ref[low : low + step, :],
+                    weight_ref[...],
+                    preferred_element_type=jnp.float32,
                 ).astype(jnp.bfloat16)
-                copies.append(
-                    pltpu.make_async_copy(result_ref.at[rows], out_hbm.at[rows], sems.at[at])
-                )
-                copies[-1].start()
+                for first in range(low, low + step, LANES):
+                    rows = slice(first, first + LANES)
+                    copies.append(
+                        pltpu.make_async_copy(
+                            result_ref.at[rows], out_hbm.at[rows], sems.at[len(copies)]
+                        )
+                    )
+                    copies[-1].start()
             for copy in copies:
                 copy.wait()
 

time: 41.1 us -> 41.1 us (level)
  no operation moved by 1% of the time
where the time goes in v8:
time: 41.1 us; the launch traced here: 41 us
  Pallas kernels  18.8 us (46%)
  starting transfers between devices  12.9 us (31%)
  waiting for transfers between devices  7.81 us (19%)
  local copies, waits for them, and re-layouts  1.16 us (3%)
    pallas_call x5, Pallas kernels, attend(): pl.pallas_call(kernel, out_shape=out_shape, in_specs=specs, **{'out_specs...  15.6 us
    ppermute x9, starting transfers between devices, across(): lax.ppermute(block, axis, [(i, i ^ flip) for i in range(lax.axis_size(axi...  12.9 us
    ppermute x9, waiting for transfers between devices, across(): lax.ppermute(block, axis, [(i, i ^ flip) for i in range(lax.axis_size(axi...  7.81 us
    pallas_call x1, Pallas kernels, order_rows(): pl.pallas_call(kernel, out_shape=[jax.ShapeDtypeStruct((high - low, 2 * w...  3.08 us
    unnamed x14, local copies, waits for them, and re-layouts  1.16 us
  transfers between devices with their start and end apart: 9, of which 5 were waited for; matrix products, arithmetic and copies ran while one was open for 0% of the time, Pallas kernels for 25%

profile of v8, /device:TPU:0, one launch (start us, length us, event | category | flops | bytes accessed | tf_op | source)
XLA Modules:
  0.0 41.0 jit_solution(3771689657918399444)
XLA Ops:
  0.0 3.1 %shard_map.55 = (bf16[128,1536]{1,0:T(8,128)(2,1)}, bf16[128,1536]{1,0:T(8,128)(2,1)}, bf16[8,1536]{1,0:T(8,128)(2,1)}) custom-call(bf16[256,512]{1,0:T(8,128)(2,1)} %constant.2.clone.select_hbm, bf16[512,768]{1,0:T(8,128)(2,1)} %bitcast.4, bf16[512,768]{1,0:T(8,128)(2,1)} %bitcast.7), custom_call_target="tpu_custom_call" | custom-call | flops 402653184 | bytes 2359296 | tf_op jit(solution)/shard_map/pallas_call | solution.py:84
  3.1 3.0 %collective-permute-start = (bf16[128,1536]{1,0:T(8,128)(2,1)}, bf16[128,1536]{1,0:T(8,128)(2,1)S(1)}, u32[]{:S(2)}, u32[]{:S(2)}) collective-permute-start(bf16[128,1536]{1,0:T(8,128)(2,1)} %get-tuple-element.20.refs_0_), channel_id=1, source_target_pairs={{0,8},{8,0},{16,24},{24,16},{1,9},{9,1},{17,25},{25,17},{2,10},{10... | collective-permute-start | bytes 1179656 | tf_op jit(solution)/shard_map/ppermute | solution.py:24
  6.1 1.5 %collective-permute-start.1 = (bf16[128,1536]{1,0:T(8,128)(2,1)}, bf16[128,1536]{1,0:T(8,128)(2,1)S(1)}, u32[]{:S(2)}, u32[]{:S(2)}) collective-permute-start(bf16[128,1536]{1,0:T(8,128)(2,1)} %get-tuple-element.20.refs_0_), channel_id=1, source_target_pairs={{0,16},{8,24},{16,0},{24,8},{1,17},{9,25},{17,1},{25,9},{2,18},{10... | collective-permute-start | bytes 1179656 | tf_op jit(solution)/shard_map/ppermute | solution.py:24
  7.6 1.6 %collective-permute-start.2 = (bf16[8,1536]{1,0:T(8,128)(2,1)}, bf16[8,1536]{1,0:T(8,128)(2,1)S(1)}, u32[]{:S(2)}, u32[]{:S(2)}) collective-permute-start(bf16[8,1536]{1,0:T(8,128)(2,1)} %get-tuple-element.21.refs_0_), channel_id=1, source_target_pairs={{0,2},{1,3},{2,0},{3,1},{4,6},{5,7},{6,4},{7,5},{8,10},{9,11},{10,... | collective-permute-start | bytes 73736 | tf_op jit(solution)/shard_map/ppermute | solution.py:24
  9.2 0.5 %collective-permute-start.7 = (bf16[128,1536]{1,0:T(8,128)(2,1)}, bf16[128,1536]{1,0:T(8,128)(2,1)S(1)}, u32[]{:S(2)}, u32[]{:S(2)}) collective-permute-start(bf16[128,1536]{1,0:T(8,128)(2,1)} %get-tuple-element.24), channel_id=1, source_target_pairs={{0,8},{8,0},{16,24},{24,16},{1,9},{9,1},{17,25},{25,17},{2,10},{10... | collective-permute-start | bytes 1179656 | tf_op jit(solution)/shard_map/ppermute | solution.py:24
  9.7 1.1 %copy-done.5 = bf16[1,512,768]{2,1,0:T(8,128)(2,1)S(1)} copy-done((bf16[1,512,768]{2,1,0:T(8,128)(2,1)S(1)}, bf16[1,512,768]{2,1,0:T(8,128)(2,1)}, u32[]{:S(2)}) %copy-start.5) | copy-done | bytes 786456
  10.9 2.6 %shard_map.56 = (f32[384,512]{1,0:T(8,128)S(1)}, f32[6,512]{1,0:T(8,128)S(1)}, f32[6,512]{1,0:T(8,128)S(1)}) custom-call(bf16[512,768]{1,0:T(8,128)(2,1)S(1)} %bitcast.10, bf16[512,768]{1,0:T(8,128)(2,1)S(1)} %bitcast.5, bf16[512,768]{1,0:T(8,128)(2,1)S(1)} %bitcast.8), custom_call_target="tpu_custom_call" | custom-call | flops 1610612736 | bytes 1572864 | tf_op jit(solution)/shard_map/pallas_call | solution.py:310
  13.5 2.7 %collective-permute-start.3 = (bf16[16,1536]{1,0:T(8,128)(2,1)S(1)}, bf16[16,1536]{1,0:T(8,128)(2,1)S(1)}, u32[]{:S(2)}, u32[]{:S(2)}) collective-permute-start(bf16[16,1536]{1,0:T(8,128)(2,1)S(1)} %shard_map.57.refs_3_.refs_0_), channel_id=1, source_target_pairs={{0,4},{1,5},{2,6},{3,7},{4,0},{5,1},{6,2},{7,3},{8,12},{9,13},{10,... | collective-permute-start | bytes 147464 | tf_op jit(solution)/shard_map/ppermute | solution.py:24
  16.2 2.6 %shard_map.58 = (f32[384,512]{1,0:T(8,128)S(1)}, f32[6,512]{1,0:T(8,128)S(1)}, f32[6,512]{1,0:T(8,128)S(1)}) custom-call(bf16[512,768]{1,0:T(8,128)(2,1)S(1)} %bitcast.11, bf16[512,768]{1,0:T(8,128)(2,1)S(1)} %bitcast.6, bf16[512,768]{1,0:T(8,128)(2,1)S(1)} %bitcast.9, bf16[16,1536]{1,0:T(8,128)(2,1)S(1)} %shard_map.57.refs_3_.refs_0_), custom_call_target="tpu_custom_call" | custom-call | flops 1610612736 | bytes 1572864 | tf_op jit(solution)/shard_map/pallas_call | solution.py:310
  18.8 0.0 copy-start.6
  18.8 0.2 collective-permute-done.3.refs_1_
  19.0 0.4 collective-permute-start.4
  19.4 2.6 %collective-permute-start.6 = (bf16[32,1536]{1,0:T(8,128)(2,1)S(1)}, bf16[32,1536]{1,0:T(8,128)(2,1)S(1)}, u32[]{:S(2)}, u32[]{:S(2)}) collective-permute-start(bf16[32,1536]{1,0:T(8,128)(2,1)S(1)} %shard_map.59.refs_1_.refs_2_.refs_4_), channel_id=1, source_target_pairs={{0,24},{8,16},{16,8},{24,0},{1,25},{9,17},{17,9},{25,1},{2,26},{10... | collective-permute-start | bytes 294920 | tf_op jit(solution)/shard_map/ppermute | solution.py:24
  22.1 0.5 %collective-permute-start.5 = (bf16[32,1536]{1,0:T(8,128)(2,1)S(1)}, bf16[32,1536]{1,0:T(8,128)(2,1)S(1)}, u32[]{:S(2)}, u32[]{:S(2)}) collective-permute-start(bf16[32,1536]{1,0:T(8,128)(2,1)S(1)} %shard_map.59.refs_1_.refs_2_.refs_4_), channel_id=1, source_target_pairs={{0,8},{8,0},{16,24},{24,16},{1,9},{9,1},{17,25},{25,17},{2,10},{10... | collective-permute-start | bytes 294920 | tf_op jit(solution)/shard_map/ppermute | solution.py:24
  22.6 2.1 %collective-permute-done.7.refs_2_ = bf16[128,1536]{1,0:T(8,128)(2,1)S(1)} collective-permute-done((bf16[128,1536]{1,0:T(8,128)(2,1)}, bf16[128,1536]{1,0:T(8,128)(2,1)S(1)}, u32[]{:S(2)}, u32[]{:S(2)}) %collective-permute-start.7) | collective-permute-done | bytes 393248 | tf_op jit(solution)/shard_map/ppermute | solution.py:24
  24.7 2.9 %shard_map.61 = (f32[768,512]{1,0:T(8,128)S(1)}, f32[12,512]{1,0:T(8,128)S(1)}, f32[12,512]{1,0:T(8,128)S(1)}) custom-call(bf16[512,768]{1,0:T(8,128)(2,1)S(1)} %bitcast.12, bf16[128,1536]{1,0:T(8,128)(2,1)S(1)} %collective-permute-done.refs_0_.refs_1_, bf16[128,1536]{1,0:T(8,128)(2,1)S(1)} %collective-permute-done.7.refs_2_, ...), custom_call_target="tpu_custom_call" | custom-call | flops 2415919104 | bytes 2752512 | tf_op jit(solution)/shard_map/pallas_call | solution.py:310
  27.6 0.7 %collective-permute-done.6.refs_7_.refs_4_ = bf16[32,1536]{1,0:T(8,128)(2,1)S(1)} collective-permute-done((bf16[32,1536]{1,0:T(8,128)(2,1)S(1)}, bf16[32,1536]{1,0:T(8,128)(2,1)S(1)}, u32[]{:S(2)}, u32[]{:S(2)}) %collective-permute-start.6) | collective-permute-done | bytes 98336 | tf_op jit(solution)/shard_map/ppermute | solution.py:24
  28.3 4.3 %collective-permute-done.4.refs_3_.refs_6_.refs_1_ = bf16[160,1536]{1,0:T(8,128)(2,1)S(1)} collective-permute-done((bf16[160,1536]{1,0:T(8,128)(2,1)S(1)}, bf16[160,1536]{1,0:T(8,128)(2,1)S(1)}, u32[]{:S(2)}, u32[]{:S(2)}) %collective-permute-start.4) | collective-permute-done | bytes 491552 | tf_op jit(solution)/shard_map/ppermute | solution.py:24
  32.6 0.1 shard_map.62
  32.7 0.1 collective-permute-start.8
  32.7 0.0 copy-start.4
  32.8 2.3 %shard_map.63 = (f32[768,512]{1,0:T(8,128)S(1)}, f32[12,512]{1,0:T(8,128)S(1)}, f32[12,512]{1,0:T(8,128)S(1)}) custom-call(bf16[512,768]{1,0:T(8,128)(2,1)S(1)} %bitcast.13, bf16[160,1536]{1,0:T(8,128)(2,1)S(1)} %collective-permute-done.4.refs_3_.refs_6_.refs_1_, bf16[32,1536]{1,0:T(8,128)(2,1)S(1)} %shard_map.59.refs_1_.refs_2_.refs_4_, ...), custom_call_target="tpu_custom_call" | custom-call | flops 1610612736 | bytes 2359296 | tf_op jit(solution)/shard_map/pallas_call | solution.py:310
  35.1 0.5 %collective-permute-done.8.refs_1_ = bf16[384,1536]{1,0:T(8,128)(2,1)S(1)} collective-permute-done((bf16[384,1536]{1,0:T(8,128)(2,1)S(1)}, bf16[384,1536]{1,0:T(8,128)(2,1)S(1)}, u32[]{:S(2)}, u32[]{:S(2)}) %collective-permute-start.8) | collective-permute-done | bytes 1179680 | tf_op jit(solution)/shard_map/ppermute | solution.py:24
  35.6 5.2 %shard_map.64 = bf16[512,768]{1,0:T(8,128)(2,1)} custom-call(bf16[512,768]{1,0:T(8,128)(2,1)S(1)} %bitcast.14, bf16[384,1536]{1,0:T(8,128)(2,1)S(1)} %collective-permute-done.8.refs_1_, f32[768,512]{1,0:T(8,128)S(1)} %get-tuple-element.32.refs_2_, f32[12,512]{1,0:T(8,128)S(1)} %get-tuple-element.33.refs_3_, f32[12,512]{1,0:T(8,128)S(1)} %get-tuple-element.34.refs_4_, ...), custom_call_target="tpu_custom_call" | custom-call | flops 2415919104 | bytes 2752512 | tf_op jit(solution)/shard_map/pallas_call | solution.py:310
  (18 shorter events, 0.1 us)
Async XLA Ops:
  0.0 9.7 %copy-start.1 = (bf16[1,512,768]{2,1,0:T(8,128)(2,1)S(1)}, bf16[1,512,768]{2,1,0:T(8,128)(2,1)}, u32[]{:S(2)}) copy-start(bf16[1,512,768]{2,1,0:T(8,128)(2,1)} %param.7) | copy-start | bytes 2359300
  0.0 9.7 %copy-start = (bf16[1,512,768]{2,1,0:T(8,128)(2,1)S(1)}, bf16[1,512,768]{2,1,0:T(8,128)(2,1)}, u32[]{:S(2)}) copy-start(bf16[1,512,768]{2,1,0:T(8,128)(2,1)} %param.6) | copy-start | bytes 2359300
  3.1 15.9 %collective-permute-start = (bf16[128,1536]{1,0:T(8,128)(2,1)}, bf16[128,1536]{1,0:T(8,128)(2,1)S(1)}, u32[]{:S(2)}, u32[]{:S(2)}) collective-permute-start(bf16[128,1536]{1,0:T(8,128)(2,1)} %get-tuple-element.20.refs_0_), channel_id=1, source_target_pairs={{0,8},{8,0},{16,24},{24,16},{1,9},{9,1},{17,25},{25,17},{2,10},{10... | collective-permute-start | bytes 1179656 | tf_op jit(solution)/shard_map/ppermute | solution.py:24
  6.1 18.6 %collective-permute-start.1 = (bf16[128,1536]{1,0:T(8,128)(2,1)}, bf16[128,1536]{1,0:T(8,128)(2,1)S(1)}, u32[]{:S(2)}, u32[]{:S(2)}) collective-permute-start(bf16[128,1536]{1,0:T(8,128)(2,1)} %get-tuple-element.20.refs_0_), channel_id=1, source_target_pairs={{0,16},{8,24},{16,0},{24,8},{1,17},{9,25},{17,1},{25,9},{2,18},{10... | collective-permute-start | bytes 1179656 | tf_op jit(solution)/shard_map/ppermute | solution.py:24
  7.6 5.9 %collective-permute-start.2 = (bf16[8,1536]{1,0:T(8,128)(2,1)}, bf16[8,1536]{1,0:T(8,128)(2,1)S(1)}, u32[]{:S(2)}, u32[]{:S(2)}) collective-permute-start(bf16[8,1536]{1,0:T(8,128)(2,1)} %get-tuple-element.21.refs_0_), channel_id=1, source_target_pairs={{0,2},{1,3},{2,0},{3,1},{4,6},{5,7},{6,4},{7,5},{8,10},{9,11},{10,... | collective-permute-start | bytes 73736 | tf_op jit(solution)/shard_map/ppermute | solution.py:24
  9.2 15.5 %collective-permute-start.7 = (bf16[128,1536]{1,0:T(8,128)(2,1)}, bf16[128,1536]{1,0:T(8,128)(2,1)S(1)}, u32[]{:S(2)}, u32[]{:S(2)}) collective-permute-start(bf16[128,1536]{1,0:T(8,128)(2,1)} %get-tuple-element.24), channel_id=1, source_target_pairs={{0,8},{8,0},{16,24},{24,16},{1,9},{9,1},{17,25},{25,17},{2,10},{10... | collective-permute-start | bytes 1179656 | tf_op jit(solution)/shard_map/ppermute | solution.py:24
  9.7 1.1 %copy-start.5 = (bf16[1,512,768]{2,1,0:T(8,128)(2,1)S(1)}, bf16[1,512,768]{2,1,0:T(8,128)(2,1)}, u32[]{:S(2)}) copy-start(bf16[1,512,768]{2,1,0:T(8,128)(2,1)} %param.5) | copy-start | bytes 2359300
  10.9 2.6 %copy-start.3 = (bf16[8,1536]{1,0:T(8,128)(2,1)S(1)}, bf16[8,1536]{1,0:T(8,128)(2,1)}, u32[]{:S(2)}) copy-start(bf16[8,1536]{1,0:T(8,128)(2,1)} %get-tuple-element.21.refs_0_) | copy-start | bytes 73732
  13.5 5.5 %collective-permute-start.3 = (bf16[16,1536]{1,0:T(8,128)(2,1)S(1)}, bf16[16,1536]{1,0:T(8,128)(2,1)S(1)}, u32[]{:S(2)}, u32[]{:S(2)}) collective-permute-start(bf16[16,1536]{1,0:T(8,128)(2,1)S(1)} %shard_map.57.refs_3_.refs_0_), channel_id=1, source_target_pairs={{0,4},{1,5},{2,6},{3,7},{4,0},{5,1},{6,2},{7,3},{8,12},{9,13},{10,... | collective-permute-start | bytes 147464 | tf_op jit(solution)/shard_map/ppermute | solution.py:24
  18.8 5.9 %copy-start.6 = (bf16[1,512,768]{2,1,0:T(8,128)(2,1)S(1)}, bf16[1,512,768]{2,1,0:T(8,128)(2,1)}, u32[]{:S(2)}) copy-start(bf16[1,512,768]{2,1,0:T(8,128)(2,1)} %param.5) | copy-start | bytes 2359300
  19.0 13.5 %collective-permute-start.4 = (bf16[160,1536]{1,0:T(8,128)(2,1)S(1)}, bf16[160,1536]{1,0:T(8,128)(2,1)S(1)}, u32[]{:S(2)}, u32[]{:S(2)}) collective-permute-start(bf16[160,1536]{1,0:T(8,128)(2,1)S(1)} %shard_map.60), channel_id=1, source_target_pairs={{0,16},{8,24},{16,0},{24,8},{1,17},{9,25},{17,1},{25,9},{2,18},{10... | collective-permute-start | bytes 1474568 | tf_op jit(solution)/shard_map/ppermute | solution.py:24
  19.4 8.9 %collective-permute-start.6 = (bf16[32,1536]{1,0:T(8,128)(2,1)S(1)}, bf16[32,1536]{1,0:T(8,128)(2,1)S(1)}, u32[]{:S(2)}, u32[]{:S(2)}) collective-permute-start(bf16[32,1536]{1,0:T(8,128)(2,1)S(1)} %shard_map.59.refs_1_.refs_2_.refs_4_), channel_id=1, source_target_pairs={{0,24},{8,16},{16,8},{24,0},{1,25},{9,17},{17,9},{25,1},{2,26},{10... | collective-permute-start | bytes 294920 | tf_op jit(solution)/shard_map/ppermute | solution.py:24
  22.1 6.3 %collective-permute-start.5 = (bf16[32,1536]{1,0:T(8,128)(2,1)S(1)}, bf16[32,1536]{1,0:T(8,128)(2,1)S(1)}, u32[]{:S(2)}, u32[]{:S(2)}) collective-permute-start(bf16[32,1536]{1,0:T(8,128)(2,1)S(1)} %shard_map.59.refs_1_.refs_2_.refs_4_), channel_id=1, source_target_pairs={{0,8},{8,0},{16,24},{24,16},{1,9},{9,1},{17,25},{25,17},{2,10},{10... | collective-permute-start | bytes 294920 | tf_op jit(solution)/shard_map/ppermute | solution.py:24
  24.7 7.9 %copy-start.2 = (bf16[128,1536]{1,0:T(8,128)(2,1)S(1)}, bf16[128,1536]{1,0:T(8,128)(2,1)}, u32[]{:S(2)}) copy-start(bf16[128,1536]{1,0:T(8,128)(2,1)} %get-tuple-element.20.refs_0_) | copy-start | bytes 1179652
  32.7 2.9 %collective-permute-start.8 = (bf16[384,1536]{1,0:T(8,128)(2,1)S(1)}, bf16[384,1536]{1,0:T(8,128)(2,1)S(1)}, u32[]{:S(2)}, u32[]{:S(2)}) collective-permute-start(bf16[384,1536]{1,0:T(8,128)(2,1)S(1)} %shard_map.62), channel_id=1, source_target_pairs={{0,1},{1,0},{2,3},{3,2},{4,5},{5,4},{6,7},{7,6},{8,9},{9,8},{10,11... | collective-permute-start | bytes 3538952 | tf_op jit(solution)/shard_map/ppermute | solution.py:24
  32.7 2.8 %copy-start.4 = (bf16[768,768]{1,0:T(8,128)(2,1)S(1)}, bf16[768,768]{1,0:T(8,128)(2,1)}, u32[]{:S(2)}) copy-start(bf16[768,768]{1,0:T(8,128)(2,1)} %refs_5_.1) | copy-start | bytes 3538948

commit v9 on v8

--- a/solution.py
+++ b/solution.py
@@ -11,7 +11,7 @@
 HEAD_DIM = 64
 GSTEP = 64
 PAIR = 2 * HEAD_DIM
-CHUNK = 256
+CHUNK = 512
 KEY_CHUNK = 512
 LANES = 128
 LOG2E = math.log2(math.e)

time: 41.1 us -> 41 us (level)
  transfers between devices with their start and end apart: 9 -> 9, of which waited for: 5 -> 5; matrix products, arithmetic and copies ran while one was open for 0% -> 0% of each run, Pallas kernels for 25% -> 26%
where the time goes in v9:
time: 41 us; the launch traced here: 40.8 us
  Pallas kernels  18.7 us (46%)
  starting transfers between devices  12.9 us (31%)
  waiting for transfers between devices  7.72 us (19%)
  local copies, waits for them, and re-layouts  1.16 us (3%)
    pallas_call x5, Pallas kernels, attend(): pl.pallas_call(kernel, out_shape=out_shape, in_specs=specs, **{'out_specs...  15.5 us
    ppermute x9, starting transfers between devices, across(): lax.ppermute(block, axis, [(i, i ^ flip) for i in range(lax.axis_size(axi...  12.9 us
    ppermute x9, waiting for transfers between devices, across(): lax.ppermute(block, axis, [(i, i ^ flip) for i in range(lax.axis_size(axi...  7.72 us
    pallas_call x1, Pallas kernels, order_rows(): pl.pallas_call(kernel, out_shape=[jax.ShapeDtypeStruct((high - low, 2 * w...  3.08 us
    unnamed x14, local copies, waits for them, and re-layouts  1.16 us
  transfers between devices with their start and end apart: 9, of which 5 were waited for; matrix products, arithmetic and copies ran while one was open for 0% of the time, Pallas kernels for 26%

profile of v9, /device:TPU:0, one launch (start us, length us, event | category | flops | bytes accessed | tf_op | source)
XLA Modules:
  0.0 40.8 jit_solution(2540023429705698106)
XLA Ops:
  0.0 3.1 %shard_map.55 = (bf16[128,1536]{1,0:T(8,128)(2,1)}, bf16[128,1536]{1,0:T(8,128)(2,1)}, bf16[8,1536]{1,0:T(8,128)(2,1)}) custom-call(bf16[256,512]{1,0:T(8,128)(2,1)} %constant.2.clone.select_hbm, bf16[512,768]{1,0:T(8,128)(2,1)} %bitcast.4, bf16[512,768]{1,0:T(8,128)(2,1)} %bitcast.7), custom_call_target="tpu_custom_call" | custom-call | flops 402653184 | bytes 2359296 | tf_op jit(solution)/shard_map/pallas_call | solution.py:84
  3.1 3.0 %collective-permute-start = (bf16[128,1536]{1,0:T(8,128)(2,1)}, bf16[128,1536]{1,0:T(8,128)(2,1)S(1)}, u32[]{:S(2)}, u32[]{:S(2)}) collective-permute-start(bf16[128,1536]{1,0:T(8,128)(2,1)} %get-tuple-element.20.refs_0_), channel_id=1, source_target_pairs={{0,8},{8,0},{16,24},{24,16},{1,9},{9,1},{17,25},{25,17},{2,10},{10... | collective-permute-start | bytes 1179656 | tf_op jit(solution)/shard_map/ppermute | solution.py:24
  6.1 1.5 %collective-permute-start.1 = (bf16[128,1536]{1,0:T(8,128)(2,1)}, bf16[128,1536]{1,0:T(8,128)(2,1)S(1)}, u32[]{:S(2)}, u32[]{:S(2)}) collective-permute-start(bf16[128,1536]{1,0:T(8,128)(2,1)} %get-tuple-element.20.refs_0_), channel_id=1, source_target_pairs={{0,16},{8,24},{16,0},{24,8},{1,17},{9,25},{17,1},{25,9},{2,18},{10... | collective-permute-start | bytes 1179656 | tf_op jit(solution)/shard_map/ppermute | solution.py:24
  7.6 1.6 %collective-permute-start.2 = (bf16[8,1536]{1,0:T(8,128)(2,1)}, bf16[8,1536]{1,0:T(8,128)(2,1)S(1)}, u32[]{:S(2)}, u32[]{:S(2)}) collective-permute-start(bf16[8,1536]{1,0:T(8,128)(2,1)} %get-tuple-element.21.refs_0_), channel_id=1, source_target_pairs={{0,2},{1,3},{2,0},{3,1},{4,6},{5,7},{6,4},{7,5},{8,10},{9,11},{10,... | collective-permute-start | bytes 73736 | tf_op jit(solution)/shard_map/ppermute | solution.py:24
  9.2 0.5 %collective-permute-start.7 = (bf16[128,1536]{1,0:T(8,128)(2,1)}, bf16[128,1536]{1,0:T(8,128)(2,1)S(1)}, u32[]{:S(2)}, u32[]{:S(2)}) collective-permute-start(bf16[128,1536]{1,0:T(8,128)(2,1)} %get-tuple-element.24), channel_id=1, source_target_pairs={{0,8},{8,0},{16,24},{24,16},{1,9},{9,1},{17,25},{25,17},{2,10},{10... | collective-permute-start | bytes 1179656 | tf_op jit(solution)/shard_map/ppermute | solution.py:24
  9.7 1.1 %copy-done.5 = bf16[1,512,768]{2,1,0:T(8,128)(2,1)S(1)} copy-done((bf16[1,512,768]{2,1,0:T(8,128)(2,1)S(1)}, bf16[1,512,768]{2,1,0:T(8,128)(2,1)}, u32[]{:S(2)}) %copy-start.5) | copy-done | bytes 786456
  10.9 2.6 %shard_map.56 = (f32[384,512]{1,0:T(8,128)S(1)}, f32[6,512]{1,0:T(8,128)S(1)}, f32[6,512]{1,0:T(8,128)S(1)}) custom-call(bf16[512,768]{1,0:T(8,128)(2,1)S(1)} %bitcast.10, bf16[512,768]{1,0:T(8,128)(2,1)S(1)} %bitcast.5, bf16[512,768]{1,0:T(8,128)(2,1)S(1)} %bitcast.8), custom_call_target="tpu_custom_call" | custom-call | flops 1610612736 | bytes 1572864 | tf_op jit(solution)/shard_map/pallas_call | solution.py:310
  13.5 2.7 %collective-permute-start.3 = (bf16[16,1536]{1,0:T(8,128)(2,1)S(1)}, bf16[16,1536]{1,0:T(8,128)(2,1)S(1)}, u32[]{:S(2)}, u32[]{:S(2)}) collective-permute-start(bf16[16,1536]{1,0:T(8,128)(2,1)S(1)} %shard_map.57.refs_3_.refs_0_), channel_id=1, source_target_pairs={{0,4},{1,5},{2,6},{3,7},{4,0},{5,1},{6,2},{7,3},{8,12},{9,13},{10,... | collective-permute-start | bytes 147464 | tf_op jit(solution)/shard_map/ppermute | solution.py:24
  16.2 2.6 %shard_map.58 = (f32[384,512]{1,0:T(8,128)S(1)}, f32[6,512]{1,0:T(8,128)S(1)}, f32[6,512]{1,0:T(8,128)S(1)}) custom-call(bf16[512,768]{1,0:T(8,128)(2,1)S(1)} %bitcast.11, bf16[512,768]{1,0:T(8,128)(2,1)S(1)} %bitcast.6, bf16[512,768]{1,0:T(8,128)(2,1)S(1)} %bitcast.9, bf16[16,1536]{1,0:T(8,128)(2,1)S(1)} %shard_map.57.refs_3_.refs_0_), custom_call_target="tpu_custom_call" | custom-call | flops 1610612736 | bytes 1572864 | tf_op jit(solution)/shard_map/pallas_call | solution.py:310
  18.8 0.0 copy-start.6
  18.8 0.2 collective-permute-done.3.refs_1_
  19.0 0.4 collective-permute-start.4
  19.4 2.6 %collective-permute-start.6 = (bf16[32,1536]{1,0:T(8,128)(2,1)S(1)}, bf16[32,1536]{1,0:T(8,128)(2,1)S(1)}, u32[]{:S(2)}, u32[]{:S(2)}) collective-permute-start(bf16[32,1536]{1,0:T(8,128)(2,1)S(1)} %shard_map.59.refs_1_.refs_2_.refs_4_), channel_id=1, source_target_pairs={{0,24},{8,16},{16,8},{24,0},{1,25},{9,17},{17,9},{25,1},{2,26},{10... | collective-permute-start | bytes 294920 | tf_op jit(solution)/shard_map/ppermute | solution.py:24
  22.1 0.5 %collective-permute-start.5 = (bf16[32,1536]{1,0:T(8,128)(2,1)S(1)}, bf16[32,1536]{1,0:T(8,128)(2,1)S(1)}, u32[]{:S(2)}, u32[]{:S(2)}) collective-permute-start(bf16[32,1536]{1,0:T(8,128)(2,1)S(1)} %shard_map.59.refs_1_.refs_2_.refs_4_), channel_id=1, source_target_pairs={{0,8},{8,0},{16,24},{24,16},{1,9},{9,1},{17,25},{25,17},{2,10},{10... | collective-permute-start | bytes 294920 | tf_op jit(solution)/shard_map/ppermute | solution.py:24
  22.6 2.1 %collective-permute-done.7.refs_2_ = bf16[128,1536]{1,0:T(8,128)(2,1)S(1)} collective-permute-done((bf16[128,1536]{1,0:T(8,128)(2,1)}, bf16[128,1536]{1,0:T(8,128)(2,1)S(1)}, u32[]{:S(2)}, u32[]{:S(2)}) %collective-permute-start.7) | collective-permute-done | bytes 393248 | tf_op jit(solution)/shard_map/ppermute | solution.py:24
  24.7 3.0 %shard_map.61 = (f32[768,512]{1,0:T(8,128)S(1)}, f32[12,512]{1,0:T(8,128)S(1)}, f32[12,512]{1,0:T(8,128)S(1)}) custom-call(bf16[512,768]{1,0:T(8,128)(2,1)S(1)} %bitcast.12, bf16[128,1536]{1,0:T(8,128)(2,1)S(1)} %collective-permute-done.refs_0_.refs_1_, bf16[128,1536]{1,0:T(8,128)(2,1)S(1)} %collective-permute-done.7.refs_2_, ...), custom_call_target="tpu_custom_call" | custom-call | flops 2415919104 | bytes 2752512 | tf_op jit(solution)/shard_map/pallas_call | solution.py:310
  27.7 0.6 %collective-permute-done.6.refs_7_.refs_4_ = bf16[32,1536]{1,0:T(8,128)(2,1)S(1)} collective-permute-done((bf16[32,1536]{1,0:T(8,128)(2,1)S(1)}, bf16[32,1536]{1,0:T(8,128)(2,1)S(1)}, u32[]{:S(2)}, u32[]{:S(2)}) %collective-permute-start.6) | collective-permute-done | bytes 98336 | tf_op jit(solution)/shard_map/ppermute | solution.py:24
  28.3 4.3 %collective-permute-done.4.refs_3_.refs_6_.refs_1_ = bf16[160,1536]{1,0:T(8,128)(2,1)S(1)} collective-permute-done((bf16[160,1536]{1,0:T(8,128)(2,1)S(1)}, bf16[160,1536]{1,0:T(8,128)(2,1)S(1)}, u32[]{:S(2)}, u32[]{:S(2)}) %collective-permute-start.4) | collective-permute-done | bytes 491552 | tf_op jit(solution)/shard_map/ppermute | solution.py:24
  32.6 0.1 shard_map.62
  32.7 0.1 collective-permute-start.8
  32.8 0.0 copy-start.4
  32.8 2.3 %shard_map.63 = (f32[768,512]{1,0:T(8,128)S(1)}, f32[12,512]{1,0:T(8,128)S(1)}, f32[12,512]{1,0:T(8,128)S(1)}) custom-call(bf16[512,768]{1,0:T(8,128)(2,1)S(1)} %bitcast.13, bf16[160,1536]{1,0:T(8,128)(2,1)S(1)} %collective-permute-done.4.refs_3_.refs_6_.refs_1_, bf16[32,1536]{1,0:T(8,128)(2,1)S(1)} %shard_map.59.refs_1_.refs_2_.refs_4_, ...), custom_call_target="tpu_custom_call" | custom-call | flops 1610612736 | bytes 2359296 | tf_op jit(solution)/shard_map/pallas_call | solution.py:310
  35.1 0.5 %collective-permute-done.8.refs_1_ = bf16[384,1536]{1,0:T(8,128)(2,1)S(1)} collective-permute-done((bf16[384,1536]{1,0:T(8,128)(2,1)S(1)}, bf16[384,1536]{1,0:T(8,128)(2,1)S(1)}, u32[]{:S(2)}, u32[]{:S(2)}) %collective-permute-start.8) | collective-permute-done | bytes 1179680 | tf_op jit(solution)/shard_map/ppermute | solution.py:24
  35.6 5.1 %shard_map.64 = bf16[512,768]{1,0:T(8,128)(2,1)} custom-call(bf16[512,768]{1,0:T(8,128)(2,1)S(1)} %bitcast.14, bf16[384,1536]{1,0:T(8,128)(2,1)S(1)} %collective-permute-done.8.refs_1_, f32[768,512]{1,0:T(8,128)S(1)} %get-tuple-element.32.refs_2_, f32[12,512]{1,0:T(8,128)S(1)} %get-tuple-element.33.refs_3_, f32[12,512]{1,0:T(8,128)S(1)} %get-tuple-element.34.refs_4_, ...), custom_call_target="tpu_custom_call" | custom-call | flops 2415919104 | bytes 2752512 | tf_op jit(solution)/shard_map/pallas_call | solution.py:310
  (18 shorter events, 0.1 us)
Async XLA Ops:
  0.0 9.7 %copy-start.1 = (bf16[1,512,768]{2,1,0:T(8,128)(2,1)S(1)}, bf16[1,512,768]{2,1,0:T(8,128)(2,1)}, u32[]{:S(2)}) copy-start(bf16[1,512,768]{2,1,0:T(8,128)(2,1)} %param.7) | copy-start | bytes 2359300
  0.0 9.7 %copy-start = (bf16[1,512,768]{2,1,0:T(8,128)(2,1)S(1)}, bf16[1,512,768]{2,1,0:T(8,128)(2,1)}, u32[]{:S(2)}) copy-start(bf16[1,512,768]{2,1,0:T(8,128)(2,1)} %param.6) | copy-start | bytes 2359300
  3.1 15.9 %collective-permute-start = (bf16[128,1536]{1,0:T(8,128)(2,1)}, bf16[128,1536]{1,0:T(8,128)(2,1)S(1)}, u32[]{:S(2)}, u32[]{:S(2)}) collective-permute-start(bf16[128,1536]{1,0:T(8,128)(2,1)} %get-tuple-element.20.refs_0_), channel_id=1, source_target_pairs={{0,8},{8,0},{16,24},{24,16},{1,9},{9,1},{17,25},{25,17},{2,10},{10... | collective-permute-start | bytes 1179656 | tf_op jit(solution)/shard_map/ppermute | solution.py:24
  6.1 18.6 %collective-permute-start.1 = (bf16[128,1536]{1,0:T(8,128)(2,1)}, bf16[128,1536]{1,0:T(8,128)(2,1)S(1)}, u32[]{:S(2)}, u32[]{:S(2)}) collective-permute-start(bf16[128,1536]{1,0:T(8,128)(2,1)} %get-tuple-element.20.refs_0_), channel_id=1, source_target_pairs={{0,16},{8,24},{16,0},{24,8},{1,17},{9,25},{17,1},{25,9},{2,18},{10... | collective-permute-start | bytes 1179656 | tf_op jit(solution)/shard_map/ppermute | solution.py:24
  7.6 5.9 %collective-permute-start.2 = (bf16[8,1536]{1,0:T(8,128)(2,1)}, bf16[8,1536]{1,0:T(8,128)(2,1)S(1)}, u32[]{:S(2)}, u32[]{:S(2)}) collective-permute-start(bf16[8,1536]{1,0:T(8,128)(2,1)} %get-tuple-element.21.refs_0_), channel_id=1, source_target_pairs={{0,2},{1,3},{2,0},{3,1},{4,6},{5,7},{6,4},{7,5},{8,10},{9,11},{10,... | collective-permute-start | bytes 73736 | tf_op jit(solution)/shard_map/ppermute | solution.py:24
  9.2 15.5 %collective-permute-start.7 = (bf16[128,1536]{1,0:T(8,128)(2,1)}, bf16[128,1536]{1,0:T(8,128)(2,1)S(1)}, u32[]{:S(2)}, u32[]{:S(2)}) collective-permute-start(bf16[128,1536]{1,0:T(8,128)(2,1)} %get-tuple-element.24), channel_id=1, source_target_pairs={{0,8},{8,0},{16,24},{24,16},{1,9},{9,1},{17,25},{25,17},{2,10},{10... | collective-permute-start | bytes 1179656 | tf_op jit(solution)/shard_map/ppermute | solution.py:24
  9.7 1.1 %copy-start.5 = (bf16[1,512,768]{2,1,0:T(8,128)(2,1)S(1)}, bf16[1,512,768]{2,1,0:T(8,128)(2,1)}, u32[]{:S(2)}) copy-start(bf16[1,512,768]{2,1,0:T(8,128)(2,1)} %param.5) | copy-start | bytes 2359300
  10.9 2.6 %copy-start.3 = (bf16[8,1536]{1,0:T(8,128)(2,1)S(1)}, bf16[8,1536]{1,0:T(8,128)(2,1)}, u32[]{:S(2)}) copy-start(bf16[8,1536]{1,0:T(8,128)(2,1)} %get-tuple-element.21.refs_0_) | copy-start | bytes 73732
  13.5 5.5 %collective-permute-start.3 = (bf16[16,1536]{1,0:T(8,128)(2,1)S(1)}, bf16[16,1536]{1,0:T(8,128)(2,1)S(1)}, u32[]{:S(2)}, u32[]{:S(2)}) collective-permute-start(bf16[16,1536]{1,0:T(8,128)(2,1)S(1)} %shard_map.57.refs_3_.refs_0_), channel_id=1, source_target_pairs={{0,4},{1,5},{2,6},{3,7},{4,0},{5,1},{6,2},{7,3},{8,12},{9,13},{10,... | collective-permute-start | bytes 147464 | tf_op jit(solution)/shard_map/ppermute | solution.py:24
  18.8 5.9 %copy-start.6 = (bf16[1,512,768]{2,1,0:T(8,128)(2,1)S(1)}, bf16[1,512,768]{2,1,0:T(8,128)(2,1)}, u32[]{:S(2)}) copy-start(bf16[1,512,768]{2,1,0:T(8,128)(2,1)} %param.5) | copy-start | bytes 2359300
  19.0 13.6 %collective-permute-start.4 = (bf16[160,1536]{1,0:T(8,128)(2,1)S(1)}, bf16[160,1536]{1,0:T(8,128)(2,1)S(1)}, u32[]{:S(2)}, u32[]{:S(2)}) collective-permute-start(bf16[160,1536]{1,0:T(8,128)(2,1)S(1)} %shard_map.60), channel_id=1, source_target_pairs={{0,16},{8,24},{16,0},{24,8},{1,17},{9,25},{17,1},{25,9},{2,18},{10... | collective-permute-start | bytes 1474568 | tf_op jit(solution)/shard_map/ppermute | solution.py:24
  19.4 8.9 %collective-permute-start.6 = (bf16[32,1536]{1,0:T(8,128)(2,1)S(1)}, bf16[32,1536]{1,0:T(8,128)(2,1)S(1)}, u32[]{:S(2)}, u32[]{:S(2)}) collective-permute-start(bf16[32,1536]{1,0:T(8,128)(2,1)S(1)} %shard_map.59.refs_1_.refs_2_.refs_4_), channel_id=1, source_target_pairs={{0,24},{8,16},{16,8},{24,0},{1,25},{9,17},{17,9},{25,1},{2,26},{10... | collective-permute-start | bytes 294920 | tf_op jit(solution)/shard_map/ppermute | solution.py:24
  22.1 6.2 %collective-permute-start.5 = (bf16[32,1536]{1,0:T(8,128)(2,1)S(1)}, bf16[32,1536]{1,0:T(8,128)(2,1)S(1)}, u32[]{:S(2)}, u32[]{:S(2)}) collective-permute-start(bf16[32,1536]{1,0:T(8,128)(2,1)S(1)} %shard_map.59.refs_1_.refs_2_.refs_4_), channel_id=1, source_target_pairs={{0,8},{8,0},{16,24},{24,16},{1,9},{9,1},{17,25},{25,17},{2,10},{10... | collective-permute-start | bytes 294920 | tf_op jit(solution)/shard_map/ppermute | solution.py:24
  24.7 7.9 %copy-start.2 = (bf16[128,1536]{1,0:T(8,128)(2,1)S(1)}, bf16[128,1536]{1,0:T(8,128)(2,1)}, u32[]{:S(2)}) copy-start(bf16[128,1536]{1,0:T(8,128)(2,1)} %get-tuple-element.20.refs_0_) | copy-start | bytes 1179652
  32.7 2.9 %collective-permute-start.8 = (bf16[384,1536]{1,0:T(8,128)(2,1)S(1)}, bf16[384,1536]{1,0:T(8,128)(2,1)S(1)}, u32[]{:S(2)}, u32[]{:S(2)}) collective-permute-start(bf16[384,1536]{1,0:T(8,128)(2,1)S(1)} %shard_map.62), channel_id=1, source_target_pairs={{0,1},{1,0},{2,3},{3,2},{4,5},{5,4},{6,7},{7,6},{8,9},{9,8},{10,11... | collective-permute-start | bytes 3538952 | tf_op jit(solution)/shard_map/ppermute | solution.py:24
  32.8 2.8 %copy-start.4 = (bf16[768,768]{1,0:T(8,128)(2,1)S(1)}, bf16[768,768]{1,0:T(8,128)(2,1)}, u32[]{:S(2)}) copy-start(bf16[768,768]{1,0:T(8,128)(2,1)} %refs_5_.1) | copy-start | bytes 3538948

commit v10 on v9

--- a/solution.py
+++ b/solution.py
@@ -13,6 +13,7 @@
 PAIR = 2 * HEAD_DIM
 CHUNK = 512
 KEY_CHUNK = 512
+OWN_PARTS = 3
 LANES = 128
 LOG2E = math.log2(math.e)
 VMEM_BYTES = 16 * 1024 * 1024
@@ -355,21 +356,19 @@
     held[1] = (across(first_a, "inner", 1), 0)
     own_set = [(own_keys, own_values)]
     own_states, moved, flip = [], far, 2
-    while flip < n_outer or len(own_states) < 2:
-        if flip < n_outer:
-            came = across(moved, "outer", flip)
-            flip *= 2
-        if len(own_states) < 2:
-            own_states.append(
-                attend(
-                    query_rows,
-                    own_set,
-                    row_strides=strides,
-                    part=(len(own_states), 2),
-                    wait=moved if own_states else None,
-                )
-            )
+
+    def own_part(wait):
+        part = (len(own_states), OWN_PARTS)
+        own_states.append(
+            attend(query_rows, own_set, row_strides=strides, part=part, wait=wait)
+        )
+
+    while flip < n_outer:
+        came = across(moved, "outer", flip)
+        if len(own_states) < OWN_PARTS - 1:
+            own_part(moved if own_states else None)
         moved = join_after([(moved, 0, moved.shape[0]), (came, 0, came.shape[0])], own_states[-1][1])
+        flip *= 2
     far = moved
     n_far = far.shape[0]
     fars = {0: (far, 0)}
@@ -401,6 +400,8 @@
     late_sets += [fars[d][0] for d in [0, 1] + late]
     late_counts.append(np.ones(n_far * (2 + len(late)), np.int64))
 
+    while len(own_states) < OWN_PARTS:
+        own_part(own_done)
     early_sets = [held[1][0], near_b] + [held[d][0] for d in known[2:]]
     early_counts = [prefix_counts(0, 0, sends[0])]
     early_counts += [prefix_counts(bit, 0, sends[bit]) for bit in range(1, inner_bits)]

time: 41 us -> 39.6 us (0.966)
  waiting for transfers between devices: 7.72 us -> 5.87 us
  Pallas kernels: 18.7 us -> 19.2 us
    ppermute x9, waiting for transfers between devices: 7.72 us -> 5.87 us  [across(): lax.ppermute(block, axis, [(i, i ^ flip) for i in range(lax.axis_size(axi...]
    pallas_call x5 -> x6, Pallas kernels: 15.5 us -> 15.9 us  [attend(): pl.pallas_call(kernel, out_shape=out_shape, in_specs=specs, **{'out_specs...]
  transfers between devices with their start and end apart: 9 -> 9, of which waited for: 5 -> 5; matrix products, arithmetic and copies ran while one was open for 0% -> 0% of each run, Pallas kernels for 26% -> 28%
where the time goes in v10:
time: 39.6 us; the launch traced here: 39.5 us
  Pallas kernels  19.2 us (48%)
  starting transfers between devices  12.9 us (33%)
  waiting for transfers between devices  5.87 us (15%)
  local copies, waits for them, and re-layouts  1.16 us (3%)
    pallas_call x6, Pallas kernels, attend(): pl.pallas_call(kernel, out_shape=out_shape, in_specs=specs, **{'out_specs...  15.9 us
    ppermute x9, starting transfers between devices, across(): lax.ppermute(block, axis, [(i, i ^ flip) for i in range(lax.axis_size(axi...  12.9 us
    ppermute x9, waiting for transfers between devices, across(): lax.ppermute(block, axis, [(i, i ^ flip) for i in range(lax.axis_size(axi...  5.87 us
    pallas_call x1, Pallas kernels, order_rows(): pl.pallas_call(kernel, out_shape=[jax.ShapeDtypeStruct((high - low, 2 * w...  3.18 us
    unnamed x14, local copies, waits for them, and re-layouts  1.16 us
  transfers between devices with their start and end apart: 9, of which 5 were waited for; matrix products, arithmetic and copies ran while one was open for 0% of the time, Pallas kernels for 28%

profile of v10, /device:TPU:0, one launch (start us, length us, event | category | flops | bytes accessed | tf_op | source)
XLA Modules:
  0.0 39.5 jit_solution(3150957333290618924)
XLA Ops:
  0.0 3.2 %shard_map.55 = (bf16[128,1536]{1,0:T(8,128)(2,1)}, bf16[128,1536]{1,0:T(8,128)(2,1)}, bf16[8,1536]{1,0:T(8,128)(2,1)}) custom-call(bf16[256,512]{1,0:T(8,128)(2,1)} %constant.2.clone.select_hbm, bf16[512,768]{1,0:T(8,128)(2,1)} %bitcast.4, bf16[512,768]{1,0:T(8,128)(2,1)} %bitcast.8), custom_call_target="tpu_custom_call" | custom-call | flops 402653184 | bytes 2359296 | tf_op jit(solution)/shard_map/pallas_call | solution.py:85
  3.2 3.0 %collective-permute-start = (bf16[128,1536]{1,0:T(8,128)(2,1)}, bf16[128,1536]{1,0:T(8,128)(2,1)S(1)}, u32[]{:S(2)}, u32[]{:S(2)}) collective-permute-start(bf16[128,1536]{1,0:T(8,128)(2,1)} %get-tuple-element.23.refs_0_), channel_id=1, source_target_pairs={{0,8},{8,0},{16,24},{24,16},{1,9},{9,1},{17,25},{25,17},{2,10},{10... | collective-permute-start | bytes 1179656 | tf_op jit(solution)/shard_map/ppermute | solution.py:25
  6.2 1.5 %collective-permute-start.1 = (bf16[128,1536]{1,0:T(8,128)(2,1)}, bf16[128,1536]{1,0:T(8,128)(2,1)S(1)}, u32[]{:S(2)}, u32[]{:S(2)}) collective-permute-start(bf16[128,1536]{1,0:T(8,128)(2,1)} %get-tuple-element.23.refs_0_), channel_id=1, source_target_pairs={{0,16},{8,24},{16,0},{24,8},{1,17},{9,25},{17,1},{25,9},{2,18},{10... | collective-permute-start | bytes 1179656 | tf_op jit(solution)/shard_map/ppermute | solution.py:25
  7.7 1.6 %collective-permute-start.2 = (bf16[8,1536]{1,0:T(8,128)(2,1)}, bf16[8,1536]{1,0:T(8,128)(2,1)S(1)}, u32[]{:S(2)}, u32[]{:S(2)}) collective-permute-start(bf16[8,1536]{1,0:T(8,128)(2,1)} %get-tuple-element.24.refs_0_), channel_id=1, source_target_pairs={{0,2},{1,3},{2,0},{3,1},{4,6},{5,7},{6,4},{7,5},{8,10},{9,11},{10,... | collective-permute-start | bytes 73736 | tf_op jit(solution)/shard_map/ppermute | solution.py:25
  9.3 0.5 %collective-permute-start.7 = (bf16[128,1536]{1,0:T(8,128)(2,1)}, bf16[128,1536]{1,0:T(8,128)(2,1)S(1)}, u32[]{:S(2)}, u32[]{:S(2)}) collective-permute-start(bf16[128,1536]{1,0:T(8,128)(2,1)} %get-tuple-element.27), channel_id=1, source_target_pairs={{0,8},{8,0},{16,24},{24,16},{1,9},{9,1},{17,25},{25,17},{2,10},{10... | collective-permute-start | bytes 1179656 | tf_op jit(solution)/shard_map/ppermute | solution.py:25
  9.8 1.1 %copy-done.5 = bf16[1,512,768]{2,1,0:T(8,128)(2,1)S(1)} copy-done((bf16[1,512,768]{2,1,0:T(8,128)(2,1)S(1)}, bf16[1,512,768]{2,1,0:T(8,128)(2,1)}, u32[]{:S(2)}) %copy-start.5) | copy-done | bytes 786456
  11.0 1.8 %shard_map.56 = (f32[256,512]{1,0:T(8,128)S(1)}, f32[4,512]{1,0:T(4,128)S(1)}, f32[4,512]{1,0:T(4,128)S(1)}) custom-call(bf16[512,768]{1,0:T(8,128)(2,1)S(1)} %bitcast.12, bf16[512,768]{1,0:T(8,128)(2,1)S(1)} %bitcast.5, bf16[512,768]{1,0:T(8,128)(2,1)S(1)} %bitcast.9), custom_call_target="tpu_custom_call" | custom-call | flops 1073741824 | bytes 1048576 | tf_op jit(solution)/shard_map/pallas_call | solution.py:311
  12.9 2.7 %collective-permute-start.3 = (bf16[16,1536]{1,0:T(8,128)(2,1)S(1)}, bf16[16,1536]{1,0:T(8,128)(2,1)S(1)}, u32[]{:S(2)}, u32[]{:S(2)}) collective-permute-start(bf16[16,1536]{1,0:T(8,128)(2,1)S(1)} %shard_map.57.refs_3_.refs_0_), channel_id=1, source_target_pairs={{0,4},{1,5},{2,6},{3,7},{4,0},{5,1},{6,2},{7,3},{8,12},{9,13},{10,... | collective-permute-start | bytes 147464 | tf_op jit(solution)/shard_map/ppermute | solution.py:25
  15.5 1.8 %shard_map.58 = (f32[256,512]{1,0:T(8,128)S(1)}, f32[4,512]{1,0:T(4,128)S(1)}, f32[4,512]{1,0:T(4,128)S(1)}) custom-call(bf16[512,768]{1,0:T(8,128)(2,1)S(1)} %bitcast.13, bf16[512,768]{1,0:T(8,128)(2,1)S(1)} %bitcast.6, bf16[512,768]{1,0:T(8,128)(2,1)S(1)} %bitcast.10, bf16[16,1536]{1,0:T(8,128)(2,1)S(1)} %shard_map.57.refs_3_.refs_0_), custom_call_target="tpu_custom_call" | custom-call | flops 1073741824 | bytes 1048576 | tf_op jit(solution)/shard_map/pallas_call | solution.py:311
  17.3 1.0 %collective-permute-done.3.refs_1_ = bf16[16,1536]{1,0:T(8,128)(2,1)S(1)} collective-permute-done((bf16[16,1536]{1,0:T(8,128)(2,1)S(1)}, bf16[16,1536]{1,0:T(8,128)(2,1)S(1)}, u32[]{:S(2)}, u32[]{:S(2)}) %collective-permute-start.3) | collective-permute-done | bytes 49184 | tf_op jit(solution)/shard_map/ppermute | solution.py:25
  18.4 0.6 %collective-permute-start.4 = (bf16[160,1536]{1,0:T(8,128)(2,1)S(1)}, bf16[160,1536]{1,0:T(8,128)(2,1)S(1)}, u32[]{:S(2)}, u32[]{:S(2)}) collective-permute-start(bf16[160,1536]{1,0:T(8,128)(2,1)S(1)} %shard_map.60.refs_3_), channel_id=1, source_target_pairs={{0,16},{8,24},{16,0},{24,8},{1,17},{9,25},{17,1},{25,9},{2,18},{10... | collective-permute-start | bytes 1474568 | tf_op jit(solution)/shard_map/ppermute | solution.py:25
  19.0 1.5 %collective-permute-start.5 = (bf16[32,1536]{1,0:T(8,128)(2,1)S(1)}, bf16[32,1536]{1,0:T(8,128)(2,1)S(1)}, u32[]{:S(2)}, u32[]{:S(2)}) collective-permute-start(bf16[32,1536]{1,0:T(8,128)(2,1)S(1)} %shard_map.59.refs_1_.refs_2_.refs_4_), channel_id=1, source_target_pairs={{0,8},{8,0},{16,24},{24,16},{1,9},{9,1},{17,25},{25,17},{2,10},{10... | collective-permute-start | bytes 294920 | tf_op jit(solution)/shard_map/ppermute | solution.py:25
  20.4 1.5 %collective-permute-start.6 = (bf16[32,1536]{1,0:T(8,128)(2,1)S(1)}, bf16[32,1536]{1,0:T(8,128)(2,1)S(1)}, u32[]{:S(2)}, u32[]{:S(2)}) collective-permute-start(bf16[32,1536]{1,0:T(8,128)(2,1)S(1)} %shard_map.59.refs_1_.refs_2_.refs_4_), channel_id=1, source_target_pairs={{0,24},{8,16},{16,8},{24,0},{1,25},{9,17},{17,9},{25,1},{2,26},{10... | collective-permute-start | bytes 294920 | tf_op jit(solution)/shard_map/ppermute | solution.py:25
  22.0 1.8 %shard_map.61 = (f32[256,512]{1,0:T(8,128)S(1)}, f32[4,512]{1,0:T(4,128)S(1)}, f32[4,512]{1,0:T(4,128)S(1)}) custom-call(bf16[512,768]{1,0:T(8,128)(2,1)S(1)} %bitcast.14, bf16[512,768]{1,0:T(8,128)(2,1)S(1)} %bitcast.7, bf16[512,768]{1,0:T(8,128)(2,1)S(1)} %bitcast.11, bf16[160,1536]{1,0:T(8,128)(2,1)S(1)} %shard_map.60.refs_3_), custom_call_target="tpu_custom_call" | custom-call | flops 1073741824 | bytes 1048576 | tf_op jit(solution)/shard_map/pallas_call | solution.py:311
  23.8 1.0 %collective-permute-done.7.refs_2_ = bf16[128,1536]{1,0:T(8,128)(2,1)S(1)} collective-permute-done((bf16[128,1536]{1,0:T(8,128)(2,1)}, bf16[128,1536]{1,0:T(8,128)(2,1)S(1)}, u32[]{:S(2)}, u32[]{:S(2)}) %collective-permute-start.7) | collective-permute-done | bytes 393248 | tf_op jit(solution)/shard_map/ppermute | solution.py:25
  24.8 3.1 %shard_map.62 = (f32[768,512]{1,0:T(8,128)S(1)}, f32[12,512]{1,0:T(8,128)S(1)}, f32[12,512]{1,0:T(8,128)S(1)}) custom-call(bf16[512,768]{1,0:T(8,128)(2,1)S(1)} %bitcast.15, bf16[128,1536]{1,0:T(8,128)(2,1)S(1)} %collective-permute-done.refs_0_.refs_1_, bf16[128,1536]{1,0:T(8,128)(2,1)S(1)} %collective-permute-done.7.refs_2_, ...), custom_call_target="tpu_custom_call" | custom-call | flops 2415919104 | bytes 2752512 | tf_op jit(solution)/shard_map/pallas_call | solution.py:311
  27.9 1.6 %collective-permute-done.6.refs_7_.refs_4_ = bf16[32,1536]{1,0:T(8,128)(2,1)S(1)} collective-permute-done((bf16[32,1536]{1,0:T(8,128)(2,1)S(1)}, bf16[32,1536]{1,0:T(8,128)(2,1)S(1)}, u32[]{:S(2)}, u32[]{:S(2)}) %collective-permute-start.6) | collective-permute-done | bytes 98336 | tf_op jit(solution)/shard_map/ppermute | solution.py:25
  29.5 1.8 %collective-permute-done.4.refs_3_.refs_6_.refs_1_ = bf16[160,1536]{1,0:T(8,128)(2,1)S(1)} collective-permute-done((bf16[160,1536]{1,0:T(8,128)(2,1)S(1)}, bf16[160,1536]{1,0:T(8,128)(2,1)S(1)}, u32[]{:S(2)}, u32[]{:S(2)}) %collective-permute-start.4) | collective-permute-done | bytes 491552 | tf_op jit(solution)/shard_map/ppermute | solution.py:25
  31.2 0.1 shard_map.63
  31.3 0.1 collective-permute-start.8
  31.4 0.0 copy-start.4
  31.4 2.3 %shard_map.64 = (f32[768,512]{1,0:T(8,128)S(1)}, f32[12,512]{1,0:T(8,128)S(1)}, f32[12,512]{1,0:T(8,128)S(1)}) custom-call(bf16[512,768]{1,0:T(8,128)(2,1)S(1)} %bitcast.16, bf16[160,1536]{1,0:T(8,128)(2,1)S(1)} %collective-permute-done.4.refs_3_.refs_6_.refs_1_, bf16[32,1536]{1,0:T(8,128)(2,1)S(1)} %shard_map.59.refs_1_.refs_2_.refs_4_, ...), custom_call_target="tpu_custom_call" | custom-call | flops 1610612736 | bytes 2359296 | tf_op jit(solution)/shard_map/pallas_call | solution.py:311
  33.7 0.5 %collective-permute-done.8.refs_1_ = bf16[384,1536]{1,0:T(8,128)(2,1)S(1)} collective-permute-done((bf16[384,1536]{1,0:T(8,128)(2,1)S(1)}, bf16[384,1536]{1,0:T(8,128)(2,1)S(1)}, u32[]{:S(2)}, u32[]{:S(2)}) %collective-permute-start.8) | collective-permute-done | bytes 1179680 | tf_op jit(solution)/shard_map/ppermute | solution.py:25
  34.2 5.0 %shard_map.65 = bf16[512,768]{1,0:T(8,128)(2,1)} custom-call(bf16[512,768]{1,0:T(8,128)(2,1)S(1)} %bitcast.17, bf16[384,1536]{1,0:T(8,128)(2,1)S(1)} %collective-permute-done.8.refs_1_, f32[768,512]{1,0:T(8,128)S(1)} %get-tuple-element.38.refs_2_, f32[12,512]{1,0:T(8,128)S(1)} %get-tuple-element.39.refs_3_, f32[12,512]{1,0:T(8,128)S(1)} %get-tuple-element.40.refs_4_, ...), custom_call_target="tpu_custom_call" | custom-call | flops 2415919104 | bytes 2752512 | tf_op jit(solution)/shard_map/pallas_call | solution.py:311
  (19 shorter events, 0.1 us)
Async XLA Ops:
  0.0 9.8 %copy-start = (bf16[1,512,768]{2,1,0:T(8,128)(2,1)S(1)}, bf16[1,512,768]{2,1,0:T(8,128)(2,1)}, u32[]{:S(2)}) copy-start(bf16[1,512,768]{2,1,0:T(8,128)(2,1)} %param.6) | copy-start | bytes 2359300
  0.0 9.8 %copy-start.1 = (bf16[1,512,768]{2,1,0:T(8,128)(2,1)S(1)}, bf16[1,512,768]{2,1,0:T(8,128)(2,1)}, u32[]{:S(2)}) copy-start(bf16[1,512,768]{2,1,0:T(8,128)(2,1)} %param.7) | copy-start | bytes 2359300
  3.2 15.2 %collective-permute-start = (bf16[128,1536]{1,0:T(8,128)(2,1)}, bf16[128,1536]{1,0:T(8,128)(2,1)S(1)}, u32[]{:S(2)}, u32[]{:S(2)}) collective-permute-start(bf16[128,1536]{1,0:T(8,128)(2,1)} %get-tuple-element.23.refs_0_), channel_id=1, source_target_pairs={{0,8},{8,0},{16,24},{24,16},{1,9},{9,1},{17,25},{25,17},{2,10},{10... | collective-permute-start | bytes 1179656 | tf_op jit(solution)/shard_map/ppermute | solution.py:25
  6.2 17.6 %collective-permute-start.1 = (bf16[128,1536]{1,0:T(8,128)(2,1)}, bf16[128,1536]{1,0:T(8,128)(2,1)S(1)}, u32[]{:S(2)}, u32[]{:S(2)}) collective-permute-start(bf16[128,1536]{1,0:T(8,128)(2,1)} %get-tuple-element.23.refs_0_), channel_id=1, source_target_pairs={{0,16},{8,24},{16,0},{24,8},{1,17},{9,25},{17,1},{25,9},{2,18},{10... | collective-permute-start | bytes 1179656 | tf_op jit(solution)/shard_map/ppermute | solution.py:25
  7.7 5.1 %collective-permute-start.2 = (bf16[8,1536]{1,0:T(8,128)(2,1)}, bf16[8,1536]{1,0:T(8,128)(2,1)S(1)}, u32[]{:S(2)}, u32[]{:S(2)}) collective-permute-start(bf16[8,1536]{1,0:T(8,128)(2,1)} %get-tuple-element.24.refs_0_), channel_id=1, source_target_pairs={{0,2},{1,3},{2,0},{3,1},{4,6},{5,7},{6,4},{7,5},{8,10},{9,11},{10,... | collective-permute-start | bytes 73736 | tf_op jit(solution)/shard_map/ppermute | solution.py:25
  9.3 15.5 %collective-permute-start.7 = (bf16[128,1536]{1,0:T(8,128)(2,1)}, bf16[128,1536]{1,0:T(8,128)(2,1)S(1)}, u32[]{:S(2)}, u32[]{:S(2)}) collective-permute-start(bf16[128,1536]{1,0:T(8,128)(2,1)} %get-tuple-element.27), channel_id=1, source_target_pairs={{0,8},{8,0},{16,24},{24,16},{1,9},{9,1},{17,25},{25,17},{2,10},{10... | collective-permute-start | bytes 1179656 | tf_op jit(solution)/shard_map/ppermute | solution.py:25
  9.8 1.1 %copy-start.5 = (bf16[1,512,768]{2,1,0:T(8,128)(2,1)S(1)}, bf16[1,512,768]{2,1,0:T(8,128)(2,1)}, u32[]{:S(2)}) copy-start(bf16[1,512,768]{2,1,0:T(8,128)(2,1)} %param.5) | copy-start | bytes 2359300
  11.0 1.9 %copy-start.3 = (bf16[8,1536]{1,0:T(8,128)(2,1)S(1)}, bf16[8,1536]{1,0:T(8,128)(2,1)}, u32[]{:S(2)}) copy-start(bf16[8,1536]{1,0:T(8,128)(2,1)} %get-tuple-element.24.refs_0_) | copy-start | bytes 73732
  11.0 4.5 %copy-start.6 = (bf16[1,512,768]{2,1,0:T(8,128)(2,1)S(1)}, bf16[1,512,768]{2,1,0:T(8,128)(2,1)}, u32[]{:S(2)}) copy-start(bf16[1,512,768]{2,1,0:T(8,128)(2,1)} %param.5) | copy-start | bytes 2359300
  12.9 5.5 %collective-permute-start.3 = (bf16[16,1536]{1,0:T(8,128)(2,1)S(1)}, bf16[16,1536]{1,0:T(8,128)(2,1)S(1)}, u32[]{:S(2)}, u32[]{:S(2)}) collective-permute-start(bf16[16,1536]{1,0:T(8,128)(2,1)S(1)} %shard_map.57.refs_3_.refs_0_), channel_id=1, source_target_pairs={{0,4},{1,5},{2,6},{3,7},{4,0},{5,1},{6,2},{7,3},{8,12},{9,13},{10,... | collective-permute-start | bytes 147464 | tf_op jit(solution)/shard_map/ppermute | solution.py:25
  18.4 12.8 %collective-permute-start.4 = (bf16[160,1536]{1,0:T(8,128)(2,1)S(1)}, bf16[160,1536]{1,0:T(8,128)(2,1)S(1)}, u32[]{:S(2)}, u32[]{:S(2)}) collective-permute-start(bf16[160,1536]{1,0:T(8,128)(2,1)S(1)} %shard_map.60.refs_3_), channel_id=1, source_target_pairs={{0,16},{8,24},{16,0},{24,8},{1,17},{9,25},{17,1},{25,9},{2,18},{10... | collective-permute-start | bytes 1474568 | tf_op jit(solution)/shard_map/ppermute | solution.py:25
  19.0 8.9 %collective-permute-start.5 = (bf16[32,1536]{1,0:T(8,128)(2,1)S(1)}, bf16[32,1536]{1,0:T(8,128)(2,1)S(1)}, u32[]{:S(2)}, u32[]{:S(2)}) collective-permute-start(bf16[32,1536]{1,0:T(8,128)(2,1)S(1)} %shard_map.59.refs_1_.refs_2_.refs_4_), channel_id=1, source_target_pairs={{0,8},{8,0},{16,24},{24,16},{1,9},{9,1},{17,25},{25,17},{2,10},{10... | collective-permute-start | bytes 294920 | tf_op jit(solution)/shard_map/ppermute | solution.py:25
  20.4 9.0 %collective-permute-start.6 = (bf16[32,1536]{1,0:T(8,128)(2,1)S(1)}, bf16[32,1536]{1,0:T(8,128)(2,1)S(1)}, u32[]{:S(2)}, u32[]{:S(2)}) collective-permute-start(bf16[32,1536]{1,0:T(8,128)(2,1)S(1)} %shard_map.59.refs_1_.refs_2_.refs_4_), channel_id=1, source_target_pairs={{0,24},{8,16},{16,8},{24,0},{1,25},{9,17},{17,9},{25,1},{2,26},{10... | collective-permute-start | bytes 294920 | tf_op jit(solution)/shard_map/ppermute | solution.py:25
  24.8 6.5 %copy-start.2 = (bf16[128,1536]{1,0:T(8,128)(2,1)S(1)}, bf16[128,1536]{1,0:T(8,128)(2,1)}, u32[]{:S(2)}) copy-start(bf16[128,1536]{1,0:T(8,128)(2,1)} %get-tuple-element.23.refs_0_) | copy-start | bytes 1179652
  31.3 2.9 %collective-permute-start.8 = (bf16[384,1536]{1,0:T(8,128)(2,1)S(1)}, bf16[384,1536]{1,0:T(8,128)(2,1)S(1)}, u32[]{:S(2)}, u32[]{:S(2)}) collective-permute-start(bf16[384,1536]{1,0:T(8,128)(2,1)S(1)} %shard_map.63), channel_id=1, source_target_pairs={{0,1},{1,0},{2,3},{3,2},{4,5},{5,4},{6,7},{7,6},{8,9},{9,8},{10,11... | collective-permute-start | bytes 3538952 | tf_op jit(solution)/shard_map/ppermute | solution.py:25
  31.4 2.8 %copy-start.4 = (bf16[768,768]{1,0:T(8,128)(2,1)S(1)}, bf16[768,768]{1,0:T(8,128)(2,1)}, u32[]{:S(2)}) copy-start(bf16[768,768]{1,0:T(8,128)(2,1)} %refs_5_.1) | copy-start | bytes 3538948
